TPU v7x, 1024 devices: a whole 4x4x32 slice. The times are simulated.
1024 devices in a mesh: node: 32 (over z), local: 32 (over x, y, core).
Axes of the slice: x: 4, y: 4, z: 32, core: 2. Of those that a mesh axis runs over, the one named last changes fastest.
Arguments:
- out_grad: bfloat16 [4096, 7168], P('node', 'local'), may hold values from -3 to 3
- node_pick: int32 [4096, 4], P('node'), may hold values from 0 to 31, all different within a row; in each aligned block of 128 rows (0 to 127, 128 to 255, ...) at most 20 rows name the same one
- expert_pick: int32 [4096, 4, 1], P('node'), may hold values from 0 to 1
- pick_weight: bfloat16 [4096, 4, 1], P('node'), may hold values from 0.049804688 to 1
- gate_weight: bfloat16 [32, 2, 7168, 1024], P('node', None, 'local'), may hold values from -0.0625 to 0.0625
- up_weight: bfloat16 [32, 2, 7168, 1024], P('node', None, 'local'), may hold values from -0.0625 to 0.0625
- down_weight: bfloat16 [32, 2, 1024, 7168], P('node', None, None, 'local'), may hold values from -0.1875 to 0.1875
- saved_gate: bfloat16 [32, 640, 1, 1024], P('node', 'local'), may hold values from -5 to 5
- saved_up: bfloat16 [32, 640, 1, 1024], P('node', 'local'), may hold values from -1.1953125 to 1.1953125
Outputs:
- input_grad: bfloat16 [4096, 7168], P('node', 'local')
- router_grad: bfloat16 [4096, 4, 1], P('node')
Inputs may be any that keep to these rules, and one draw needn't show every extreme that they name: `node_pick`: each token names 4 different node groups; among the tokens of one node group no node group is named by more than 20 tokens, and one is named by exactly 20. `expert_pick`: the 1 expert of each token and node group are different.
All inputs are finite; a program needn't handle non-finite values.
Results may differ from a plain program's by a relative error of at most 0.0057.
Values may be sent and summed in bfloat16 or wider, within the bound.
No kernel may reach another device: no remote copies, remote signals or barrier semaphores. Data moves between devices by JAX's collectives and lax.ppermute only.
A program may use at most 64 MiB of HBM per device.

v0:
```python
import jax
import jax.numpy as jnp
from jax import lax
from jax.sharding import PartitionSpec as P


def per_device(
    out_grad,
    node_pick,
    expert_pick,
    pick_weight,
    gate_weight,
    up_weight,
    down_weight,
    saved_gate,
    saved_up,
):
    node_count = lax.axis_size("node")
    local_count = lax.axis_size("local")
    tokens_here, groups = node_pick.shape
    picks = expert_pick.shape[2]
    feature_width = out_grad.shape[1]
    experts = gate_weight.shape[1]
    own_slots = saved_gate.shape[1]
    slot_count = own_slots * local_count
    capacity = slot_count // node_count
    pair_count = tokens_here * groups
    expert_range = jnp.arange(experts, dtype=jnp.int32)
    target = node_pick.reshape(pair_count)
    matches = (target[:, None] == jnp.arange(node_count, dtype=jnp.int32)[None, :]).astype(
        jnp.int32
    )
    before = jnp.cumsum(matches, axis=0) - matches
    position = jnp.sum(before * matches, axis=1)
    send_slot = target * capacity + position
    placing = (jnp.arange(slot_count, dtype=jnp.int32)[:, None] == send_slot[None, :]).astype(
        jnp.bfloat16
    )
    token_map = jnp.sum(placing.reshape(slot_count, tokens_here, groups), axis=2)
    send_rows = jnp.dot(token_map, out_grad, preferred_element_type=jnp.float32).astype(
        jnp.bfloat16
    )
    send_rows = send_rows.reshape(node_count, capacity, feature_width)
    send_weight = jnp.dot(
        placing, pick_weight.reshape(pair_count, picks), preferred_element_type=jnp.float32
    ).astype(jnp.bfloat16)
    send_weight = send_weight.reshape(node_count, capacity, picks)
    send_ids = jnp.dot(
        placing,
        expert_pick.reshape(pair_count, picks).astype(jnp.bfloat16),
        preferred_element_type=jnp.float32,
    ).astype(jnp.bfloat16)
    send_ids = send_ids.reshape(node_count, capacity, picks)
    arrived, weights_in, ids_in = (
        lax.all_to_all(send_rows, "node", split_axis=0, concat_axis=0, tiled=True),
        lax.all_to_all(send_weight, "node", split_axis=0, concat_axis=0, tiled=True),
        lax.all_to_all(send_ids, "node", split_axis=0, concat_axis=0, tiled=True),
    )
    arrived = arrived.reshape(slot_count, feature_width)
    ids_all = ids_in.reshape(slot_count, picks).astype(jnp.int32)
    weights_all = weights_in.reshape(slot_count, picks).astype(jnp.float32)
    down_local = down_weight[0]
    gate_local = gate_weight[0]
    up_local = up_weight[0]
    first_slot = lax.axis_index("local") * own_slots
    own_ids = lax.dynamic_slice_in_dim(ids_all, first_slot, own_slots, 0)
    own_weight = lax.dynamic_slice_in_dim(weights_all, first_slot, own_slots, 0)
    own_onehot = (own_ids[:, :, None] == expert_range[None, None, :]).astype(jnp.float32)
    projected = jnp.einsum("sd,efd->sef", arrived, down_local, preferred_element_type=jnp.float32)
    summed = lax.psum_scatter(
        projected.reshape(own_slots * experts * lax.axis_size("local"), projected.shape[2]),
        "local",
        scatter_dimension=0,
        tiled=True,
    )
    summed = summed.reshape(own_slots, 1, experts, summed.shape[1])
    raw_grad = jnp.sum(own_onehot[:, :, :, None] * summed, axis=2)
    gate_saved = saved_gate[0].astype(jnp.float32)
    up_saved = saved_up[0].astype(jnp.float32)
    gate_sigmoid = jax.nn.sigmoid(gate_saved)
    activated = gate_saved * gate_sigmoid
    hidden = activated * up_saved
    router_slot = jnp.sum(hidden * raw_grad, axis=2).astype(jnp.bfloat16)
    hidden_grad = own_weight[:, :, None] * raw_grad
    gate_grad = (
        hidden_grad * up_saved * gate_sigmoid * (1.0 + gate_saved * (1.0 - gate_sigmoid))
    ).astype(jnp.bfloat16)
    up_grad = (hidden_grad * activated).astype(jnp.bfloat16)

    def spread_picks(selection, grads):
        return jnp.einsum(
            "spe,spf->sef", selection, grads, preferred_element_type=jnp.float32
        ).astype(jnp.bfloat16)

    spread_mask = own_onehot.astype(jnp.bfloat16)
    gate_spread = spread_picks(spread_mask, gate_grad)
    up_spread = spread_picks(spread_mask, up_grad)
    gate_piece = lax.all_gather(gate_spread, "local", axis=0, tiled=True)
    up_piece = lax.all_gather(up_spread, "local", axis=0, tiled=True)
    route_piece = lax.all_gather(router_slot, "local", axis=0, tiled=True)
    back_gate = jnp.einsum(
        "sef,edf->sd", gate_piece, gate_local, preferred_element_type=jnp.float32
    )
    back_up = jnp.einsum("sef,edf->sd", up_piece, up_local, preferred_element_type=jnp.float32)
    contrib = back_gate + back_up
    back_rows = contrib.astype(jnp.bfloat16).reshape(node_count, capacity, feature_width)
    route_rows = route_piece.reshape(node_count, capacity, picks)
    returned, route_back = (
        lax.all_to_all(back_rows, "node", split_axis=0, concat_axis=0, tiled=True),
        lax.all_to_all(route_rows, "node", split_axis=0, concat_axis=0, tiled=True),
    )
    input_grad = jnp.dot(
        token_map.T, returned.reshape(slot_count, feature_width), preferred_element_type=jnp.float32
    ).astype(jnp.bfloat16)
    router_grad = jnp.dot(
        placing.T, route_back.reshape(slot_count, picks), preferred_element_type=jnp.float32
    ).astype(jnp.bfloat16)
    return (input_grad, router_grad.reshape(tokens_here, groups, picks))


def solution(mesh):
    return jax.shard_map(
        per_device,
        mesh=mesh,
        in_specs=(
            P("node", "local"),
            P("node", None),
            P("node", None, None),
            P("node", None, None),
            P("node", None, "local", None),
            P("node", None, "local", None),
            P("node", None, None, "local"),
            P("node", "local", None, None),
            P("node", "local", None, None),
        ),
        out_specs=(P("node", "local"), P("node", None, None)),
        check_vma=False,
    )
```

profile of v0, /device:TPU:1, one launch (start us, length us, event | category | flops | bytes accessed | tf_op | source)
XLA Modules:
  0.0 487.9 jit_solution(2719922128097835103)
XLA Ops:
  7.2 0.9 copy.61
  8.3 1.2 reduce-window.6
  10.0 0.7 multiply_add_fusion.1
  10.9 1.1 convolution_convert_fusion
  12.2 81.0 %all_to_all.25 = bf16[32,20,224]{2,1,0:T(8,128)(2,1)S(1)} all-to-all(bf16[32,20,224]{2,1,0:T(8,128)(2,1)S(1)} %reshape.274), channel_id=1, replica_groups=mesh['node'=32,'local'=32] {'node'}, dimensions={0} | all-to-all | bytes 573440 | tf_op jit(solution)/shard_map/all_to_all | solution.py:55
  93.4 0.8 fusion.24
  94.3 6.4 %copy.71 = f32[640,2,1024]{2,1,0:T(2,128)} copy(f32[640,2,1024]{2,0,1:T(8,128)S(1)} %fusion.24) | data formatting | bytes 10485760 | tf_op jit(solution)/shard_map/sd,efd->sef/dot_general | solution.py:69
  100.7 7.6 %reshape.276 = f32[1280,1024]{1,0:T(8,128)} reshape(f32[640,2,1024]{2,1,0:T(2,128)} %copy.71) | data formatting | bytes 10485760 | tf_op jit(solution)/shard_map/reshape | solution.py:71
  108.3 0.6 copy-done.3
  109.2 0.3 fusion.20
  109.6 0.7 reshape.304
  110.3 4.4 all-to-all-start
  115.3 0.7 reshape.306
  116.0 19.8 %all-to-all-done = bf16[32,20,1]{1,2,0:T(2,128)(2,1)S(1)} async-done(((bf16[32,20,1]{1,2,0:T(2,128)(2,1)}), bf16[32,20,1]{1,2,0:T(2,128)(2,1)S(1)}, u32[]{:S(2)}, u32[]{:S(2)}) %all-to-all-start) | async-done | bytes 1312 | tf_op jit(solution)/shard_map/all_to_all | solution.py:57
  135.8 3.8 all-to-all-start.1
  139.8 21.0 %all-to-all-done.1 = bf16[32,20,1]{1,2,0:T(2,128)(2,1)S(1)} async-done(((bf16[32,20,1]{1,2,0:T(2,128)(2,1)}), bf16[32,20,1]{1,2,0:T(2,128)(2,1)S(1)}, u32[]{:S(2)}, u32[]{:S(2)}) %all-to-all-start.1) | async-done | bytes 1312 | tf_op jit(solution)/shard_map/all_to_all | solution.py:56
  161.2 67.7 %reduce-scatter.2.cloned.1.call-done = f32[40,1024]{1,0:T(8,128)} async-done(((f32[1280,1024]{1,0:T(8,128)}), f32[40,1024]{1,0:T(8,128)}) %reduce-scatter.2.cloned.1.call-update) | async-done | bytes 163856 | tf_op jit(solution)/shard_map/reduce_scatter | solution.py:70
  228.9 1.0 reshape.277
  230.4 0.9 multiply_convert_fusion
  231.3 0.7 all-gather.6.cloned.1.call-update
  232.0 1.3 dynamic-slice
  234.2 64.4 %all-reduce = bf16[640]{0:T(1024)(128)(2,1)S(1)} all-reduce(bf16[640]{0:T(1024)(128)(2,1)S(1)} %dynamic-update-slice), channel_id=2, replica_groups=mesh['node'=32,'local'=32] {'local'}, use_global_device_ids=true, to_apply=%add | all-reduce | flops 640 | bytes 2560
  298.6 0.7 reshape.307
  299.3 22.8 %all-to-all-start.4 = ((bf16[32,20,1]{1,2,0:T(2,128)(2,1)}), bf16[32,20,1]{1,2,0:T(2,128)(2,1)S(1)}, u32[]{:S(2)}, u32[]{:S(2)}) async-start(bf16[32,20,1]{1,2,0:T(2,128)(2,1)} %reshape.307), calls=%async_computation.5 | async-start | bytes 32768 | tf_op jit(solution)/shard_map/all_to_all | solution.py:110
  322.2 3.8 fusion.8
  326.0 75.1 %all-gather.6.cloned.1.call-done = bf16[640,2,1024]{2,1,0:T(2,128)(2,1)} async-done(((bf16[20,2,1024]{2,1,0:T(2,128)(2,1)}), bf16[640,2,1024]{2,1,0:T(2,128)(2,1)}) %all-gather.6.cloned.1.call-update) | async-done | bytes 2621456 | tf_op jit(solution)/shard_map/all_gather | solution.py:99
  401.1 3.0 fusion.17
  404.3 0.8 reshape.278
  405.1 22.6 %all-to-all-start.3 = ((bf16[32,20,224]{2,1,0:T(8,128)(2,1)}), bf16[32,20,224]{2,1,0:T(8,128)(2,1)S(1)}, u32[]{:S(2)}, u32[]{:S(2)}) async-start(bf16[32,20,224]{2,1,0:T(8,128)(2,1)} %reshape.278), calls=%async_computation.4 | async-start | bytes 786432 | tf_op jit(solution)/shard_map/all_to_all | solution.py:109
  428.4 0.7 copy.76
  429.0 51.2 %all-to-all-done.3 = bf16[32,20,224]{2,1,0:T(8,128)(2,1)S(1)} async-done(((bf16[32,20,224]{2,1,0:T(8,128)(2,1)}), bf16[32,20,224]{2,1,0:T(8,128)(2,1)S(1)}, u32[]{:S(2)}, u32[]{:S(2)}) %all-to-all-start.3) | async-done | bytes 286752 | tf_op jit(solution)/shard_map/all_to_all | solution.py:109
  480.4 0.9 convolution_convert_fusion.1
  (58 shorter events, 4.5 us)
Async XLA Ops:
  7.2 86.2 %copy-start = (bf16[1,2,1024,224]{2,3,1,0:T(8,128)(2,1)S(1)}, bf16[1,2,1024,224]{2,3,1,0:T(8,128)(2,1)}, u32[]{:S(2)}) copy-start(bf16[1,2,1024,224]{2,3,1,0:T(8,128)(2,1)} %param.15) | copy-start | bytes 2752516
  7.2 221.7 %reduce-scatter.2.cloned.1.call-start = ((), (), s32[]{:S(2)}) async-start(), calls=%async_computation.6 | async-start | bytes 5406720 | tf_op jit(solution)/shard_map/reduce_scatter | solution.py:70
  108.3 0.7 copy-start.3
  108.3 6.4 %copy-start.4 = (bf16[128,4,1]{0,1,2:T(4,128)(2,1)S(1)}, bf16[128,4,1]{0,1,2:T(4,128)(2,1)}, u32[]{:S(2)}) copy-start(bf16[128,4,1]{0,1,2:T(4,128)(2,1)} %param.12) | copy-start | bytes 3076
  108.3 121.9 %copy-start.1 = (bf16[1,20,1,1024]{3,1,2,0:T(8,128)(2,1)S(1)}, bf16[1,20,1,1024]{3,1,2,0:T(8,128)(2,1)}, u32[]{:S(2)}) copy-start(bf16[1,20,1,1024]{3,1,2,0:T(8,128)(2,1)} %param.17) | copy-start | bytes 122884
  108.3 121.9 %copy-start.2 = (bf16[1,20,1,1024]{3,1,2,0:T(8,128)(2,1)S(1)}, bf16[1,20,1,1024]{3,1,2,0:T(8,128)(2,1)}, u32[]{:S(2)}) copy-start(bf16[1,20,1,1024]{3,1,2,0:T(8,128)(2,1)} %param.16) | copy-start | bytes 122884
  108.9 213.2 %copy-start.5 = (bf16[1,2,224,1024]{3,2,1,0:T(8,128)(2,1)S(1)}, bf16[1,2,224,1024]{3,2,1,0:T(8,128)(2,1)}, u32[]{:S(2)}) copy-start(bf16[1,2,224,1024]{3,2,1,0:T(8,128)(2,1)} %param.13) | copy-start | bytes 2752516
  110.3 25.5 %all-to-all-start = ((bf16[32,20,1]{1,2,0:T(2,128)(2,1)}), bf16[32,20,1]{1,2,0:T(2,128)(2,1)S(1)}, u32[]{:S(2)}, u32[]{:S(2)}) async-start(bf16[32,20,1]{1,2,0:T(2,128)(2,1)} %reshape.304), calls=%async_computation | async-start | bytes 32768 | tf_op jit(solution)/shard_map/all_to_all | solution.py:57
  135.8 25.0 %all-to-all-start.1 = ((bf16[32,20,1]{1,2,0:T(2,128)(2,1)}), bf16[32,20,1]{1,2,0:T(2,128)(2,1)S(1)}, u32[]{:S(2)}, u32[]{:S(2)}) async-start(bf16[32,20,1]{1,2,0:T(2,128)(2,1)} %reshape.306), calls=%async_computation.1 | async-start | bytes 32768 | tf_op jit(solution)/shard_map/all_to_all | solution.py:56
  139.6 182.5 %all-gather.4.cloned.1.call-start = ((), (), s32[]{:S(2)}) async-start(), calls=%async_computation.7 | async-start | bytes 2703360 | tf_op jit(solution)/shard_map/all_gather | solution.py:98
  231.3 169.8 %all-gather.6.cloned.1.call-start = ((), (), s32[]{:S(2)}) async-start(), calls=%async_computation.8 | async-start | bytes 2703360 | tf_op jit(solution)/shard_map/all_gather | solution.py:99
  299.3 105.8 %all-to-all-start.4 = ((bf16[32,20,1]{1,2,0:T(2,128)(2,1)}), bf16[32,20,1]{1,2,0:T(2,128)(2,1)S(1)}, u32[]{:S(2)}, u32[]{:S(2)}) async-start(bf16[32,20,1]{1,2,0:T(2,128)(2,1)} %reshape.307), calls=%async_computation.5 | async-start | bytes 32768 | tf_op jit(solution)/shard_map/all_to_all | solution.py:110
  322.1 78.9 %copy-start.6 = (bf16[1,2,224,1024]{3,2,1,0:T(8,128)(2,1)S(1)}, bf16[1,2,224,1024]{3,2,1,0:T(8,128)(2,1)}, u32[]{:S(2)}) copy-start(bf16[1,2,224,1024]{3,2,1,0:T(8,128)(2,1)} %param.14) | copy-start | bytes 2752516
  405.1 75.2 %all-to-all-start.3 = ((bf16[32,20,224]{2,1,0:T(8,128)(2,1)}), bf16[32,20,224]{2,1,0:T(8,128)(2,1)S(1)}, u32[]{:S(2)}, u32[]{:S(2)}) async-start(bf16[32,20,224]{2,1,0:T(8,128)(2,1)} %reshape.278), calls=%async_computation.4 | async-start | bytes 786432 | tf_op jit(solution)/shard_map/all_to_all | solution.py:109
Sparse Core Ops, SparseCore 0:
  108.4 120.4 reduce-scatter.1
  234.0 82.0 all-gather.3
  321.1 79.9 all-gather.5
where the time goes:
time: 489 us; the launch traced here: 488 us
  waiting for transfers between devices  236 us (48%)
  blocking collectives  145 us (30%)
  starting transfers between devices  53.7 us (11%)
  local copies, waits for them, and re-layouts  24.1 us (5%)
  between operations  14.7 us (3%)
  matrix products  10.6 us (2%)
    all_to_all x1, blocking collectives, per_device(): lax.all_to_all(send_rows, 'node', split_axis=0, concat_axis=0, tiled=True)  81 us
    all_gather x1, waiting for transfers between devices, per_device(): up_piece = lax.all_gather(up_spread, 'local', axis=0, tiled=True)  75.1 us
    reduce_scatter x1, waiting for transfers between devices, per_device(): lax.psum_scatter(projected.reshape(own_slots * experts * lax.axis_size('l...  67.7 us
    unnamed x1, blocking collectives  64.4 us
    all_to_all x1, waiting for transfers between devices, per_device(): lax.all_to_all(back_rows, 'node', split_axis=0, concat_axis=0, tiled=True)  51.2 us
    all_to_all x1, starting transfers between devices, per_device(): lax.all_to_all(route_rows, 'node', split_axis=0, concat_axis=0, tiled=True)  22.8 us
    all_to_all x1, starting transfers between devices, per_device(): lax.all_to_all(back_rows, 'node', split_axis=0, concat_axis=0, tiled=True)  22.6 us
    all_to_all x1, waiting for transfers between devices, per_device(): lax.all_to_all(send_weight, 'node', split_axis=0, concat_axis=0, tiled=True)  21 us
  transfers between devices with their start and end apart: 7, of which 5 were waited for; matrix products, arithmetic and copies ran while one was open for 3% of the time, Pallas kernels for 0%

commit v1 on v0

v1 whole, which is shorter than its diff:
```python
import functools

import jax
import jax.numpy as jnp
from jax import lax
from jax.experimental import pallas as pl
from jax.experimental.pallas import tpu as pltpu
from jax.sharding import PartitionSpec as P

BF16 = jnp.bfloat16
F32 = jnp.float32
LANES = 128
FOLD = 4
VMEM_LIMIT = 40 * 1024 * 1024


def round_up(value, unit):
    return -(-value // unit) * unit


def nn(a, b):
    return lax.dot_general(a, b, (((1,), (0,)), ((), ())), preferred_element_type=F32)


def nt(a, b):
    return lax.dot_general(a, b, (((1,), (1,)), ((), ())), preferred_element_type=F32)


def tn(a, b):
    return lax.dot_general(a, b, (((0,), (0,)), ((), ())), preferred_element_type=F32)


def iota(shape, axis):
    return lax.broadcasted_iota(jnp.int32, shape, axis)


def call(kernel, out_shape, **extra):
    return pl.pallas_call(
        kernel,
        out_shape=out_shape,
        compiler_params=pltpu.CompilerParams(vmem_limit_bytes=VMEM_LIMIT),
        **extra,
    )


def pair_maps(pick, nodes):
    groups, tokens = pick.shape
    rows = nodes * FOLD
    node_of = iota((rows, tokens), 0) // FOLD
    hits = [(pick[g : g + 1, :] == node_of).astype(F32) for g in range(groups)]
    named = functools.reduce(jnp.add, hits)
    earlier = (iota((tokens, tokens), 0) < iota((tokens, tokens), 1)).astype(BF16)
    slot = nn(named.astype(BF16), earlier).astype(jnp.int32)
    return named, slot, hits


def placing(named, slot, piece):
    row = iota(named.shape, 0) % FOLD
    return jnp.where(slot == piece * FOLD + row, named, 0.0)


def prepare_kernel(pieces, pick_ref, expert_ref, weight_ref, rows_ref, out_ref):
    nodes = out_ref.shape[0]
    width, tokens = rows_ref.shape
    rows = nodes * FOLD
    pick = pick_ref[...]
    named, slot, hits = pair_maps(pick, nodes)
    expert = functools.reduce(
        jnp.add, [hit * expert_ref[g].astype(F32) for g, hit in enumerate(hits)]
    )
    weights = weight_ref[...].astype(F32)
    weight = functools.reduce(
        jnp.add, [hit * weights[g : g + 1, :] for g, hit in enumerate(hits)]
    )
    token_rows = rows_ref[...]
    spare = out_ref.shape[2] - pieces * width
    lane = iota((rows, spare), 1)
    meta = jnp.zeros((rows, spare), F32)
    parts = []
    for piece in range(pieces):
        place = placing(named, slot, piece)
        parts.append(nt(place.astype(BF16), token_rows))
        picked = jnp.sum(place * expert, axis=1, keepdims=True)
        scale = jnp.sum(place * weight, axis=1, keepdims=True)
        meta = jnp.where(lane == piece, picked, meta)
        meta = jnp.where(lane == pieces + piece, scale, meta)
    block = jnp.concatenate(parts + [meta], axis=1)
    out_ref[...] = block.reshape(nodes, FOLD, block.shape[1]).astype(BF16)


def factors_kernel(gate_ref, up_ref, out_ref):
    gate = gate_ref[...].astype(F32)
    up = up_ref[...].astype(F32)
    sig = jax.nn.sigmoid(gate)
    slots, units = gate.shape
    rest = jnp.zeros((out_ref.shape[1] - slots, units), F32)
    by_gate = up * sig * (1.0 + gate * (1.0 - sig))
    by_up = gate * sig
    out_ref[0] = jnp.concatenate([by_gate, rest], axis=0).astype(BF16)
    out_ref[1] = jnp.concatenate([by_up, rest], axis=0).astype(BF16)


def unfold_matrix(blocks, pieces, held):
    shape = (blocks * held, pieces * blocks * FOLD)
    row, column = iota(shape, 0), iota(shape, 1)
    slot = row % held
    source = (slot // FOLD) * (blocks * FOLD) + (row // held) * FOLD + slot % FOLD
    return jnp.where(jnp.logical_and(source == column, slot < pieces * FOLD), 1.0, 0.0).astype(BF16)


def raw_kernel(pieces, width, held, adds, which_ref, in_ref, down_ref, *refs):
    other_ref = refs[0] if adds else None
    out_ref, meta_ref = refs[-2:]
    blocks, units = out_ref.shape[0], out_ref.shape[2]
    folded = in_ref[:, 0].astype(F32).reshape(blocks * FOLD, in_ref.shape[3])
    base = pieces * width
    pad = 2 * LANES - width
    stacked = []
    for piece in range(pieces):
        columns = [
            folded[:, piece * width : (piece + 1) * width],
            folded[:, base + piece : base + piece + 1],
            folded[:, base + pieces + piece : base + pieces + piece + 1],
            jnp.zeros((blocks * FOLD, pad - 2), F32),
        ]
        stacked.append(jnp.concatenate(columns, axis=1))
    stacked = jnp.concatenate(stacked, axis=0).astype(BF16)
    rows = nn(unfold_matrix(blocks, pieces, held), stacked)
    arrived = rows[:, :width]
    meta = rows[:, width : width + 2]
    first = meta[:, 0:1] == 0.0
    zero = jnp.zeros_like(arrived)
    raw = nn(jnp.where(first, arrived, zero).astype(BF16), down_ref[0])
    raw = raw + nn(jnp.where(first, zero, arrived).astype(BF16), down_ref[1])
    raw = raw.reshape(blocks, held, units)
    if adds:
        raw = raw + other_ref[...].astype(F32)
    out_ref[...] = raw.astype(BF16)
    meta_ref[...] = meta


def hidden_kernel(parts_ref, gate_ref, up_ref, out_ref):
    blocks, held, units = parts_ref.shape
    total = parts_ref[0].astype(F32)
    for at in range(1, blocks):
        total = total + parts_ref[at].astype(F32)
    slots = gate_ref.shape[0]
    raw = total[:slots]
    gate = gate_ref[...].astype(F32)
    up = up_ref[...].astype(F32)
    hidden = gate * jax.nn.sigmoid(gate) * up
    router = jnp.sum(hidden * raw, axis=1, keepdims=True)
    diagonal = iota((slots, units), 0) == iota((slots, units), 1)
    router_row = jnp.sum(jnp.where(diagonal, router, 0.0), axis=0, keepdims=True)
    rest = jnp.zeros((held - slots - 1, units), F32)
    block = jnp.concatenate([raw, router_row, rest], axis=0).astype(BF16)
    for at in range(blocks):
        out_ref[at] = block


def back_kernel(pieces, width, merges, which_ref, raw_ref, factor_ref, meta_ref, gate_ref, up_ref, *refs):
    blocks, held, units = raw_ref.shape
    out_ref = refs[-1]
    slots = pieces * FOLD
    raw = raw_ref[...].astype(F32)
    by_gate = (raw * factor_ref[:, 0, 0].astype(F32)).astype(BF16).reshape(blocks * held, units)
    by_up = (raw * factor_ref[:, 0, 1].astype(F32)).astype(BF16).reshape(blocks * held, units)
    meta = meta_ref[...]
    first = meta[:, 0:1] == 0.0
    back = jnp.where(
        first,
        nt(by_gate, gate_ref[0]) + nt(by_up, up_ref[0]),
        nt(by_gate, gate_ref[1]) + nt(by_up, up_ref[1]),
    )
    back = (back * meta[:, 1:2]).astype(BF16)
    folded = tn(unfold_matrix(blocks, pieces, held), back)
    rows = blocks * FOLD
    parts = [folded[piece * rows : (piece + 1) * rows] for piece in range(pieces)]
    router = raw[:, slots, :LANES].astype(BF16)
    spread = (iota((rows, blocks), 0) // FOLD == iota((rows, blocks), 1)).astype(F32).astype(BF16)
    router = nn(spread, router)
    kept = jnp.logical_and(
        iota((rows, LANES), 1) % FOLD == iota((rows, LANES), 0) % FOLD,
        iota((rows, LANES), 1) < slots,
    )
    router = jnp.where(kept, router, 0.0).astype(BF16)
    spare = out_ref.shape[-1] - pieces * width
    gather = (iota((LANES, spare), 0) // FOLD == iota((LANES, spare), 1)).astype(F32).astype(BF16)
    parts.append(nn(router, gather))
    block = jnp.concatenate(parts, axis=1)
    block = block.reshape(blocks, FOLD, block.shape[1]).astype(BF16)
    if merges:
        which = which_ref[0]
        out_ref[:, which] = block
        out_ref[:, 1 - which] = refs[0][...]
    else:
        out_ref[...] = block


def finish_kernel(pieces, width, in_ref, pick_ref, grad_ref, router_ref):
    nodes = in_ref.shape[0]
    pick = pick_ref[...]
    groups, tokens = pick.shape
    named, slot, hits = pair_maps(pick, nodes)
    rows = in_ref[...].astype(F32).reshape(nodes * FOLD, in_ref.shape[2])
    base = pieces * width
    total = jnp.zeros((width, tokens), F32)
    routed = jnp.zeros((nodes * FOLD, tokens), F32)
    for piece in range(pieces):
        place = placing(named, slot, piece)
        total = total + tn(
            rows[:, piece * width : (piece + 1) * width].astype(BF16), place.astype(BF16)
        )
        routed = routed + place * rows[:, base + piece : base + piece + 1]
    grad_ref[...] = total.astype(BF16)
    router = [jnp.sum(routed * hit, axis=0, keepdims=True) for hit in hits]
    router_ref[...] = jnp.concatenate(router, axis=0).astype(BF16)


def per_device(
    out_grad,
    node_pick,
    expert_pick,
    pick_weight,
    gate_weight,
    up_weight,
    down_weight,
    saved_gate,
    saved_up,
):
    nodes = lax.axis_size("node")
    local_count = lax.axis_size("local")
    tokens, width = out_grad.shape
    groups = node_pick.shape[1]
    experts, units = gate_weight.shape[1], gate_weight.shape[3]
    slots = saved_gate.shape[1]
    chips = local_count // 2
    pieces = slots // FOLD
    held = round_up(slots + 1, 8)
    block = round_up(pieces * width + 2 * pieces, LANES)
    core = (lax.axis_index("local") % 2).astype(jnp.int32)
    mine = core.reshape(1)
    other = 1 - mine
    same_core = [[2 * chip + c for chip in range(chips)] for c in range(2)]
    swap = [(at, at ^ 1) for at in range(local_count)]

    pick = node_pick.T
    gate_saved = saved_gate.reshape(slots, units)
    up_saved = saved_up.reshape(slots, units)
    down = jnp.swapaxes(down_weight[0], 1, 2)

    factors = call(factors_kernel, jax.ShapeDtypeStruct((2, held, units), BF16))(
        gate_saved, up_saved
    )
    factors = lax.all_gather(factors, "local", axis=0, tiled=False)
    factors = factors.reshape(chips, 2, 2, held, units)

    sent = call(
        functools.partial(prepare_kernel, pieces),
        jax.ShapeDtypeStruct((nodes, FOLD, block), BF16),
    )(pick, jnp.transpose(expert_pick, (1, 2, 0)), pick_weight[:, :, 0].T, out_grad.T)
    arrived = lax.all_to_all(sent, "node", split_axis=0, concat_axis=0, tiled=True)
    arrived = arrived.reshape(nodes // 2, 2, FOLD, block)

    def whole(shape):
        return pl.BlockSpec(shape, lambda i, which: (0,) * len(shape))

    def raw_part(which, received):
        adds = received is not None
        half = nodes // 2
        grid_spec = pltpu.PrefetchScalarGridSpec(
            num_scalar_prefetch=1,
            grid=(1,),
            in_specs=[
                pl.BlockSpec((half, 1, FOLD, block), lambda i, which: (0, which[0], 0, 0)),
                whole(down.shape),
            ]
            + ([whole((half, held, units))] if adds else []),
            out_specs=[whole((half, held, units)), whole((half * held, 2))],
        )
        return call(
            functools.partial(raw_kernel, pieces, width, held, adds),
            (
                jax.ShapeDtypeStruct((half, held, units), BF16),
                jax.ShapeDtypeStruct((half * held, 2), F32),
            ),
            grid_spec=grid_spec,
        )(which, arrived, down, *([received] if adds else []))

    theirs, other_meta = raw_part(other, None)
    received = lax.ppermute(theirs, "local", swap)
    partial, mine_meta = raw_part(mine, received)
    parts = lax.all_to_all(
        partial, "local", split_axis=0, concat_axis=0, axis_index_groups=same_core, tiled=True
    )
    spread = call(hidden_kernel, jax.ShapeDtypeStruct((chips, held, units), BF16))(
        parts, gate_saved, up_saved
    )
    raw_mine = lax.all_to_all(
        spread, "local", split_axis=0, concat_axis=0, axis_index_groups=same_core, tiled=True
    )
    raw_other = lax.ppermute(raw_mine, "local", swap)

    def back_part(which, raw, meta, done):
        merges = done is not None
        half = nodes // 2
        shape = (half, 2, FOLD, block) if merges else (half, FOLD, block)
        grid_spec = pltpu.PrefetchScalarGridSpec(
            num_scalar_prefetch=1,
            grid=(1,),
            in_specs=[
                whole((half, held, units)),
                pl.BlockSpec(
                    (half, 1, 2, held, units), lambda i, which: (0, which[0], 0, 0, 0)
                ),
                whole(meta.shape),
                whole((experts, width, units)),
                whole((experts, width, units)),
            ]
            + ([whole(done.shape)] if merges else []),
            out_specs=whole(shape),
        )
        return call(
            functools.partial(back_kernel, pieces, width, merges),
            jax.ShapeDtypeStruct(shape, BF16),
            grid_spec=grid_spec,
        )(which, raw, factors, meta, gate_weight[0], up_weight[0], *([done] if merges else []))

    back = back_part(mine, raw_mine, mine_meta, None)
    back = back_part(other, raw_other, other_meta, back)
    back = back.reshape(nodes, FOLD, block)
    returned = lax.all_to_all(back, "node", split_axis=0, concat_axis=0, tiled=True)
    grad, router = call(
        functools.partial(finish_kernel, pieces, width),
        (
            jax.ShapeDtypeStruct((width, tokens), BF16),
            jax.ShapeDtypeStruct((groups, tokens), BF16),
        ),
    )(returned, pick)
    return grad.T, router.T.reshape(tokens, groups, 1)


def solution(mesh):
    return jax.shard_map(
        per_device,
        mesh=mesh,
        in_specs=(
            P("node", "local"),
            P("node", None),
            P("node", None, None),
            P("node", None, None),
            P("node", None, "local", None),
            P("node", None, "local", None),
            P("node", None, None, "local"),
            P("node", "local", None, None),
            P("node", "local", None, None),
        ),
        out_specs=(P("node", "local"), P("node", None, None)),
        check_vma=False,
    )
```

time: 489 us -> 206 us (0.42)
  waiting for transfers between devices: 236 us -> 46.4 us
  blocking collectives: 145 us -> 87.4 us
  starting transfers between devices: 53.7 us -> 38.4 us
  local copies, waits for them, and re-layouts: 24.1 us -> 9.89 us
  matrix products: 10.6 us -> 0 us
  Pallas kernels: 0 us -> 9.21 us
    all_gather x2 -> x1, waiting for transfers between devices: 75.1 us -> 0.02 us  [per_device(): factors = lax.all_gather(factors, 'local', axis=0, tiled=False)]
    reduce_scatter x1 -> x0, waiting for transfers between devices: 67.7 us -> none  [per_device(): lax.psum_scatter(projected.reshape(own_slots * experts * lax.axis_size('l...]
    unnamed x1 -> x0, blocking collectives: 64.4 us -> none
    all_to_all x4 -> x1, waiting for transfers between devices: 92 us -> 44.5 us  [per_device(): lax.all_to_all(sent, 'node', split_axis=0, concat_axis=0, tiled=True)]
    all_to_all x4 -> x1, starting transfers between devices: 53.6 us -> 29.3 us  [per_device(): lax.all_to_all(sent, 'node', split_axis=0, concat_axis=0, tiled=True)]
    reshape x10 -> x0, local copies, waits for them, and re-layouts: 12.1 us -> none  [the longest x1 7.59 us: per_device(): projected.reshape(own_slots * experts * lax.axis_size('local'), projected...]
    dot_general x8 -> x0, matrix products: 10.6 us -> none  [the longest x1 3.77 us: per_device(): jnp.einsum('sef,edf->sd', gate_piece, gate_local, preferred_element_type=...]
    pallas_call x0 -> x8, Pallas kernels: none -> 9.21 us  [the longest x2 3.25 us: back_part(): call(functools.partial(back_kernel, pieces, width, merges), jax.ShapeDtyp...]
  transfers between devices with their start and end apart: 7 -> 4, of which waited for: 5 -> 2; matrix products, arithmetic and copies ran while one was open for 3% -> 0% of each run, Pallas kernels for 0% -> 3%
where the time goes in v1:
time: 206 us
  blocking collectives  87.4 us (42%)
  waiting for transfers between devices  46.4 us (23%)
  starting transfers between devices  38.4 us (19%)
  between operations  14.2 us (7%)
  local copies, waits for them, and re-layouts  9.89 us (5%)
  Pallas kernels  9.21 us (4%)
    all_to_all x1, blocking collectives, per_device(): lax.all_to_all(back, 'node', split_axis=0, concat_axis=0, tiled=True)  52.4 us
    all_to_all x1, waiting for transfers between devices, per_device(): lax.all_to_all(sent, 'node', split_axis=0, concat_axis=0, tiled=True)  44.5 us
    all_to_all x1, starting transfers between devices, per_device(): lax.all_to_all(sent, 'node', split_axis=0, concat_axis=0, tiled=True)  29.3 us
    all_to_all x1, blocking collectives, per_device(): lax.all_to_all(partial, 'local', split_axis=0, concat_axis=0, axis_index_...  19.8 us
    all_to_all x1, blocking collectives, per_device(): lax.all_to_all(spread, 'local', split_axis=0, concat_axis=0, axis_index_g...  15.1 us
    unnamed x38, local copies, waits for them, and re-layouts  9.89 us
    ppermute x1, starting transfers between devices, per_device(): raw_other = lax.ppermute(raw_mine, 'local', swap)  5.24 us
  transfers between devices with their start and end apart: 4, of which 2 were waited for; matrix products, arithmetic and copies ran while one was open for 0% of the time, Pallas kernels for 3%

profile of v1, /device:TPU:1, one launch (start us, length us, event | category | flops | bytes accessed | tf_op | source)
XLA Modules:
  0.0 205.5 jit_solution(7468839221384545266)
XLA Ops:
  7.2 0.0 all-gather.3.cloned.1.call-start
  7.2 0.8 copy-done.10
  8.0 0.8 copy-done.12
  8.8 0.7 shard_map.108
  9.5 0.0 all-gather.3.cloned.1.call-update
  9.5 0.8 copy-done.14
  10.4 0.7 copy-done.15
  11.0 0.7 copy-done.17
  11.7 0.7 copy-done.18
  12.4 1.4 shard_map.104
  13.8 29.3 %all-to-all-start = ((bf16[32,4,1152]{2,1,0:T(4,128)(2,1)}), bf16[32,4,1152]{2,1,0:T(4,128)(2,1)S(1)}, u32[]{:S(2)}, u32[]{:S(2)}) async-start(bf16[32,4,1152]{2,1,0:T(4,128)(2,1)} %shard_map.104), calls=%async_computation | async-start | bytes 589824 | tf_op jit(solution)/shard_map/all_to_all | solution.py:262
  43.1 44.5 %all-to-all-done = bf16[32,4,1152]{2,1,0:T(4,128)(2,1)S(1)} async-done(((bf16[32,4,1152]{2,1,0:T(4,128)(2,1)}), bf16[32,4,1152]{2,1,0:T(4,128)(2,1)S(1)}, u32[]{:S(2)}, u32[]{:S(2)}) %all-to-all-start) | async-done | bytes 294944 | tf_op jit(solution)/shard_map/all_to_all | solution.py:262
  87.5 1.2 copy-done.4
  88.7 1.2 shard_map.105
  90.0 0.0 copy-start.2
  90.0 0.0 copy-start.3
  90.0 3.9 %collective-permute-start = (bf16[16,24,1024]{2,1,0:T(8,128)(2,1)S(1)}, bf16[16,24,1024]{2,1,0:T(8,128)(2,1)S(1)}, u32[]{:S(2)}, u32[]{:S(2)}) collective-permute-start(bf16[16,24,1024]{2,1,0:T(8,128)(2,1)S(1)} %get-tuple-element.8), channel_id=1, source_target_pairs={{0,1},{1,0},{2,3},{3,2},{4,5},{5,4},{6,7},{7,6},{8,9},{9,8},{10,11... | collective-permute-start | bytes 2359304 | tf_op jit(solution)/shard_map/ppermute | solution.py:291
  93.9 1.9 collective-permute-done.refs_0_
  95.8 1.2 copy-done.5
  96.9 1.2 shard_map.106
  98.2 19.8 %all_to_all.20.parts_ref = bf16[16,24,1024]{2,1,0:T(8,128)(2,1)S(1)} all-to-all(bf16[16,24,1024]{2,1,0:T(8,128)(2,1)S(1)} %get-tuple-element.9), channel_id=1, replica_groups={{0,2,4,6,8,10,12,14,16,18,20,22,24,26,28,30},{1,3,5,7,9,11,13,15,17,19,..., dimensions={0} | all-to-all | bytes 1572864 | tf_op jit(solution)/shard_map/all_to_all | solution.py:293
  118.0 0.2 shard_map.107
  118.2 15.1 %all_to_all.21.raw_ref = bf16[16,24,1024]{2,1,0:T(8,128)(2,1)S(1)} all-to-all(bf16[16,24,1024]{2,1,0:T(8,128)(2,1)S(1)} %shard_map.107), channel_id=1, replica_groups={{0,2,4,6,8,10,12,14,16,18,20,22,24,26,28,30},{1,3,5,7,9,11,13,15,17,19,..., dimensions={0} | all-to-all | bytes 1572864 | tf_op jit(solution)/shard_map/all_to_all | solution.py:299
  133.4 5.2 %collective-permute-start.1 = (bf16[16,24,1024]{2,1,0:T(8,128)(2,1)S(1)}, bf16[16,24,1024]{2,1,0:T(8,128)(2,1)S(1)}, u32[]{:S(2)}, u32[]{:S(2)}) collective-permute-start(bf16[16,24,1024]{2,1,0:T(8,128)(2,1)S(1)} %all_to_all.21.raw_ref), channel_id=1, source_target_pairs={{0,1},{1,0},{2,3},{3,2},{4,5},{5,4},{6,7},{7,6},{8,9},{9,8},{10,11... | collective-permute-start | bytes 2359304 | tf_op jit(solution)/shard_map/ppermute | solution.py:302
  138.6 0.0 all-gather.3.cloned.1.call-done
  138.7 1.9 copy-done
  140.5 0.9 copy-done.9
  141.5 1.6 shard_map.109.refs_0_
  143.1 0.2 copy-done.1
  143.4 1.6 shard_map.110
  145.0 52.4 %all_to_all.22.in_ref = bf16[32,4,1152]{2,1,0:T(4,128)(2,1)S(1)} all-to-all(bf16[32,4,1152]{2,1,0:T(4,128)(2,1)S(1)} %bitcast.31), channel_id=1, replica_groups=mesh['node'=32,'local'=32] {'node'}, dimensions={0} | all-to-all | bytes 589824 | tf_op jit(solution)/shard_map/all_to_all | solution.py:332
  197.4 1.2 shard_map.111
  (26 shorter events, 0.1 us)
Async XLA Ops:
  7.2 131.5 %all-gather.3.cloned.1.call-start = ((), (), s32[]{:S(2)}) async-start(), calls=%async_computation.4 | async-start | bytes 3244032 | tf_op jit(solution)/shard_map/all_gather | solution.py:255
  7.2 0.8 copy-start.10
  8.0 0.8 copy-start.12
  8.8 109.2 %copy-start.11 = (bf16[1,20,1,1024]{3,1,2,0:T(8,128)(2,1)S(1)}, bf16[1,20,1,1024]{3,1,2,0:T(8,128)(2,1)}, u32[]{:S(2)}) copy-start(bf16[1,20,1,1024]{3,1,2,0:T(8,128)(2,1)} %param.16) | copy-start | bytes 122884
  8.8 109.2 %copy-start.13 = (bf16[1,20,1,1024]{3,1,2,0:T(8,128)(2,1)S(1)}, bf16[1,20,1,1024]{3,1,2,0:T(8,128)(2,1)}, u32[]{:S(2)}) copy-start(bf16[1,20,1,1024]{3,1,2,0:T(8,128)(2,1)} %param.17) | copy-start | bytes 122884
  9.5 0.8 copy-start.14
  10.4 0.7 copy-start.15
  11.0 0.7 copy-start.17
  11.7 0.7 copy-start.18
  13.8 73.8 %all-to-all-start = ((bf16[32,4,1152]{2,1,0:T(4,128)(2,1)}), bf16[32,4,1152]{2,1,0:T(4,128)(2,1)S(1)}, u32[]{:S(2)}, u32[]{:S(2)}) async-start(bf16[32,4,1152]{2,1,0:T(4,128)(2,1)} %shard_map.104), calls=%async_computation | async-start | bytes 589824 | tf_op jit(solution)/shard_map/all_to_all | solution.py:262
  87.5 1.2 copy-start.4
  90.0 8.2 %copy-start.6 = (f32[384,2]{1,0:T(8,128)}, f32[384,2]{1,0:T(8,128)S(1)}, u32[]{:S(2)}) copy-start(f32[384,2]{1,0:T(8,128)S(1)} %get-tuple-element.10.meta_ref) | copy-start | bytes 9220
  90.0 48.7 %copy-start.2 = (bf16[1,2,224,1024]{3,2,1,0:T(8,128)(2,1)S(1)}, bf16[1,2,224,1024]{3,2,1,0:T(8,128)(2,1)}, u32[]{:S(2)}) copy-start(bf16[1,2,224,1024]{3,2,1,0:T(8,128)(2,1)} %param.13) | copy-start | bytes 2752516
  90.0 48.7 %copy-start.3 = (bf16[1,2,224,1024]{3,2,1,0:T(8,128)(2,1)S(1)}, bf16[1,2,224,1024]{3,2,1,0:T(8,128)(2,1)}, u32[]{:S(2)}) copy-start(bf16[1,2,224,1024]{3,2,1,0:T(8,128)(2,1)} %param.14) | copy-start | bytes 2752516
  90.0 5.8 %collective-permute-start = (bf16[16,24,1024]{2,1,0:T(8,128)(2,1)S(1)}, bf16[16,24,1024]{2,1,0:T(8,128)(2,1)S(1)}, u32[]{:S(2)}, u32[]{:S(2)}) collective-permute-start(bf16[16,24,1024]{2,1,0:T(8,128)(2,1)S(1)} %get-tuple-element.8), channel_id=1, source_target_pairs={{0,1},{1,0},{2,3},{3,2},{4,5},{5,4},{6,7},{7,6},{8,9},{9,8},{10,11... | collective-permute-start | bytes 2359304 | tf_op jit(solution)/shard_map/ppermute | solution.py:291
  95.8 1.2 copy-start.5
  98.2 35.2 %copy-start.8 = (f32[384,2]{1,0:T(8,128)}, f32[384,2]{1,0:T(8,128)S(1)}, u32[]{:S(2)}) copy-start(f32[384,2]{1,0:T(8,128)S(1)} %get-tuple-element.11.meta_ref) | copy-start | bytes 9220
  133.4 9.7 %collective-permute-start.1 = (bf16[16,24,1024]{2,1,0:T(8,128)(2,1)S(1)}, bf16[16,24,1024]{2,1,0:T(8,128)(2,1)S(1)}, u32[]{:S(2)}, u32[]{:S(2)}) collective-permute-start(bf16[16,24,1024]{2,1,0:T(8,128)(2,1)S(1)} %all_to_all.21.raw_ref), channel_id=1, source_target_pairs={{0,1},{1,0},{2,3},{3,2},{4,5},{5,4},{6,7},{7,6},{8,9},{9,8},{10,11... | collective-permute-start | bytes 2359304 | tf_op jit(solution)/shard_map/ppermute | solution.py:302
  138.7 1.9 copy-start
  140.5 0.9 copy-start.9
  141.5 1.9 copy-start.1
  141.5 1.9 copy-start.7
  143.4 54.1 %copy-start.16 = (s32[128,4]{0,1:T(4,128)S(1)}, s32[128,4]{0,1:T(4,128)}, u32[]{:S(2)}) copy-start(s32[128,4]{0,1:T(4,128)} %param.10) | copy-start | bytes 6148
Sparse Core Ops, SparseCore 0:
  12.3 89.6 all-gather.2

commit v2 on v1

v2 whole, which is shorter than its diff:
```python
import functools

import jax
import jax.numpy as jnp
from jax import lax
from jax.experimental import pallas as pl
from jax.experimental.pallas import tpu as pltpu
from jax.sharding import PartitionSpec as P

BF16 = jnp.bfloat16
F32 = jnp.float32
LANES = 128
FOLD = 4
VMEM_LIMIT = 32 * 1024 * 1024
VMEM_MOST = 58 * 1024 * 1024
VMEM_BACK = 48 * 1024 * 1024


def round_up(value, unit):
    return -(-value // unit) * unit


def nn(a, b):
    return lax.dot_general(a, b, (((1,), (0,)), ((), ())), preferred_element_type=F32)


def nt(a, b):
    return lax.dot_general(a, b, (((1,), (1,)), ((), ())), preferred_element_type=F32)


def tn(a, b):
    return lax.dot_general(a, b, (((0,), (0,)), ((), ())), preferred_element_type=F32)


def iota(shape, axis):
    return lax.broadcasted_iota(jnp.int32, shape, axis)


def call(kernel, out_shape, limit=VMEM_LIMIT, **extra):
    return pl.pallas_call(
        kernel,
        out_shape=out_shape,
        compiler_params=pltpu.CompilerParams(vmem_limit_bytes=limit),
        **extra,
    )


def pair_maps(pick, nodes):
    groups, tokens = pick.shape
    rows = nodes * FOLD
    node_of = iota((rows, tokens), 0) // FOLD
    hits = [(pick[g : g + 1, :] == node_of).astype(F32) for g in range(groups)]
    named = functools.reduce(jnp.add, hits)
    earlier = (iota((tokens, tokens), 0) < iota((tokens, tokens), 1)).astype(BF16)
    slot = nn(named.astype(BF16), earlier).astype(jnp.int32)
    return named, slot, hits


def placing(named, slot, piece):
    row = iota(named.shape, 0) % FOLD
    return jnp.where(slot == piece * FOLD + row, named, 0.0)


def fetch(copies):
    for copy in copies:
        copy.start()


def pack(rows, slots):
    tiles = rows.shape[-1] // LANES
    axis = rows.ndim - 2
    pieces = [
        rows[..., :slots, tile * LANES : (tile + 1) * LANES] for tile in range(tiles)
    ]
    return [jnp.concatenate(pieces[at : at + 4], axis=axis) for at in range(0, tiles, 4)]


def prepare_kernel(
    pieces,
    pick_hbm,
    expert_hbm,
    weight_hbm,
    rows_hbm,
    gate_hbm,
    up_hbm,
    out_ref,
    factor_ref,
    pick_ref,
    expert_ref,
    weight_ref,
    rows_ref,
    gate_ref,
    up_ref,
    sems,
):
    pairs = [
        (pick_hbm, pick_ref),
        (expert_hbm, expert_ref),
        (weight_hbm, weight_ref),
        (rows_hbm, rows_ref),
        (gate_hbm, gate_ref),
        (up_hbm, up_ref),
    ]
    copies = [
        pltpu.make_async_copy(source, target, sems.at[at])
        for at, (source, target) in enumerate(pairs)
    ]
    fetch(copies)
    nodes = out_ref.shape[0]
    width, tokens = rows_ref.shape
    rows = nodes * FOLD
    for copy in copies[:4]:
        copy.wait()
    pick = pick_ref[...]
    named, slot, hits = pair_maps(pick, nodes)
    expert = functools.reduce(
        jnp.add, [hit * expert_ref[g].astype(F32) for g, hit in enumerate(hits)]
    )
    weights = weight_ref[...].astype(F32)
    weight = functools.reduce(
        jnp.add, [hit * weights[g : g + 1, :] for g, hit in enumerate(hits)]
    )
    token_rows = rows_ref[...]
    spare = out_ref.shape[2] - pieces * width
    lane = iota((rows, spare), 1)
    meta = jnp.zeros((rows, spare), F32)
    parts = []
    for piece in range(pieces):
        place = placing(named, slot, piece)
        parts.append(nt(place.astype(BF16), token_rows))
        picked = jnp.sum(place * expert, axis=1, keepdims=True)
        scale = jnp.sum(place * weight, axis=1, keepdims=True)
        meta = jnp.where(lane == piece, picked, meta)
        meta = jnp.where(lane == pieces + piece, scale, meta)
    block = jnp.concatenate(parts + [meta], axis=1)
    out_ref[...] = block.reshape(nodes, FOLD, block.shape[1]).astype(BF16)
    for copy in copies[4:]:
        copy.wait()
    gate = gate_ref[...].astype(F32)
    up = up_ref[...].astype(F32)
    sig = jax.nn.sigmoid(gate)
    slots = gate.shape[0]
    by_gate = up * sig * (1.0 + gate * (1.0 - sig))
    by_up = gate * sig
    for at, factor in enumerate((by_gate, by_up)):
        factor_ref[at] = jnp.concatenate(pack(factor, slots), axis=0).astype(BF16)


def keep_kernel(in_ref, after_ref, out_ref):
    out_ref[...] = in_ref[...]


def unfold_matrix(blocks, pieces, held):
    shape = (blocks * held, pieces * blocks * FOLD)
    row, column = iota(shape, 0), iota(shape, 1)
    slot = row % held
    source = (slot // FOLD) * (blocks * FOLD) + (row // held) * FOLD + slot % FOLD
    return jnp.where(jnp.logical_and(source == column, slot < pieces * FOLD), 1.0, 0.0).astype(BF16)


def raw_kernel(pieces, width, held, which_ref, in_ref, down_ref, out_ref, meta_ref):
    blocks = out_ref.shape[0]
    units = down_ref.shape[2]
    slots = pieces * FOLD
    folded = in_ref[:, which_ref[0]].astype(F32).reshape(blocks * FOLD, in_ref.shape[3])
    base = pieces * width
    pad = 2 * LANES - width
    stacked = []
    for piece in range(pieces):
        columns = [
            folded[:, piece * width : (piece + 1) * width],
            folded[:, base + piece : base + piece + 1],
            folded[:, base + pieces + piece : base + pieces + piece + 1],
            jnp.zeros((blocks * FOLD, pad - 2), F32),
        ]
        stacked.append(jnp.concatenate(columns, axis=1))
    stacked = jnp.concatenate(stacked, axis=0).astype(BF16)
    rows = nn(unfold_matrix(blocks, pieces, held), stacked)
    arrived = rows[:, :width]
    meta = rows[:, width : width + 2]
    first = meta[:, 0:1] == 0.0
    zero = jnp.zeros_like(arrived)
    raw = nn(jnp.where(first, arrived, zero).astype(BF16), down_ref[0])
    raw = raw + nn(jnp.where(first, zero, arrived).astype(BF16), down_ref[1])
    parts = pack(raw.reshape(blocks, held, units), slots)
    rows = parts[0].shape[1]
    for at, part in enumerate(parts):
        out_ref[:, at * rows : (at + 1) * rows, :] = part.astype(out_ref.dtype)
    meta_ref[...] = meta


def add_kernel(mine_ref, other_ref, out_ref):
    out_ref[...] = (mine_ref[...] + other_ref[...].astype(F32)).astype(BF16)


def hidden_kernel(parts_ref, gate_ref, up_ref, out_ref):
    blocks, rows, _ = parts_ref.shape
    total = parts_ref[0].astype(F32)
    for at in range(1, blocks):
        total = total + parts_ref[at].astype(F32)
    slots, units = gate_ref.shape
    raw = jnp.concatenate(
        [total[tile * slots : (tile + 1) * slots] for tile in range(units // LANES)], axis=1
    )
    gate = gate_ref[...].astype(F32)
    up = up_ref[...].astype(F32)
    hidden = gate * jax.nn.sigmoid(gate) * up
    router = jnp.sum(hidden * raw, axis=1, keepdims=True)
    diagonal = iota((slots, LANES), 0) == iota((slots, LANES), 1)
    router_row = jnp.sum(jnp.where(diagonal, router, 0.0), axis=0, keepdims=True)
    spare = out_ref.shape[1] - rows
    extra = jnp.where(iota((spare, LANES), 0) == 0, router_row, 0.0)
    block = jnp.concatenate([total, extra], axis=0).astype(BF16)
    for at in range(blocks):
        out_ref[at] = block


def back_kernel(
    pieces, width, held, merges, which_ref, raw_ref, meta_hbm, gate_ref, up_ref, *refs
):
    blocks = raw_ref.shape[0]
    units = gate_ref.shape[2]
    tiles = units // LANES
    slots = pieces * FOLD
    which = which_ref[0]
    if merges:
        factor_ref, done_ref, out_ref, meta_ref, sems = refs
        copies = [pltpu.make_async_copy(meta_hbm, meta_ref, sems.at[0])]
    else:
        factor_hbm, out_ref, later_ref, factor_ref, meta_ref, sems = refs
        copies = [
            pltpu.make_async_copy(meta_hbm, meta_ref, sems.at[0]),
            pltpu.make_async_copy(factor_hbm.at[:, which], factor_ref, sems.at[1]),
            pltpu.make_async_copy(factor_hbm.at[:, 1 - which], later_ref, sems.at[2]),
        ]
    fetch(copies)
    unfold = unfold_matrix(blocks, pieces, held)
    raw = raw_ref[...].astype(F32)
    for copy in copies[:2]:
        copy.wait()
    spare = jnp.zeros((blocks, held - slots + 4, LANES), F32)

    def spread(at):
        packed = raw[:, : tiles * slots] * factor_ref[:, at].astype(F32)
        packed = jnp.concatenate([packed, spare], axis=1)
        parts = [
            packed[:, tile * slots : tile * slots + held].reshape(blocks * held, LANES)
            for tile in range(tiles)
        ]
        return jnp.concatenate(parts, axis=1).astype(BF16)

    by_gate = spread(0)
    by_up = spread(1)
    meta = meta_ref[...]
    first = meta[:, 0:1] == 0.0
    back = jnp.where(
        first,
        nt(by_gate, gate_ref[0]) + nt(by_up, up_ref[0]),
        nt(by_gate, gate_ref[1]) + nt(by_up, up_ref[1]),
    )
    back = (back * meta[:, 1:2]).astype(BF16)
    folded = tn(unfold, back)
    rows = blocks * FOLD
    parts = [folded[piece * rows : (piece + 1) * rows] for piece in range(pieces)]
    router = raw[:, tiles * slots].astype(BF16)
    repeat = (iota((rows, blocks), 0) // FOLD == iota((rows, blocks), 1)).astype(F32).astype(BF16)
    router = nn(repeat, router)
    kept = jnp.logical_and(
        iota((rows, LANES), 1) % FOLD == iota((rows, LANES), 0) % FOLD,
        iota((rows, LANES), 1) < slots,
    )
    router = jnp.where(kept, router, 0.0).astype(BF16)
    lanes_left = out_ref.shape[-1] - pieces * width
    gather = iota((LANES, lanes_left), 0) // FOLD == iota((LANES, lanes_left), 1)
    parts.append(nn(router, gather.astype(F32).astype(BF16)))
    block = jnp.concatenate(parts, axis=1)
    block = block.reshape(blocks, FOLD, block.shape[1]).astype(BF16)
    if merges:
        out_ref[:, which] = block
        out_ref[:, 1 - which] = done_ref[...]
    else:
        out_ref[...] = block
    for copy in copies[2:]:
        copy.wait()


def finish_kernel(pieces, width, in_ref, pick_ref, grad_ref, router_ref):
    nodes = in_ref.shape[0]
    pick = pick_ref[...]
    groups, tokens = pick.shape
    named, slot, hits = pair_maps(pick, nodes)
    rows = in_ref[...].astype(F32).reshape(nodes * FOLD, in_ref.shape[2])
    base = pieces * width
    total = jnp.zeros((width, tokens), F32)
    routed = jnp.zeros((nodes * FOLD, tokens), F32)
    for piece in range(pieces):
        place = placing(named, slot, piece)
        total = total + tn(
            rows[:, piece * width : (piece + 1) * width].astype(BF16), place.astype(BF16)
        )
        routed = routed + place * rows[:, base + piece : base + piece + 1]
    grad_ref[...] = total.astype(BF16)
    router = [jnp.sum(routed * hit, axis=0, keepdims=True) for hit in hits]
    router_ref[...] = jnp.concatenate(router, axis=0).astype(BF16)


def per_device(
    out_grad,
    node_pick,
    expert_pick,
    pick_weight,
    gate_weight,
    up_weight,
    down_weight,
    saved_gate,
    saved_up,
):
    nodes = lax.axis_size("node")
    local_count = lax.axis_size("local")
    tokens, width = out_grad.shape
    groups = node_pick.shape[1]
    experts, units = gate_weight.shape[1], gate_weight.shape[3]
    slots = saved_gate.shape[1]
    chips = local_count // 2
    pieces = slots // FOLD
    tiles = units // LANES
    half = nodes // 2
    held = round_up(slots, 8)
    packed = tiles * slots
    block = round_up(pieces * width + 2 * pieces, LANES)
    core = (lax.axis_index("local") % 2).astype(jnp.int32)
    mine = core.reshape(1)
    other = 1 - mine
    same_core = [[2 * chip + c for chip in range(chips)] for c in range(2)]
    swap = [(at, at ^ 1) for at in range(local_count)]

    pick = node_pick.T
    gate_saved = saved_gate.reshape(slots, units)
    up_saved = saved_up.reshape(slots, units)
    down = jnp.swapaxes(down_weight[0], 1, 2)
    hbm = pl.BlockSpec(memory_space=pltpu.HBM)
    vmem = pl.BlockSpec(memory_space=pltpu.VMEM)
    smem = pl.BlockSpec(memory_space=pltpu.SMEM)

    sent, factors = call(
        functools.partial(prepare_kernel, pieces),
        (
            jax.ShapeDtypeStruct((nodes, FOLD, block), BF16),
            jax.ShapeDtypeStruct((2, packed, LANES), BF16),
        ),
        limit=VMEM_MOST,
        in_specs=[hbm] * 6,
        out_specs=[vmem] * 2,
        scratch_shapes=[
            pltpu.VMEM((groups, tokens), jnp.int32),
            pltpu.VMEM((groups, 1, tokens), jnp.int32),
            pltpu.VMEM((groups, tokens), BF16),
            pltpu.VMEM((width, tokens), BF16),
            pltpu.VMEM((slots, units), BF16),
            pltpu.VMEM((slots, units), BF16),
            pltpu.SemaphoreType.DMA((6,)),
        ],
    )(
        pick,
        jnp.transpose(expert_pick, (1, 2, 0)),
        pick_weight[:, :, 0].T,
        out_grad.T,
        gate_saved,
        up_saved,
    )
    down = call(
        keep_kernel,
        jax.ShapeDtypeStruct(down.shape, BF16),
        in_specs=[vmem, hbm],
        out_specs=vmem,
    )(down, factors)
    factors = lax.all_gather(factors, "local", axis=0, tiled=False)
    factors = factors.reshape(chips, 2, 2, packed, LANES)
    arrived = lax.all_to_all(sent, "node", split_axis=0, concat_axis=0, tiled=True)
    arrived = arrived.reshape(half, 2, FOLD, block)

    def raw_part(which, dtype):
        return call(
            functools.partial(raw_kernel, pieces, width, held),
            (
                jax.ShapeDtypeStruct((half, packed, LANES), dtype),
                jax.ShapeDtypeStruct((half * held, 2), F32),
            ),
            in_specs=[smem, vmem, vmem],
            out_specs=[vmem, vmem],
        )(which, arrived, down)

    theirs, other_meta = raw_part(other, BF16)
    received = lax.ppermute(theirs, "local", swap)
    partial, mine_meta = raw_part(mine, F32)
    partial = call(add_kernel, jax.ShapeDtypeStruct((half, packed, LANES), BF16))(
        partial, received
    )
    parts = lax.all_to_all(
        partial, "local", split_axis=0, concat_axis=0, axis_index_groups=same_core, tiled=True
    )
    spread = call(
        hidden_kernel, jax.ShapeDtypeStruct((chips, packed + 16, LANES), BF16)
    )(parts, gate_saved, up_saved)
    raw_mine = lax.all_to_all(
        spread, "local", split_axis=0, concat_axis=0, axis_index_groups=same_core, tiled=True
    )
    raw_other = lax.ppermute(raw_mine, "local", swap)

    factor_shape = (half, 2, packed, LANES)
    meta_shape = (half * held, 2)
    back, later = call(
        functools.partial(back_kernel, pieces, width, held, False),
        (
            jax.ShapeDtypeStruct((half, FOLD, block), BF16),
            jax.ShapeDtypeStruct(factor_shape, BF16),
        ),
        limit=VMEM_BACK,
        in_specs=[smem, vmem, hbm, vmem, vmem, hbm],
        out_specs=[vmem, vmem],
        scratch_shapes=[
            pltpu.VMEM(factor_shape, BF16),
            pltpu.VMEM(meta_shape, F32),
            pltpu.SemaphoreType.DMA((3,)),
        ],
    )(mine, raw_mine, mine_meta, gate_weight[0], up_weight[0], factors)
    back = call(
        functools.partial(back_kernel, pieces, width, held, True),
        jax.ShapeDtypeStruct((half, 2, FOLD, block), BF16),
        in_specs=[smem, vmem, hbm, vmem, vmem, vmem, vmem],
        out_specs=vmem,
        scratch_shapes=[pltpu.VMEM(meta_shape, F32), pltpu.SemaphoreType.DMA((1,))],
    )(other, raw_other, other_meta, gate_weight[0], up_weight[0], later, back)
    back = back.reshape(nodes, FOLD, block)
    returned = lax.all_to_all(back, "node", split_axis=0, concat_axis=0, tiled=True)
    grad, router = call(
        functools.partial(finish_kernel, pieces, width),
        (
            jax.ShapeDtypeStruct((width, tokens), BF16),
            jax.ShapeDtypeStruct((groups, tokens), BF16),
        ),
    )(returned, pick)
    return grad.T, router.T.reshape(tokens, groups, 1)


def solution(mesh):
    return jax.shard_map(
        per_device,
        mesh=mesh,
        in_specs=(
            P("node", "local"),
            P("node", None),
            P("node", None, None),
            P("node", None, None),
            P("node", None, "local", None),
            P("node", None, "local", None),
            P("node", None, None, "local"),
            P("node", "local", None, None),
            P("node", "local", None, None),
        ),
        out_specs=(P("node", "local"), P("node", None, None)),
        check_vma=False,
    )
```

time: 206 us -> 195 us (0.947)
  local copies, waits for them, and re-layouts: 9.89 us -> 3.7 us
  waiting for transfers between devices: 46.4 us -> 42.4 us
  blocking collectives: 87.4 us -> 84.9 us
  Pallas kernels: 9.21 us -> 11.5 us
    unnamed x38 -> x18, local copies, waits for them, and re-layouts: 9.89 us -> 3.7 us
    pallas_call x7 -> x8, Pallas kernels: 7.99 us -> 10.3 us  [the longest x1 2.97 us: per_device(): call(functools.partial(back_kernel, pieces, width, held, False), (jax.Sha...]
    all_to_all x1, waiting for transfers between devices: 44.5 us -> 42.4 us  [per_device(): lax.all_to_all(sent, 'node', split_axis=0, concat_axis=0, tiled=True)]
  transfers between devices with their start and end apart: 4 -> 4, of which waited for: 2 -> 1; matrix products, arithmetic and copies ran while one was open for 0% -> 0% of each run, Pallas kernels for 3% -> 3%
where the time goes in v2:
time: 195 us
  blocking collectives  84.9 us (44%)
  waiting for transfers between devices  42.4 us (22%)
  starting transfers between devices  37.9 us (19%)
  between operations  14.2 us (7%)
  Pallas kernels  11.5 us (6%)
  local copies, waits for them, and re-layouts  3.7 us (2%)
    all_to_all x1, blocking collectives, per_device(): lax.all_to_all(back, 'node', split_axis=0, concat_axis=0, tiled=True)  51.1 us
    all_to_all x1, waiting for transfers between devices, per_device(): lax.all_to_all(sent, 'node', split_axis=0, concat_axis=0, tiled=True)  42.4 us
    all_to_all x1, starting transfers between devices, per_device(): lax.all_to_all(sent, 'node', split_axis=0, concat_axis=0, tiled=True)  29.3 us
    all_to_all x1, blocking collectives, per_device(): lax.all_to_all(partial, 'local', split_axis=0, concat_axis=0, axis_index_...  18.9 us
    all_to_all x1, blocking collectives, per_device(): lax.all_to_all(spread, 'local', split_axis=0, concat_axis=0, axis_index_g...  14.9 us
    ppermute x1, starting transfers between devices, per_device(): raw_other = lax.ppermute(raw_mine, 'local', swap)  4.87 us
  transfers between devices with their start and end apart: 4, of which 1 were waited for; matrix products, arithmetic and copies ran while one was open for 0% of the time, Pallas kernels for 3%

profile of v2, /device:TPU:1, one launch (start us, length us, event | category | flops | bytes accessed | tf_op | source)
XLA Modules:
  0.0 194.6 jit_solution(15633252306898116756)
XLA Ops:
  7.2 0.0 all-gather.3.cloned.1.call-start
  7.2 2.3 %shard_map.104 = (bf16[32,4,1152]{2,1,0:T(4,128)(2,1)}, bf16[2,160,128]{2,1,0:T(8,128)(2,1)}) custom-call(s32[4,128]{1,0:T(4,128)} %bitcast.33, s32[4,1,128]{2,1,0:T(1,128)} %bitcast.37, bf16[4,128]{1,0:T(4,128)(2,1)} %bitcast.38, bf16[224,128]{1,0:T(8,128)(2,1)} %bitcast.36, bf16[20,1024]{1,0:T(8,128)(2,1)} %bitcast.29, bf16[20,1024]{1,0:T(8,128)(2,1)} %bitcast.31), custom_call_target="tpu_custom_call" | custom-call | tf_op jit(solution)/shard_map/pallas_call | solution.py:345
  9.5 0.0 all-gather.3.cloned.1.call-update
  9.6 29.3 %all-to-all-start = ((bf16[32,4,1152]{2,1,0:T(4,128)(2,1)}), bf16[32,4,1152]{2,1,0:T(4,128)(2,1)S(1)}, u32[]{:S(2)}, u32[]{:S(2)}) async-start(bf16[32,4,1152]{2,1,0:T(4,128)(2,1)} %get-tuple-element.12), calls=%async_computation | async-start | bytes 589824 | tf_op jit(solution)/shard_map/all_to_all | solution.py:379
  38.9 0.0 copy-start.2
  38.9 1.2 copy-done.2
  40.1 0.9 copy-done.3
  40.9 0.1 shard_map.105.down_ref
  41.0 42.4 %all-to-all-done = bf16[32,4,1152]{2,1,0:T(4,128)(2,1)S(1)} async-done(((bf16[32,4,1152]{2,1,0:T(4,128)(2,1)}), bf16[32,4,1152]{2,1,0:T(4,128)(2,1)S(1)}, u32[]{:S(2)}, u32[]{:S(2)}) %all-to-all-start) | async-done | bytes 294944 | tf_op jit(solution)/shard_map/all_to_all | solution.py:379
  83.4 1.2 shard_map.107
  84.6 3.7 %collective-permute-start = (bf16[16,160,128]{2,1,0:T(8,128)(2,1)S(1)}, bf16[16,160,128]{2,1,0:T(8,128)(2,1)S(1)}, u32[]{:S(2)}, u32[]{:S(2)}) collective-permute-start(bf16[16,160,128]{2,1,0:T(8,128)(2,1)S(1)} %get-tuple-element.15), channel_id=1, source_target_pairs={{0,1},{1,0},{2,3},{3,2},{4,5},{5,4},{6,7},{7,6},{8,9},{9,8},{10,11... | collective-permute-start | bytes 1966088 | tf_op jit(solution)/shard_map/ppermute | solution.py:394
  88.3 1.2 shard_map.106
  89.5 0.0 copy-start.4
  89.5 0.7 copy-done.4
  90.2 0.0 collective-permute-done.other_ref
  90.2 0.1 shard_map.108
  90.4 0.0 copy-start.6
  90.4 0.0 copy-start.7
  90.4 18.9 %all_to_all.20.parts_ref = bf16[16,160,128]{2,1,0:T(8,128)(2,1)S(1)} all-to-all(bf16[16,160,128]{2,1,0:T(8,128)(2,1)S(1)} %shard_map.108), channel_id=1, replica_groups={{0,2,4,6,8,10,12,14,16,18,20,22,24,26,28,30},{1,3,5,7,9,11,13,15,17,19,..., dimensions={0} | all-to-all | bytes 1310720 | tf_op jit(solution)/shard_map/all_to_all | solution.py:399
  109.3 0.0 copy-done.7
  109.3 0.2 shard_map.109
  109.5 14.9 %all_to_all.21.raw_ref = bf16[16,176,128]{2,1,0:T(8,128)(2,1)S(1)} all-to-all(bf16[16,176,128]{2,1,0:T(8,128)(2,1)S(1)} %shard_map.109), channel_id=1, replica_groups={{0,2,4,6,8,10,12,14,16,18,20,22,24,26,28,30},{1,3,5,7,9,11,13,15,17,19,..., dimensions={0} | all-to-all | bytes 1441792 | tf_op jit(solution)/shard_map/all_to_all | solution.py:405
  124.4 4.9 %collective-permute-start.1 = (bf16[16,176,128]{2,1,0:T(8,128)(2,1)S(1)}, bf16[16,176,128]{2,1,0:T(8,128)(2,1)S(1)}, u32[]{:S(2)}, u32[]{:S(2)}) collective-permute-start(bf16[16,176,128]{2,1,0:T(8,128)(2,1)S(1)} %all_to_all.21.raw_ref), channel_id=1, source_target_pairs={{0,1},{1,0},{2,3},{3,2},{4,5},{5,4},{6,7},{7,6},{8,9},{9,8},{10,11... | collective-permute-start | bytes 2162696 | tf_op jit(solution)/shard_map/ppermute | solution.py:408
  129.3 0.0 all-gather.3.cloned.1.call-done
  129.3 0.9 copy-done.5
  130.3 3.0 %shard_map.110 = (bf16[16,4,1152]{2,1,0:T(4,128)(2,1)S(1)}, bf16[16,2,160,128]{3,2,1,0:T(8,128)(2,1)S(1)}) custom-call(s32[1]{0:T(128)} %bitcast.which_ref, bf16[16,176,128]{2,1,0:T(8,128)(2,1)S(1)} %all_to_all.21.raw_ref, f32[384,2]{1,0:T(8,128)S(1)} %copy-done.5, bf16[2,224,1024]{2,1,0:T(8,128)(2,1)S(1)} %bitcast.21, bf16[2,224,1024]{2,1,0:T(8,128)(2,1)S(1)} %bitcast.23, ...), custom_call_target="tpu_custom_call" | custom-call | tf_op jit(solution)/shard_map/pallas_call | solution.py:412
  133.2 0.0 collective-permute-done.1.raw_ref
  133.2 0.0 copy-start.8
  133.2 2.1 %shard_map.111 = bf16[16,2,4,1152]{3,2,1,0:T(4,128)(2,1)S(1)} custom-call(s32[1]{0:T(128)S(6)} %sub.3.which_ref, bf16[16,176,128]{2,1,0:T(8,128)(2,1)S(1)} %collective-permute-done.1.raw_ref, f32[384,2]{1,0:T(8,128)S(1)} %get-tuple-element.16.meta_hbm, bf16[2,224,1024]{2,1,0:T(8,128)(2,1)S(1)} %bitcast.22, bf16[2,224,1024]{2,1,0:T(8,128)(2,1)S(1)} %bitcast.24, ...), custom_call_target="tpu_custom_call" | custom-call | tf_op jit(solution)/shard_map/pallas_call | solution.py:427
  135.4 51.1 %all_to_all.22.in_ref = bf16[32,4,1152]{2,1,0:T(4,128)(2,1)S(1)} all-to-all(bf16[32,4,1152]{2,1,0:T(4,128)(2,1)S(1)} %bitcast.27), channel_id=1, replica_groups=mesh['node'=32,'local'=32] {'node'}, dimensions={0} | all-to-all | bytes 589824 | tf_op jit(solution)/shard_map/all_to_all | solution.py:435
  186.5 0.0 copy-done.8
  186.5 1.2 shard_map.112
  (7 shorter events, 0.0 us)
Async XLA Ops:
  7.2 122.1 %all-gather.3.cloned.1.call-start = ((), (), s32[]{:S(2)}) async-start(), calls=%async_computation.4 | async-start | bytes 2703360 | tf_op jit(solution)/shard_map/all_gather | solution.py:377
  9.6 73.8 %all-to-all-start = ((bf16[32,4,1152]{2,1,0:T(4,128)(2,1)}), bf16[32,4,1152]{2,1,0:T(4,128)(2,1)S(1)}, u32[]{:S(2)}, u32[]{:S(2)}) async-start(bf16[32,4,1152]{2,1,0:T(4,128)(2,1)} %get-tuple-element.12), calls=%async_computation | async-start | bytes 589824 | tf_op jit(solution)/shard_map/all_to_all | solution.py:379
  38.9 1.2 copy-start.2
  40.1 0.9 copy-start.3
  84.6 5.6 %collective-permute-start = (bf16[16,160,128]{2,1,0:T(8,128)(2,1)S(1)}, bf16[16,160,128]{2,1,0:T(8,128)(2,1)S(1)}, u32[]{:S(2)}, u32[]{:S(2)}) collective-permute-start(bf16[16,160,128]{2,1,0:T(8,128)(2,1)S(1)} %get-tuple-element.15), channel_id=1, source_target_pairs={{0,1},{1,0},{2,3},{3,2},{4,5},{5,4},{6,7},{7,6},{8,9},{9,8},{10,11... | collective-permute-start | bytes 1966088 | tf_op jit(solution)/shard_map/ppermute | solution.py:394
  89.5 0.7 copy-start.4
  90.4 18.9 %copy-start.6 = (bf16[1,20,1,1024]{3,1,2,0:T(8,128)(2,1)S(1)}, bf16[1,20,1,1024]{3,1,2,0:T(8,128)(2,1)}, u32[]{:S(2)}) copy-start(bf16[1,20,1,1024]{3,1,2,0:T(8,128)(2,1)} %param.16) | copy-start | bytes 122884
  90.4 18.9 %copy-start.7 = (bf16[1,20,1,1024]{3,1,2,0:T(8,128)(2,1)S(1)}, bf16[1,20,1,1024]{3,1,2,0:T(8,128)(2,1)}, u32[]{:S(2)}) copy-start(bf16[1,20,1,1024]{3,1,2,0:T(8,128)(2,1)} %param.17) | copy-start | bytes 122884
  109.3 20.0 %copy-start = (bf16[1,2,224,1024]{3,2,1,0:T(8,128)(2,1)S(1)}, bf16[1,2,224,1024]{3,2,1,0:T(8,128)(2,1)}, u32[]{:S(2)}) copy-start(bf16[1,2,224,1024]{3,2,1,0:T(8,128)(2,1)} %param.13) | copy-start | bytes 2752516
  109.3 20.0 %copy-start.1 = (bf16[1,2,224,1024]{3,2,1,0:T(8,128)(2,1)S(1)}, bf16[1,2,224,1024]{3,2,1,0:T(8,128)(2,1)}, u32[]{:S(2)}) copy-start(bf16[1,2,224,1024]{3,2,1,0:T(8,128)(2,1)} %param.14) | copy-start | bytes 2752516
  124.4 8.8 %collective-permute-start.1 = (bf16[16,176,128]{2,1,0:T(8,128)(2,1)S(1)}, bf16[16,176,128]{2,1,0:T(8,128)(2,1)S(1)}, u32[]{:S(2)}, u32[]{:S(2)}) collective-permute-start(bf16[16,176,128]{2,1,0:T(8,128)(2,1)S(1)} %all_to_all.21.raw_ref), channel_id=1, source_target_pairs={{0,1},{1,0},{2,3},{3,2},{4,5},{5,4},{6,7},{7,6},{8,9},{9,8},{10,11... | collective-permute-start | bytes 2162696 | tf_op jit(solution)/shard_map/ppermute | solution.py:408
  129.3 0.9 copy-start.5
  133.2 53.3 %copy-start.8 = (s32[128,4]{0,1:T(4,128)S(1)}, s32[128,4]{0,1:T(4,128)}, u32[]{:S(2)}) copy-start(s32[128,4]{0,1:T(4,128)} %param.10) | copy-start | bytes 6148
Sparse Core Ops, SparseCore 0:
  12.3 89.0 all-gather.2

commit v3 on v2

v3 whole, which is shorter than its diff:
```python
import functools

import jax
import jax.numpy as jnp
from jax import lax
from jax.experimental import pallas as pl
from jax.experimental.pallas import tpu as pltpu
from jax.sharding import PartitionSpec as P

BF16 = jnp.bfloat16
F32 = jnp.float32
LANES = 128
FOLD = 4
VMEM_LIMIT = 32 * 1024 * 1024
VMEM_MOST = 58 * 1024 * 1024


def round_up(value, unit):
    return -(-value // unit) * unit


def nn(a, b):
    return lax.dot_general(a, b, (((1,), (0,)), ((), ())), preferred_element_type=F32)


def nt(a, b):
    return lax.dot_general(a, b, (((1,), (1,)), ((), ())), preferred_element_type=F32)


def tn(a, b):
    return lax.dot_general(a, b, (((0,), (0,)), ((), ())), preferred_element_type=F32)


def iota(shape, axis):
    return lax.broadcasted_iota(jnp.int32, shape, axis)


def call(kernel, out_shape, limit=VMEM_LIMIT, **extra):
    return pl.pallas_call(
        kernel,
        out_shape=out_shape,
        compiler_params=pltpu.CompilerParams(vmem_limit_bytes=limit),
        **extra,
    )


def pair_maps(pick, nodes):
    groups, tokens = pick.shape
    rows = nodes * FOLD
    node_of = iota((rows, tokens), 0) // FOLD
    hits = [(pick[g : g + 1, :] == node_of).astype(F32) for g in range(groups)]
    named = functools.reduce(jnp.add, hits)
    earlier = (iota((tokens, tokens), 0) < iota((tokens, tokens), 1)).astype(BF16)
    slot = nn(named.astype(BF16), earlier).astype(jnp.int32)
    return named, slot, hits


def placing(named, slot, piece):
    row = iota(named.shape, 0) % FOLD
    return jnp.where(slot == piece * FOLD + row, named, 0.0)


def fetch(copies):
    for copy in copies:
        copy.start()


def pack(rows, slots):
    tiles = rows.shape[-1] // LANES
    axis = rows.ndim - 2
    pieces = [
        rows[..., :slots, tile * LANES : (tile + 1) * LANES] for tile in range(tiles)
    ]
    return [jnp.concatenate(pieces[at : at + 4], axis=axis) for at in range(0, tiles, 4)]


def prepare_kernel(
    pieces,
    pick_hbm,
    expert_hbm,
    weight_hbm,
    rows_hbm,
    out_ref,
    pick_ref,
    expert_ref,
    weight_ref,
    rows_ref,
    sems,
):
    pairs = [
        (pick_hbm, pick_ref),
        (expert_hbm, expert_ref),
        (weight_hbm, weight_ref),
        (rows_hbm, rows_ref),
    ]
    copies = [
        pltpu.make_async_copy(source, target, sems.at[at])
        for at, (source, target) in enumerate(pairs)
    ]
    fetch(copies)
    nodes = out_ref.shape[0]
    width, tokens = rows_ref.shape
    rows = nodes * FOLD
    for copy in copies:
        copy.wait()
    pick = pick_ref[...]
    named, slot, hits = pair_maps(pick, nodes)
    expert = functools.reduce(
        jnp.add, [hit * expert_ref[g].astype(F32) for g, hit in enumerate(hits)]
    )
    weights = weight_ref[...].astype(F32)
    weight = functools.reduce(
        jnp.add, [hit * weights[g : g + 1, :] for g, hit in enumerate(hits)]
    )
    token_rows = rows_ref[...]
    spare = out_ref.shape[2] - pieces * width
    lane = iota((rows, spare), 1)
    meta = jnp.zeros((rows, spare), F32)
    parts = []
    for piece in range(pieces):
        place = placing(named, slot, piece)
        parts.append(nt(place.astype(BF16), token_rows))
        picked = jnp.sum(place * expert, axis=1, keepdims=True)
        scale = jnp.sum(place * weight, axis=1, keepdims=True)
        meta = jnp.where(lane == piece, picked, meta)
        meta = jnp.where(lane == pieces + piece, scale, meta)
    block = jnp.concatenate(parts + [meta], axis=1)
    out_ref[...] = block.reshape(nodes, FOLD, block.shape[1]).astype(BF16)

def keep_kernel(in_ref, after_ref, out_ref):
    out_ref[...] = in_ref[...]


def unfold_matrix(blocks, pieces, held):
    shape = (blocks * held, pieces * blocks * FOLD)
    row, column = iota(shape, 0), iota(shape, 1)
    slot = row % held
    source = (slot // FOLD) * (blocks * FOLD) + (row // held) * FOLD + slot % FOLD
    return jnp.where(jnp.logical_and(source == column, slot < pieces * FOLD), 1.0, 0.0).astype(BF16)


def raw_kernel(pieces, width, held, which_ref, in_ref, down_ref, out_ref):
    blocks = out_ref.shape[0]
    units = down_ref.shape[2]
    slots = pieces * FOLD
    folded = in_ref[:, which_ref[0]].astype(F32).reshape(blocks * FOLD, in_ref.shape[3])
    base = pieces * width
    spare = jnp.zeros((blocks * FOLD, 2 * LANES - width - 1), F32)
    stacked = []
    for piece in range(pieces):
        columns = [
            folded[:, piece * width : (piece + 1) * width],
            folded[:, base + piece : base + piece + 1],
            spare,
        ]
        stacked.append(jnp.concatenate(columns, axis=1))
    stacked = jnp.concatenate(stacked, axis=0).astype(BF16)
    rows = nn(unfold_matrix(blocks, pieces, held), stacked)
    arrived = rows[:, :width]
    first = rows[:, width : width + 1] == 0.0
    zero = jnp.zeros_like(arrived)
    raw = nn(jnp.where(first, arrived, zero).astype(BF16), down_ref[0])
    raw = raw + nn(jnp.where(first, zero, arrived).astype(BF16), down_ref[1])
    parts = pack(raw.reshape(blocks, held, units), slots)
    rows = parts[0].shape[1]
    for at, part in enumerate(parts):
        out_ref[:, at * rows : (at + 1) * rows, :] = part.astype(out_ref.dtype)


def add_kernel(mine_ref, other_ref, out_ref):
    out_ref[...] = (mine_ref[...] + other_ref[...].astype(F32)).astype(BF16)


def lanes_of(column):
    shape = (column.shape[0], LANES)
    return jnp.sum(jnp.where(iota(shape, 0) == iota(shape, 1), column, 0.0), axis=0, keepdims=True)


def hidden_kernel(pieces, width, at_ref, parts_ref, in_ref, gate_ref, up_ref, out_ref):
    blocks, packed, _ = parts_ref.shape
    total = parts_ref[0].astype(F32)
    for at in range(1, blocks):
        total = total + parts_ref[at].astype(F32)
    slots, units = gate_ref.shape
    raw = jnp.concatenate(
        [total[tile * slots : (tile + 1) * slots] for tile in range(units // LANES)], axis=1
    )
    own = in_ref[at_ref[0] >> 1, at_ref[0] & 1].astype(F32)
    base = pieces * width
    picked = jnp.concatenate(
        [own[:, base + at : base + at + 1] for at in range(pieces)], axis=0
    )
    base = base + pieces
    weight = jnp.concatenate(
        [own[:, base + at : base + at + 1] for at in range(pieces)], axis=0
    )
    gate = gate_ref[...].astype(F32)
    up = up_ref[...].astype(F32)
    sig = jax.nn.sigmoid(gate)
    active = gate * sig
    router = jnp.sum(active * up * raw, axis=1, keepdims=True)
    scaled = weight * raw
    by_gate = scaled * up * sig * (1.0 + gate * (1.0 - sig))
    by_up = scaled * active
    spare = out_ref.shape[1] - 2 * packed
    row = iota((spare, LANES), 0)
    extra = jnp.where(row == 0, lanes_of(router), jnp.where(row == 1, lanes_of(picked), 0.0))
    block = jnp.concatenate(pack(by_gate, slots) + pack(by_up, slots) + [extra], axis=0)
    block = block.astype(BF16)
    for at in range(blocks):
        out_ref[at] = block


def back_kernel(pieces, width, held, merges, which_ref, in_ref, gate_ref, up_ref, *refs):
    out_ref = refs[-1]
    blocks = in_ref.shape[0]
    units = gate_ref.shape[2]
    tiles = units // LANES
    slots = pieces * FOLD
    packed = tiles * slots
    unfold = unfold_matrix(blocks, pieces, held)
    block = in_ref[...].astype(F32)

    def spread(start):
        parts = [
            block[:, start + tile * slots : start + tile * slots + held].reshape(
                blocks * held, LANES
            )
            for tile in range(tiles)
        ]
        return jnp.concatenate(parts, axis=1).astype(BF16)

    by_gate = spread(0)
    by_up = spread(packed)
    shape = (blocks, held, LANES)
    picked = jnp.where(
        iota(shape, 1) == iota(shape, 2), block[:, 2 * packed + 1 : 2 * packed + 2], 0.0
    )
    picked = jnp.sum(picked, axis=2, keepdims=True).reshape(blocks * held, 1)
    back = jnp.where(
        picked == 0.0,
        nt(by_gate, gate_ref[0]) + nt(by_up, up_ref[0]),
        nt(by_gate, gate_ref[1]) + nt(by_up, up_ref[1]),
    )
    folded = tn(unfold, back.astype(BF16))
    rows = blocks * FOLD
    parts = [folded[piece * rows : (piece + 1) * rows] for piece in range(pieces)]
    router = block[:, 2 * packed].astype(BF16)
    repeat = (iota((rows, blocks), 0) // FOLD == iota((rows, blocks), 1)).astype(F32).astype(BF16)
    router = nn(repeat, router)
    kept = jnp.logical_and(
        iota((rows, LANES), 1) % FOLD == iota((rows, LANES), 0) % FOLD,
        iota((rows, LANES), 1) < slots,
    )
    router = jnp.where(kept, router, 0.0).astype(BF16)
    lanes_left = out_ref.shape[-1] - pieces * width
    gather = iota((LANES, lanes_left), 0) // FOLD == iota((LANES, lanes_left), 1)
    parts.append(nn(router, gather.astype(F32).astype(BF16)))
    sent = jnp.concatenate(parts, axis=1)
    sent = sent.reshape(blocks, FOLD, sent.shape[1]).astype(BF16)
    if merges:
        which = which_ref[0]
        out_ref[:, which] = sent
        out_ref[:, 1 - which] = refs[0][...]
    else:
        out_ref[...] = sent


def finish_kernel(pieces, width, in_ref, pick_ref, grad_ref, router_ref):
    nodes = in_ref.shape[0]
    pick = pick_ref[...]
    groups, tokens = pick.shape
    named, slot, hits = pair_maps(pick, nodes)
    rows = in_ref[...].astype(F32).reshape(nodes * FOLD, in_ref.shape[2])
    base = pieces * width
    total = jnp.zeros((width, tokens), F32)
    routed = jnp.zeros((nodes * FOLD, tokens), F32)
    for piece in range(pieces):
        place = placing(named, slot, piece)
        total = total + tn(
            rows[:, piece * width : (piece + 1) * width].astype(BF16), place.astype(BF16)
        )
        routed = routed + place * rows[:, base + piece : base + piece + 1]
    grad_ref[...] = total.astype(BF16)
    router = [jnp.sum(routed * hit, axis=0, keepdims=True) for hit in hits]
    router_ref[...] = jnp.concatenate(router, axis=0).astype(BF16)


def per_device(
    out_grad,
    node_pick,
    expert_pick,
    pick_weight,
    gate_weight,
    up_weight,
    down_weight,
    saved_gate,
    saved_up,
):
    nodes = lax.axis_size("node")
    local_count = lax.axis_size("local")
    tokens, width = out_grad.shape
    groups = node_pick.shape[1]
    experts, units = gate_weight.shape[1], gate_weight.shape[3]
    slots = saved_gate.shape[1]
    chips = local_count // 2
    pieces = slots // FOLD
    tiles = units // LANES
    half = nodes // 2
    held = round_up(slots, 8)
    packed = tiles * slots
    block = round_up(pieces * width + 2 * pieces, LANES)
    place = lax.axis_index("local").astype(jnp.int32)
    own = place.reshape(1)
    mine = own & 1
    other = 1 - mine
    same_core = [[2 * chip + c for chip in range(chips)] for c in range(2)]
    swap = [(at, at ^ 1) for at in range(local_count)]

    pick = node_pick.T
    gate_saved = saved_gate.reshape(slots, units)
    up_saved = saved_up.reshape(slots, units)
    down = jnp.swapaxes(down_weight[0], 1, 2)
    hbm = pl.BlockSpec(memory_space=pltpu.HBM)
    vmem = pl.BlockSpec(memory_space=pltpu.VMEM)
    smem = pl.BlockSpec(memory_space=pltpu.SMEM)

    sent = call(
        functools.partial(prepare_kernel, pieces),
        jax.ShapeDtypeStruct((nodes, FOLD, block), BF16),
        limit=VMEM_MOST,
        in_specs=[hbm] * 4,
        out_specs=vmem,
        scratch_shapes=[
            pltpu.VMEM((groups, tokens), jnp.int32),
            pltpu.VMEM((groups, 1, tokens), jnp.int32),
            pltpu.VMEM((groups, tokens), BF16),
            pltpu.VMEM((width, tokens), BF16),
            pltpu.SemaphoreType.DMA((4,)),
        ],
    )(pick, jnp.transpose(expert_pick, (1, 2, 0)), pick_weight[:, :, 0].T, out_grad.T)
    down = call(
        keep_kernel,
        jax.ShapeDtypeStruct(down.shape, BF16),
        in_specs=[vmem, hbm],
        out_specs=vmem,
    )(down, sent)
    arrived = lax.all_to_all(sent, "node", split_axis=0, concat_axis=0, tiled=True)
    arrived = arrived.reshape(half, 2, FOLD, block)

    def raw_part(which, dtype):
        return call(
            functools.partial(raw_kernel, pieces, width, held),
            jax.ShapeDtypeStruct((half, packed, LANES), dtype),
            in_specs=[smem, vmem, vmem],
            out_specs=vmem,
        )(which, arrived, down)

    theirs = raw_part(other, BF16)
    received = lax.ppermute(theirs, "local", swap)
    partial = raw_part(mine, F32)
    partial = call(add_kernel, jax.ShapeDtypeStruct((half, packed, LANES), BF16))(
        partial, received
    )
    parts = lax.all_to_all(
        partial, "local", split_axis=0, concat_axis=0, axis_index_groups=same_core, tiled=True
    )
    hidden = call(
        functools.partial(hidden_kernel, pieces, width),
        jax.ShapeDtypeStruct((chips, 2 * packed + 16, LANES), BF16),
        in_specs=[smem, vmem, vmem, vmem, vmem],
        out_specs=vmem,
    )(own, parts, arrived, gate_saved, up_saved)
    hidden_mine = lax.all_to_all(
        hidden, "local", split_axis=0, concat_axis=0, axis_index_groups=same_core, tiled=True
    )
    hidden_other = lax.ppermute(hidden_mine, "local", swap)
    back = call(
        functools.partial(back_kernel, pieces, width, held, False),
        jax.ShapeDtypeStruct((half, FOLD, block), BF16),
        in_specs=[smem, vmem, vmem, vmem],
        out_specs=vmem,
    )(mine, hidden_mine, gate_weight[0], up_weight[0])
    back = call(
        functools.partial(back_kernel, pieces, width, held, True),
        jax.ShapeDtypeStruct((half, 2, FOLD, block), BF16),
        in_specs=[smem, vmem, vmem, vmem, vmem],
        out_specs=vmem,
    )(other, hidden_other, gate_weight[0], up_weight[0], back)
    back = back.reshape(nodes, FOLD, block)
    returned = lax.all_to_all(back, "node", split_axis=0, concat_axis=0, tiled=True)
    grad, router = call(
        functools.partial(finish_kernel, pieces, width),
        (
            jax.ShapeDtypeStruct((width, tokens), BF16),
            jax.ShapeDtypeStruct((groups, tokens), BF16),
        ),
    )(returned, pick)
    return grad.T, router.T.reshape(tokens, groups, 1)


def solution(mesh):
    return jax.shard_map(
        per_device,
        mesh=mesh,
        in_specs=(
            P("node", "local"),
            P("node", None),
            P("node", None, None),
            P("node", None, None),
            P("node", None, "local", None),
            P("node", None, "local", None),
            P("node", None, None, "local"),
            P("node", "local", None, None),
            P("node", "local", None, None),
        ),
        out_specs=(P("node", "local"), P("node", None, None)),
        check_vma=False,
    )
```

time: 195 us -> 183 us (0.938)
  between operations: 14.2 us -> 0.79 us
  blocking collectives: 84.9 us -> 87.7 us
  waiting for transfers between devices: 42.4 us -> 45.1 us
  local copies, waits for them, and re-layouts: 3.7 us -> 1.02 us
  Pallas kernels: 11.5 us -> 9.45 us
    all_to_all x1, blocking collectives: 14.9 us -> 21.4 us  [per_device(): lax.all_to_all(hidden, 'local', split_axis=0, concat_axis=0, axis_index_g...]
    all_to_all x1, blocking collectives: 51.1 us -> 47.7 us  [per_device(): lax.all_to_all(back, 'node', split_axis=0, concat_axis=0, tiled=True)]
    unnamed x18 -> x14, local copies, waits for them, and re-layouts: 3.7 us -> 1.02 us
  transfers between devices with their start and end apart: 4 -> 3, of which waited for: 1 -> 3; matrix products, arithmetic and copies ran while one was open for 0% -> 0% of each run, Pallas kernels for 3% -> 2%
where the time goes in v3:
time: 183 us; the launch traced here: 182 us
  blocking collectives  87.7 us (48%)
  waiting for transfers between devices  45.1 us (25%)
  starting transfers between devices  38.3 us (21%)
  Pallas kernels  9.45 us (5%)
    all_to_all x1, blocking collectives, per_device(): lax.all_to_all(back, 'node', split_axis=0, concat_axis=0, tiled=True)  47.7 us
    all_to_all x1, waiting for transfers between devices, per_device(): lax.all_to_all(sent, 'node', split_axis=0, concat_axis=0, tiled=True)  43.4 us
    all_to_all x1, starting transfers between devices, per_device(): lax.all_to_all(sent, 'node', split_axis=0, concat_axis=0, tiled=True)  29.3 us
    all_to_all x1, blocking collectives, per_device(): lax.all_to_all(hidden, 'local', split_axis=0, concat_axis=0, axis_index_g...  21.4 us
    all_to_all x1, blocking collectives, per_device(): lax.all_to_all(partial, 'local', split_axis=0, concat_axis=0, axis_index_...  18.5 us
    ppermute x1, starting transfers between devices, per_device(): hidden_other = lax.ppermute(hidden_mine, 'local', swap)  5.28 us
    ppermute x1, starting transfers between devices, per_device(): received = lax.ppermute(theirs, 'local', swap)  3.68 us
  transfers between devices with their start and end apart: 3, of which 3 were waited for; matrix products, arithmetic and copies ran while one was open for 0% of the time, Pallas kernels for 2%

profile of v3, /device:TPU:1, one launch (start us, length us, event | category | flops | bytes accessed | tf_op | source)
XLA Modules:
  0.0 182.3 jit_solution(12172714155482012506)
XLA Ops:
  0.6 0.0 copy-start.3
  0.6 2.3 %shard_map.104.after_ref = bf16[32,4,1152]{2,1,0:T(4,128)(2,1)} custom-call(s32[4,128]{1,0:T(4,128)} %bitcast.31, s32[4,1,128]{2,1,0:T(1,128)} %bitcast.34, bf16[4,128]{1,0:T(4,128)(2,1)} %bitcast.35, bf16[224,128]{1,0:T(8,128)(2,1)} %bitcast.33), custom_call_target="tpu_custom_call" | custom-call | tf_op jit(solution)/shard_map/pallas_call | solution.py:328
  3.0 29.3 %all-to-all-start = ((bf16[32,4,1152]{2,1,0:T(4,128)(2,1)}), bf16[32,4,1152]{2,1,0:T(4,128)(2,1)S(1)}, u32[]{:S(2)}, u32[]{:S(2)}) async-start(bf16[32,4,1152]{2,1,0:T(4,128)(2,1)} %shard_map.104.after_ref), calls=%async_computation | async-start | bytes 589824 | tf_op jit(solution)/shard_map/all_to_all | solution.py:348
  32.3 0.0 copy-done.3
  32.3 0.0 copy-start.2
  32.3 1.0 copy-done.2
  33.3 0.1 shard_map.105.down_ref
  33.4 43.4 %all-to-all-done = bf16[32,4,1152]{2,1,0:T(4,128)(2,1)S(1)} async-done(((bf16[32,4,1152]{2,1,0:T(4,128)(2,1)}), bf16[32,4,1152]{2,1,0:T(4,128)(2,1)S(1)}, u32[]{:S(2)}, u32[]{:S(2)}) %all-to-all-start) | async-done | bytes 294944 | tf_op jit(solution)/shard_map/all_to_all | solution.py:348
  76.8 1.2 shard_map.107
  78.0 3.7 %collective-permute-start = (bf16[16,160,128]{2,1,0:T(8,128)(2,1)S(1)}, bf16[16,160,128]{2,1,0:T(8,128)(2,1)S(1)}, u32[]{:S(2)}, u32[]{:S(2)}) collective-permute-start(bf16[16,160,128]{2,1,0:T(8,128)(2,1)S(1)} %shard_map.107), channel_id=1, source_target_pairs={{0,1},{1,0},{2,3},{3,2},{4,5},{5,4},{6,7},{7,6},{8,9},{9,8},{10,11... | collective-permute-start | bytes 1966088 | tf_op jit(solution)/shard_map/ppermute | solution.py:360
  81.7 1.2 shard_map.106.mine_ref
  82.9 0.0 copy-start.4
  82.9 0.0 copy-start.5
  82.9 0.5 collective-permute-done.other_ref
  83.4 0.1 shard_map.108
  83.5 18.5 %all_to_all.20.parts_ref = bf16[16,160,128]{2,1,0:T(8,128)(2,1)S(1)} all-to-all(bf16[16,160,128]{2,1,0:T(8,128)(2,1)S(1)} %shard_map.108), channel_id=1, replica_groups={{0,2,4,6,8,10,12,14,16,18,20,22,24,26,28,30},{1,3,5,7,9,11,13,15,17,19,..., dimensions={0} | all-to-all | bytes 1310720 | tf_op jit(solution)/shard_map/all_to_all | solution.py:365
  102.0 0.0 copy-done.4
  102.0 0.0 copy-done.5
  102.0 0.3 shard_map.109
  102.3 0.0 copy-start
  102.4 0.0 copy-start.1
  102.4 21.4 %all_to_all.21.in_ref = bf16[16,336,128]{2,1,0:T(8,128)(2,1)S(1)} all-to-all(bf16[16,336,128]{2,1,0:T(8,128)(2,1)S(1)} %shard_map.109), channel_id=1, replica_groups={{0,2,4,6,8,10,12,14,16,18,20,22,24,26,28,30},{1,3,5,7,9,11,13,15,17,19,..., dimensions={0} | all-to-all | bytes 2752512 | tf_op jit(solution)/shard_map/all_to_all | solution.py:374
  123.8 5.3 %collective-permute-start.1 = (bf16[16,336,128]{2,1,0:T(8,128)(2,1)S(1)}, bf16[16,336,128]{2,1,0:T(8,128)(2,1)S(1)}, u32[]{:S(2)}, u32[]{:S(2)}) collective-permute-start(bf16[16,336,128]{2,1,0:T(8,128)(2,1)S(1)} %all_to_all.21.in_ref), channel_id=1, source_target_pairs={{0,1},{1,0},{2,3},{3,2},{4,5},{5,4},{6,7},{7,6},{8,9},{9,8},{10,11... | collective-permute-start | bytes 4128776 | tf_op jit(solution)/shard_map/ppermute | solution.py:377
  129.1 0.0 copy-done
  129.1 0.0 copy-done.1
  129.1 1.5 shard_map.110.refs_0_
  130.6 0.0 copy-start.6
  130.6 1.2 collective-permute-done.1.in_ref
  131.8 1.5 shard_map.111
  133.3 47.7 %all_to_all.22.in_ref = bf16[32,4,1152]{2,1,0:T(4,128)(2,1)S(1)} all-to-all(bf16[32,4,1152]{2,1,0:T(4,128)(2,1)S(1)} %bitcast.27), channel_id=1, replica_groups=mesh['node'=32,'local'=32] {'node'}, dimensions={0} | all-to-all | bytes 589824 | tf_op jit(solution)/shard_map/all_to_all | solution.py:391
  181.1 0.0 copy-done.6
  181.1 1.2 shard_map.112
Async XLA Ops:
  0.6 31.7 %copy-start.3 = (bf16[1,2,1024,224]{2,3,1,0:T(8,128)(2,1)S(1)}, bf16[1,2,1024,224]{2,3,1,0:T(8,128)(2,1)}, u32[]{:S(2)}) copy-start(bf16[1,2,1024,224]{2,3,1,0:T(8,128)(2,1)} %param.15) | copy-start | bytes 2752516
  3.0 73.8 %all-to-all-start = ((bf16[32,4,1152]{2,1,0:T(4,128)(2,1)}), bf16[32,4,1152]{2,1,0:T(4,128)(2,1)S(1)}, u32[]{:S(2)}, u32[]{:S(2)}) async-start(bf16[32,4,1152]{2,1,0:T(4,128)(2,1)} %shard_map.104.after_ref), calls=%async_computation | async-start | bytes 589824 | tf_op jit(solution)/shard_map/all_to_all | solution.py:348
  32.3 1.0 copy-start.2
  78.0 5.4 %collective-permute-start = (bf16[16,160,128]{2,1,0:T(8,128)(2,1)S(1)}, bf16[16,160,128]{2,1,0:T(8,128)(2,1)S(1)}, u32[]{:S(2)}, u32[]{:S(2)}) collective-permute-start(bf16[16,160,128]{2,1,0:T(8,128)(2,1)S(1)} %shard_map.107), channel_id=1, source_target_pairs={{0,1},{1,0},{2,3},{3,2},{4,5},{5,4},{6,7},{7,6},{8,9},{9,8},{10,11... | collective-permute-start | bytes 1966088 | tf_op jit(solution)/shard_map/ppermute | solution.py:360
  82.9 19.1 %copy-start.4 = (bf16[1,20,1,1024]{3,1,2,0:T(8,128)(2,1)S(1)}, bf16[1,20,1,1024]{3,1,2,0:T(8,128)(2,1)}, u32[]{:S(2)}) copy-start(bf16[1,20,1,1024]{3,1,2,0:T(8,128)(2,1)} %param.16) | copy-start | bytes 122884
  82.9 19.1 %copy-start.5 = (bf16[1,20,1,1024]{3,1,2,0:T(8,128)(2,1)S(1)}, bf16[1,20,1,1024]{3,1,2,0:T(8,128)(2,1)}, u32[]{:S(2)}) copy-start(bf16[1,20,1,1024]{3,1,2,0:T(8,128)(2,1)} %param.17) | copy-start | bytes 122884
  102.3 26.7 %copy-start = (bf16[1,2,224,1024]{3,2,1,0:T(8,128)(2,1)S(1)}, bf16[1,2,224,1024]{3,2,1,0:T(8,128)(2,1)}, u32[]{:S(2)}) copy-start(bf16[1,2,224,1024]{3,2,1,0:T(8,128)(2,1)} %param.13) | copy-start | bytes 2752516
  102.4 26.7 %copy-start.1 = (bf16[1,2,224,1024]{3,2,1,0:T(8,128)(2,1)S(1)}, bf16[1,2,224,1024]{3,2,1,0:T(8,128)(2,1)}, u32[]{:S(2)}) copy-start(bf16[1,2,224,1024]{3,2,1,0:T(8,128)(2,1)} %param.14) | copy-start | bytes 2752516
  123.8 8.0 %collective-permute-start.1 = (bf16[16,336,128]{2,1,0:T(8,128)(2,1)S(1)}, bf16[16,336,128]{2,1,0:T(8,128)(2,1)S(1)}, u32[]{:S(2)}, u32[]{:S(2)}) collective-permute-start(bf16[16,336,128]{2,1,0:T(8,128)(2,1)S(1)} %all_to_all.21.in_ref), channel_id=1, source_target_pairs={{0,1},{1,0},{2,3},{3,2},{4,5},{5,4},{6,7},{7,6},{8,9},{9,8},{10,11... | collective-permute-start | bytes 4128776 | tf_op jit(solution)/shard_map/ppermute | solution.py:377
  130.6 50.5 %copy-start.6 = (s32[128,4]{0,1:T(4,128)S(1)}, s32[128,4]{0,1:T(4,128)}, u32[]{:S(2)}) copy-start(s32[128,4]{0,1:T(4,128)} %param.10) | copy-start | bytes 6148

commit v4 on v3

--- a/solution.py
+++ b/solution.py
@@ -12,6 +12,7 @@
 LANES = 128
 FOLD = 4
 VMEM_LIMIT = 32 * 1024 * 1024
+CURVE = (0, 1, 5, 4, 8, 12, 13, 9, 10, 14, 15, 11, 7, 6, 2, 3)
 VMEM_MOST = 58 * 1024 * 1024
 
 
@@ -44,10 +45,16 @@
     )
 
 
-def pair_maps(pick, nodes):
+def chip_order(chips):
+    return CURVE if chips == len(CURVE) else tuple(range(chips))
+
+
+def pair_maps(pick, nodes, backwards):
     groups, tokens = pick.shape
     rows = nodes * FOLD
     node_of = iota((rows, tokens), 0) // FOLD
+    if backwards:
+        node_of = nodes - 1 - node_of
     hits = [(pick[g : g + 1, :] == node_of).astype(F32) for g in range(groups)]
     named = functools.reduce(jnp.add, hits)
     earlier = (iota((tokens, tokens), 0) < iota((tokens, tokens), 1)).astype(BF16)
@@ -104,7 +111,7 @@
     for copy in copies:
         copy.wait()
     pick = pick_ref[...]
-    named, slot, hits = pair_maps(pick, nodes)
+    named, slot, hits = pair_maps(pick, nodes, True)
     expert = functools.reduce(
         jnp.add, [hit * expert_ref[g].astype(F32) for g, hit in enumerate(hits)]
     )
@@ -139,11 +146,12 @@
     return jnp.where(jnp.logical_and(source == column, slot < pieces * FOLD), 1.0, 0.0).astype(BF16)
 
 
-def raw_kernel(pieces, width, held, which_ref, in_ref, down_ref, out_ref):
+def raw_kernel(pieces, width, held, which_ref, in_ref, down_ref, *refs):
+    out_ref = refs[-1]
     blocks = out_ref.shape[0]
     units = down_ref.shape[2]
     slots = pieces * FOLD
-    folded = in_ref[:, which_ref[0]].astype(F32).reshape(blocks * FOLD, in_ref.shape[3])
+    folded = in_ref[:, 1 - which_ref[0]].astype(F32).reshape(blocks * FOLD, in_ref.shape[3])
     base = pieces * width
     spare = jnp.zeros((blocks * FOLD, 2 * LANES - width - 1), F32)
     stacked = []
@@ -164,11 +172,12 @@
     parts = pack(raw.reshape(blocks, held, units), slots)
     rows = parts[0].shape[1]
     for at, part in enumerate(parts):
-        out_ref[:, at * rows : (at + 1) * rows, :] = part.astype(out_ref.dtype)
-
-
-def add_kernel(mine_ref, other_ref, out_ref):
-    out_ref[...] = (mine_ref[...] + other_ref[...].astype(F32)).astype(BF16)
+        span = slice(at * rows, (at + 1) * rows)
+        for to, chip in enumerate(chip_order(blocks)):
+            block = part[blocks - 1 - chip]
+            if len(refs) > 1:
+                block = block + refs[0][to, span]
+            out_ref[to, span] = block.astype(out_ref.dtype)
 
 
 def lanes_of(column):
@@ -185,7 +194,8 @@
     raw = jnp.concatenate(
         [total[tile * slots : (tile + 1) * slots] for tile in range(units // LANES)], axis=1
     )
-    own = in_ref[at_ref[0] >> 1, at_ref[0] & 1].astype(F32)
+    at = 2 * in_ref.shape[0] - 1 - at_ref[0]
+    own = in_ref[at >> 1, at & 1].astype(F32)
     base = pieces * width
     picked = jnp.concatenate(
         [own[:, base + at : base + at + 1] for at in range(pieces)], axis=0
@@ -260,17 +270,19 @@
     sent = sent.reshape(blocks, FOLD, sent.shape[1]).astype(BF16)
     if merges:
         which = which_ref[0]
-        out_ref[:, which] = sent
         out_ref[:, 1 - which] = refs[0][...]
-    else:
-        out_ref[...] = sent
+    for at, chip in enumerate(chip_order(blocks)):
+        if merges:
+            out_ref[chip, which] = sent[at]
+        else:
+            out_ref[chip] = sent[at]
 
 
 def finish_kernel(pieces, width, in_ref, pick_ref, grad_ref, router_ref):
     nodes = in_ref.shape[0]
     pick = pick_ref[...]
     groups, tokens = pick.shape
-    named, slot, hits = pair_maps(pick, nodes)
+    named, slot, hits = pair_maps(pick, nodes, False)
     rows = in_ref[...].astype(F32).reshape(nodes * FOLD, in_ref.shape[2])
     base = pieces * width
     total = jnp.zeros((width, tokens), F32)
@@ -314,7 +326,8 @@
     own = place.reshape(1)
     mine = own & 1
     other = 1 - mine
-    same_core = [[2 * chip + c for chip in range(chips)] for c in range(2)]
+    same_core = [[2 * chip + c for chip in chip_order(chips)] for c in range(2)]
+    backwards = [list(range(nodes))[::-1]]
     swap = [(at, at ^ 1) for at in range(local_count)]
 
     pick = node_pick.T
@@ -345,23 +358,23 @@
         in_specs=[vmem, hbm],
         out_specs=vmem,
     )(down, sent)
-    arrived = lax.all_to_all(sent, "node", split_axis=0, concat_axis=0, tiled=True)
+    other_down = lax.ppermute(down, "local", swap)
+    arrived = lax.all_to_all(
+        sent, "node", split_axis=0, concat_axis=0, axis_index_groups=backwards, tiled=True
+    )
     arrived = arrived.reshape(half, 2, FOLD, block)
 
-    def raw_part(which, dtype):
+    def raw_part(rows, weight, dtype, *before):
         return call(
             functools.partial(raw_kernel, pieces, width, held),
             jax.ShapeDtypeStruct((half, packed, LANES), dtype),
-            in_specs=[smem, vmem, vmem],
+            in_specs=[smem, vmem, vmem] + [vmem] * len(before),
             out_specs=vmem,
-        )(which, arrived, down)
-
-    theirs = raw_part(other, BF16)
-    received = lax.ppermute(theirs, "local", swap)
-    partial = raw_part(mine, F32)
-    partial = call(add_kernel, jax.ShapeDtypeStruct((half, packed, LANES), BF16))(
-        partial, received
-    )
+        )(mine, rows, weight, *before)
+
+    received = lax.ppermute(arrived, "local", swap)
+    partial = raw_part(arrived, down, F32)
+    partial = raw_part(received, other_down, BF16, partial)
     parts = lax.all_to_all(
         partial, "local", split_axis=0, concat_axis=0, axis_index_groups=same_core, tiled=True
     )

time: 183 us -> 181 us (0.989)
  waiting for transfers between devices: 45.1 us -> 30.1 us
  blocking collectives: 87.7 us -> 99.3 us
  starting transfers between devices: 38.3 us -> 40.2 us
    all_to_all x1, waiting for transfers between devices: 43.4 us -> 28.9 us  [per_device(): lax.all_to_all(sent, 'node', split_axis=0, concat_axis=0, axis_index_grou...]
    all_to_all x1, blocking collectives: 47.7 us -> 58.1 us  [per_device(): lax.all_to_all(back, 'node', split_axis=0, concat_axis=0, tiled=True)]
    ppermute x1 -> x2, starting transfers between devices: 3.68 us -> 6.51 us  [the longest x1 3.37 us: per_device(): received = lax.ppermute(arrived, 'local', swap)]
  transfers between devices with their start and end apart: 3 -> 4, of which waited for: 3 -> 2; matrix products, arithmetic and copies ran while one was open for 0% -> 0% of each run, Pallas kernels for 2% -> 2%
where the time goes in v4:
time: 181 us
  blocking collectives  99.3 us (55%)
  starting transfers between devices  40.2 us (22%)
  waiting for transfers between devices  30.1 us (17%)
  Pallas kernels  9.35 us (5%)
    all_to_all x1, blocking collectives, per_device(): lax.all_to_all(back, 'node', split_axis=0, concat_axis=0, tiled=True)  58.1 us
    all_to_all x1, starting transfers between devices, per_device(): lax.all_to_all(sent, 'node', split_axis=0, concat_axis=0, axis_index_grou...  29.4 us
    all_to_all x1, waiting for transfers between devices, per_device(): lax.all_to_all(sent, 'node', split_axis=0, concat_axis=0, axis_index_grou...  28.9 us
    all_to_all x1, blocking collectives, per_device(): lax.all_to_all(hidden, 'local', split_axis=0, concat_axis=0, axis_index_g...  21.9 us
    all_to_all x1, blocking collectives, per_device(): lax.all_to_all(partial, 'local', split_axis=0, concat_axis=0, axis_index_...  19.3 us
    ppermute x1, starting transfers between devices, per_device(): hidden_other = lax.ppermute(hidden_mine, 'local', swap)  4.27 us
  transfers between devices with their start and end apart: 4, of which 2 were waited for; matrix products, arithmetic and copies ran while one was open for 0% of the time, Pallas kernels for 2%

profile of v4, /device:TPU:1, one launch (start us, length us, event | category | flops | bytes accessed | tf_op | source)
XLA Modules:
  0.0 180.8 jit_solution(6929465627020294106)
XLA Ops:
  0.6 0.0 copy-start.3
  0.6 2.4 %shard_map.104.after_ref = bf16[32,4,1152]{2,1,0:T(4,128)(2,1)} custom-call(s32[4,128]{1,0:T(4,128)} %bitcast.31, s32[4,1,128]{2,1,0:T(1,128)} %bitcast.34, bf16[4,128]{1,0:T(4,128)(2,1)} %bitcast.35, bf16[224,128]{1,0:T(8,128)(2,1)} %bitcast.33), custom_call_target="tpu_custom_call" | custom-call | tf_op jit(solution)/shard_map/pallas_call | solution.py:341
  3.0 29.4 %all-to-all-start = ((bf16[32,4,1152]{2,1,0:T(4,128)(2,1)}), bf16[32,4,1152]{2,1,0:T(4,128)(2,1)S(1)}, u32[]{:S(2)}, u32[]{:S(2)}) async-start(bf16[32,4,1152]{2,1,0:T(4,128)(2,1)} %shard_map.104.after_ref), calls=%async_computation | async-start | bytes 589824 | tf_op jit(solution)/shard_map/all_to_all | solution.py:362
  32.4 0.0 copy-done.3
  32.4 0.0 copy-start.2
  32.5 1.0 copy-done.2
  33.4 0.1 shard_map.105.down_ref
  33.5 3.1 %collective-permute-start.1 = (bf16[2,224,1024]{2,1,0:T(8,128)(2,1)S(1)}, bf16[2,224,1024]{2,1,0:T(8,128)(2,1)S(1)}, u32[]{:S(2)}, u32[]{:S(2)}) collective-permute-start(bf16[2,224,1024]{2,1,0:T(8,128)(2,1)S(1)} %shard_map.105.down_ref), channel_id=1, source_target_pairs={{0,1},{1,0},{2,3},{3,2},{4,5},{5,4},{6,7},{7,6},{8,9},{9,8},{10,11... | collective-permute-start | bytes 2752520 | tf_op jit(solution)/shard_map/ppermute | solution.py:361
  36.7 28.9 %all-to-all-done = bf16[32,4,1152]{2,1,0:T(4,128)(2,1)S(1)} async-done(((bf16[32,4,1152]{2,1,0:T(4,128)(2,1)}), bf16[32,4,1152]{2,1,0:T(4,128)(2,1)S(1)}, u32[]{:S(2)}, u32[]{:S(2)}) %all-to-all-start) | async-done | bytes 294944 | tf_op jit(solution)/shard_map/all_to_all | solution.py:362
  65.5 3.4 %collective-permute-start = (bf16[16,2,4,1152]{3,2,1,0:T(4,128)(2,1)S(1)}, bf16[16,2,4,1152]{3,2,1,0:T(4,128)(2,1)S(1)}, u32[]{:S(2)}, u32[]{:S(2)}) collective-permute-start(bf16[16,2,4,1152]{3,2,1,0:T(4,128)(2,1)S(1)} %bitcast.24), channel_id=1, source_target_pairs={{0,1},{1,0},{2,3},{3,2},{4,5},{5,4},{6,7},{7,6},{8,9},{9,8},{10,11... | collective-permute-start | bytes 884744 | tf_op jit(solution)/shard_map/ppermute | solution.py:375
  68.9 1.2 shard_map.106.refs_0_
  70.1 0.0 copy-start.4
  70.1 0.0 copy-start.5
  70.1 0.0 collective-permute-done.1.down_ref
  70.2 0.0 collective-permute-done.in_ref
  70.2 1.2 shard_map.107
  71.4 19.3 %all_to_all.20.parts_ref = bf16[16,160,128]{2,1,0:T(8,128)(2,1)S(1)} all-to-all(bf16[16,160,128]{2,1,0:T(8,128)(2,1)S(1)} %shard_map.107), channel_id=1, replica_groups={{0,2,10,8,16,24,26,18,20,28,30,22,14,12,4,6},{1,3,11,9,17,25,27,19,21,2..., dimensions={0} | all-to-all | bytes 1310720 | tf_op jit(solution)/shard_map/all_to_all | solution.py:378
  90.6 0.0 copy-done.4
  90.6 0.0 copy-done.5
  90.6 0.3 shard_map.108
  91.0 0.0 copy-start
  91.0 0.0 copy-start.1
  91.0 21.9 %all_to_all.21.in_ref = bf16[16,336,128]{2,1,0:T(8,128)(2,1)S(1)} all-to-all(bf16[16,336,128]{2,1,0:T(8,128)(2,1)S(1)} %shard_map.108), channel_id=1, replica_groups={{0,2,10,8,16,24,26,18,20,28,30,22,14,12,4,6},{1,3,11,9,17,25,27,19,21,2..., dimensions={0} | all-to-all | bytes 2752512 | tf_op jit(solution)/shard_map/all_to_all | solution.py:387
  112.9 4.3 %collective-permute-start.2 = (bf16[16,336,128]{2,1,0:T(8,128)(2,1)S(1)}, bf16[16,336,128]{2,1,0:T(8,128)(2,1)S(1)}, u32[]{:S(2)}, u32[]{:S(2)}) collective-permute-start(bf16[16,336,128]{2,1,0:T(8,128)(2,1)S(1)} %all_to_all.21.in_ref), channel_id=1, source_target_pairs={{0,1},{1,0},{2,3},{3,2},{4,5},{5,4},{6,7},{7,6},{8,9},{9,8},{10,11... | collective-permute-start | bytes 4128776 | tf_op jit(solution)/shard_map/ppermute | solution.py:390
  117.2 0.0 copy-done
  117.2 1.5 shard_map.109.refs_0_
  118.7 0.0 copy-start.6
  118.7 1.2 collective-permute-done.2.in_ref
  119.9 1.5 shard_map.110
  121.4 58.1 %all_to_all.22.in_ref = bf16[32,4,1152]{2,1,0:T(4,128)(2,1)S(1)} all-to-all(bf16[32,4,1152]{2,1,0:T(4,128)(2,1)S(1)} %bitcast.27), channel_id=1, replica_groups=mesh['node'=32,'local'=32] {'node'}, dimensions={0} | all-to-all | bytes 589824 | tf_op jit(solution)/shard_map/all_to_all | solution.py:404
  179.5 0.0 copy-done.6
  179.5 1.2 shard_map.111
  (1 shorter events, 0.0 us)
Async XLA Ops:
  0.6 31.8 %copy-start.3 = (bf16[1,2,1024,224]{2,3,1,0:T(8,128)(2,1)S(1)}, bf16[1,2,1024,224]{2,3,1,0:T(8,128)(2,1)}, u32[]{:S(2)}) copy-start(bf16[1,2,1024,224]{2,3,1,0:T(8,128)(2,1)} %param.15) | copy-start | bytes 2752516
  3.0 62.5 %all-to-all-start = ((bf16[32,4,1152]{2,1,0:T(4,128)(2,1)}), bf16[32,4,1152]{2,1,0:T(4,128)(2,1)S(1)}, u32[]{:S(2)}, u32[]{:S(2)}) async-start(bf16[32,4,1152]{2,1,0:T(4,128)(2,1)} %shard_map.104.after_ref), calls=%async_computation | async-start | bytes 589824 | tf_op jit(solution)/shard_map/all_to_all | solution.py:362
  32.4 1.0 copy-start.2
  33.5 36.6 %collective-permute-start.1 = (bf16[2,224,1024]{2,1,0:T(8,128)(2,1)S(1)}, bf16[2,224,1024]{2,1,0:T(8,128)(2,1)S(1)}, u32[]{:S(2)}, u32[]{:S(2)}) collective-permute-start(bf16[2,224,1024]{2,1,0:T(8,128)(2,1)S(1)} %shard_map.105.down_ref), channel_id=1, source_target_pairs={{0,1},{1,0},{2,3},{3,2},{4,5},{5,4},{6,7},{7,6},{8,9},{9,8},{10,11... | collective-permute-start | bytes 2752520 | tf_op jit(solution)/shard_map/ppermute | solution.py:361
  65.5 4.6 %collective-permute-start = (bf16[16,2,4,1152]{3,2,1,0:T(4,128)(2,1)S(1)}, bf16[16,2,4,1152]{3,2,1,0:T(4,128)(2,1)S(1)}, u32[]{:S(2)}, u32[]{:S(2)}) collective-permute-start(bf16[16,2,4,1152]{3,2,1,0:T(4,128)(2,1)S(1)} %bitcast.24), channel_id=1, source_target_pairs={{0,1},{1,0},{2,3},{3,2},{4,5},{5,4},{6,7},{7,6},{8,9},{9,8},{10,11... | collective-permute-start | bytes 884744 | tf_op jit(solution)/shard_map/ppermute | solution.py:375
  70.1 20.5 %copy-start.4 = (bf16[1,20,1,1024]{3,1,2,0:T(8,128)(2,1)S(1)}, bf16[1,20,1,1024]{3,1,2,0:T(8,128)(2,1)}, u32[]{:S(2)}) copy-start(bf16[1,20,1,1024]{3,1,2,0:T(8,128)(2,1)} %param.16) | copy-start | bytes 122884
  70.1 20.5 %copy-start.5 = (bf16[1,20,1,1024]{3,1,2,0:T(8,128)(2,1)S(1)}, bf16[1,20,1,1024]{3,1,2,0:T(8,128)(2,1)}, u32[]{:S(2)}) copy-start(bf16[1,20,1,1024]{3,1,2,0:T(8,128)(2,1)} %param.17) | copy-start | bytes 122884
  91.0 26.2 %copy-start = (bf16[1,2,224,1024]{3,2,1,0:T(8,128)(2,1)S(1)}, bf16[1,2,224,1024]{3,2,1,0:T(8,128)(2,1)}, u32[]{:S(2)}) copy-start(bf16[1,2,224,1024]{3,2,1,0:T(8,128)(2,1)} %param.13) | copy-start | bytes 2752516
  91.0 26.2 %copy-start.1 = (bf16[1,2,224,1024]{3,2,1,0:T(8,128)(2,1)S(1)}, bf16[1,2,224,1024]{3,2,1,0:T(8,128)(2,1)}, u32[]{:S(2)}) copy-start(bf16[1,2,224,1024]{3,2,1,0:T(8,128)(2,1)} %param.14) | copy-start | bytes 2752516
  112.9 7.0 %collective-permute-start.2 = (bf16[16,336,128]{2,1,0:T(8,128)(2,1)S(1)}, bf16[16,336,128]{2,1,0:T(8,128)(2,1)S(1)}, u32[]{:S(2)}, u32[]{:S(2)}) collective-permute-start(bf16[16,336,128]{2,1,0:T(8,128)(2,1)S(1)} %all_to_all.21.in_ref), channel_id=1, source_target_pairs={{0,1},{1,0},{2,3},{3,2},{4,5},{5,4},{6,7},{7,6},{8,9},{9,8},{10,11... | collective-permute-start | bytes 4128776 | tf_op jit(solution)/shard_map/ppermute | solution.py:390
  118.7 60.8 %copy-start.6 = (s32[128,4]{0,1:T(4,128)S(1)}, s32[128,4]{0,1:T(4,128)}, u32[]{:S(2)}) copy-start(s32[128,4]{0,1:T(4,128)} %param.10) | copy-start | bytes 6148

commit v5 on v4

--- a/solution.py
+++ b/solution.py
@@ -52,19 +52,19 @@
 def pair_maps(pick, nodes, backwards):
     groups, tokens = pick.shape
     rows = nodes * FOLD
-    node_of = iota((rows, tokens), 0) // FOLD
+    row = iota((rows, tokens), 0)
+    node_of = row // FOLD
     if backwards:
         node_of = nodes - 1 - node_of
-    hits = [(pick[g : g + 1, :] == node_of).astype(F32) for g in range(groups)]
-    named = functools.reduce(jnp.add, hits)
-    earlier = (iota((tokens, tokens), 0) < iota((tokens, tokens), 1)).astype(BF16)
-    slot = nn(named.astype(BF16), earlier).astype(jnp.int32)
-    return named, slot, hits
-
-
-def placing(named, slot, piece):
-    row = iota(named.shape, 0) % FOLD
-    return jnp.where(slot == piece * FOLD + row, named, 0.0)
+    hits = [pick[g : g + 1, :] == node_of for g in range(groups)]
+    named = functools.reduce(jnp.logical_or, hits)
+    earlier = (iota((tokens, tokens), 0) < iota((tokens, tokens), 1)).astype(F32).astype(BF16)
+    slot = nn(named.astype(F32).astype(BF16), earlier).astype(jnp.int32)
+    return jnp.where(named, slot - row % FOLD, -FOLD), hits
+
+
+def placing(slot, piece):
+    return jnp.where(slot == piece * FOLD, 1.0, 0.0)
 
 
 def fetch(copies):
@@ -110,32 +110,33 @@
     rows = nodes * FOLD
     for copy in copies:
         copy.wait()
-    pick = pick_ref[...]
-    named, slot, hits = pair_maps(pick, nodes, True)
-    expert = functools.reduce(
-        jnp.add, [hit * expert_ref[g].astype(F32) for g, hit in enumerate(hits)]
-    )
+    slot, hits = pair_maps(pick_ref[...], nodes, True)
     weights = weight_ref[...].astype(F32)
-    weight = functools.reduce(
-        jnp.add, [hit * weights[g : g + 1, :] for g, hit in enumerate(hits)]
-    )
-    token_rows = rows_ref[...]
+    signed = functools.reduce(
+        jnp.add,
+        [
+            jnp.where(hit, weights[g : g + 1, :] * (1.0 - 2.0 * expert_ref[g].astype(F32)), 0.0)
+            for g, hit in enumerate(hits)
+        ],
+    )
     spare = out_ref.shape[2] - pieces * width
     lane = iota((rows, spare), 1)
     meta = jnp.zeros((rows, spare), F32)
-    parts = []
-    for piece in range(pieces):
-        place = placing(named, slot, piece)
-        parts.append(nt(place.astype(BF16), token_rows))
-        picked = jnp.sum(place * expert, axis=1, keepdims=True)
-        scale = jnp.sum(place * weight, axis=1, keepdims=True)
-        meta = jnp.where(lane == piece, picked, meta)
-        meta = jnp.where(lane == pieces + piece, scale, meta)
+    places = [placing(slot, piece) for piece in range(pieces)]
+    sent = nt(jnp.concatenate(places, axis=0).astype(BF16), rows_ref[...])
+    for piece, place in enumerate(places):
+        scale = jnp.sum(place * signed, axis=1, keepdims=True)
+        meta = jnp.where(lane == piece, jnp.where(scale < 0.0, 1.0, 0.0), meta)
+        meta = jnp.where(lane == pieces + piece, jnp.abs(scale), meta)
+    parts = [sent[piece * rows : (piece + 1) * rows] for piece in range(pieces)]
     block = jnp.concatenate(parts + [meta], axis=1)
     out_ref[...] = block.reshape(nodes, FOLD, block.shape[1]).astype(BF16)
 
-def keep_kernel(in_ref, after_ref, out_ref):
-    out_ref[...] = in_ref[...]
+
+def keep_kernel(after_ref, *refs):
+    half = len(refs) // 2
+    for in_ref, out_ref in zip(refs[:half], refs[half:]):
+        out_ref[...] = in_ref[...]
 
 
 def unfold_matrix(blocks, pieces, held):
@@ -221,8 +222,7 @@
         out_ref[at] = block
 
 
-def back_kernel(pieces, width, held, merges, which_ref, in_ref, gate_ref, up_ref, *refs):
-    out_ref = refs[-1]
+def back_kernel(pieces, width, held, in_ref, gate_ref, up_ref, out_ref):
     blocks = in_ref.shape[0]
     units = gate_ref.shape[2]
     tiles = units // LANES
@@ -268,33 +268,31 @@
     parts.append(nn(router, gather.astype(F32).astype(BF16)))
     sent = jnp.concatenate(parts, axis=1)
     sent = sent.reshape(blocks, FOLD, sent.shape[1]).astype(BF16)
-    if merges:
-        which = which_ref[0]
-        out_ref[:, 1 - which] = refs[0][...]
     for at, chip in enumerate(chip_order(blocks)):
-        if merges:
-            out_ref[chip, which] = sent[at]
-        else:
-            out_ref[chip] = sent[at]
+        out_ref[chip] = sent[at]
+
+
+def merge_kernel(which_ref, mine_ref, other_ref, out_ref):
+    which = which_ref[0]
+    out_ref[:, which] = mine_ref[...]
+    out_ref[:, 1 - which] = other_ref[...]
 
 
 def finish_kernel(pieces, width, in_ref, pick_ref, grad_ref, router_ref):
     nodes = in_ref.shape[0]
-    pick = pick_ref[...]
-    groups, tokens = pick.shape
-    named, slot, hits = pair_maps(pick, nodes, False)
+    slot, hits = pair_maps(pick_ref[...], nodes, False)
     rows = in_ref[...].astype(F32).reshape(nodes * FOLD, in_ref.shape[2])
     base = pieces * width
-    total = jnp.zeros((width, tokens), F32)
-    routed = jnp.zeros((nodes * FOLD, tokens), F32)
-    for piece in range(pieces):
-        place = placing(named, slot, piece)
-        total = total + tn(
-            rows[:, piece * width : (piece + 1) * width].astype(BF16), place.astype(BF16)
-        )
+    routed = jnp.zeros(slot.shape, F32)
+    places = [placing(slot, piece) for piece in range(pieces)]
+    for piece, place in enumerate(places):
         routed = routed + place * rows[:, base + piece : base + piece + 1]
+    stacked = jnp.concatenate(
+        [rows[:, piece * width : (piece + 1) * width] for piece in range(pieces)], axis=0
+    )
+    total = tn(stacked.astype(BF16), jnp.concatenate(places, axis=0).astype(BF16))
     grad_ref[...] = total.astype(BF16)
-    router = [jnp.sum(routed * hit, axis=0, keepdims=True) for hit in hits]
+    router = [jnp.sum(jnp.where(hit, routed, 0.0), axis=0, keepdims=True) for hit in hits]
     router_ref[...] = jnp.concatenate(router, axis=0).astype(BF16)
 
 
@@ -325,7 +323,6 @@
     place = lax.axis_index("local").astype(jnp.int32)
     own = place.reshape(1)
     mine = own & 1
-    other = 1 - mine
     same_core = [[2 * chip + c for chip in chip_order(chips)] for c in range(2)]
     backwards = [list(range(nodes))[::-1]]
     swap = [(at, at ^ 1) for at in range(local_count)]
@@ -352,13 +349,20 @@
             pltpu.SemaphoreType.DMA((4,)),
         ],
     )(pick, jnp.transpose(expert_pick, (1, 2, 0)), pick_weight[:, :, 0].T, out_grad.T)
-    down = call(
-        keep_kernel,
-        jax.ShapeDtypeStruct(down.shape, BF16),
-        in_specs=[vmem, hbm],
-        out_specs=vmem,
-    )(down, sent)
-    other_down = lax.ppermute(down, "local", swap)
+    others = [lax.ppermute(weight[0], "local", swap) for weight in (gate_weight, up_weight)]
+
+    def keep(after, limit, *weights):
+        return call(
+            keep_kernel,
+            tuple(jax.ShapeDtypeStruct(weight.shape, BF16) for weight in weights),
+            limit=limit,
+            in_specs=[hbm] + [vmem] * len(weights),
+            out_specs=(vmem,) * len(weights),
+        )(after, *weights)
+
+    others = keep(sent, VMEM_MOST, *others)
+    (sent_down,) = keep(others[0], VMEM_LIMIT, down)
+    other_down = lax.ppermute(sent_down, "local", swap)
     arrived = lax.all_to_all(
         sent, "node", split_axis=0, concat_axis=0, axis_index_groups=backwards, tiled=True
     )
@@ -387,19 +391,22 @@
     hidden_mine = lax.all_to_all(
         hidden, "local", split_axis=0, concat_axis=0, axis_index_groups=same_core, tiled=True
     )
-    hidden_other = lax.ppermute(hidden_mine, "local", swap)
+
+    def back_part(gate, up):
+        return call(
+            functools.partial(back_kernel, pieces, width, held),
+            jax.ShapeDtypeStruct((half, FOLD, block), BF16),
+            in_specs=[vmem] * 3,
+            out_specs=vmem,
+        )(hidden_mine, gate, up)
+
+    theirs = lax.ppermute(back_part(*others), "local", swap)
     back = call(
-        functools.partial(back_kernel, pieces, width, held, False),
-        jax.ShapeDtypeStruct((half, FOLD, block), BF16),
-        in_specs=[smem, vmem, vmem, vmem],
+        merge_kernel,
+        jax.ShapeDtypeStruct((half, 2, FOLD, block), BF16),
+        in_specs=[smem, vmem, vmem],
         out_specs=vmem,
-    )(mine, hidden_mine, gate_weight[0], up_weight[0])
-    back = call(
-        functools.partial(back_kernel, pieces, width, held, True),
-        jax.ShapeDtypeStruct((half, 2, FOLD, block), BF16),
-        in_specs=[smem, vmem, vmem, vmem, vmem],
-        out_specs=vmem,
-    )(other, hidden_other, gate_weight[0], up_weight[0], back)
+    )(mine, back_part(gate_weight[0], up_weight[0]), theirs)
     back = back.reshape(nodes, FOLD, block)
     returned = lax.all_to_all(back, "node", split_axis=0, concat_axis=0, tiled=True)
     grad, router = call(

time: 181 us -> 181 us (level)
  waiting for transfers between devices: 30.1 us -> 21 us
  starting transfers between devices: 40.2 us -> 44.3 us
  Pallas kernels: 9.35 us -> 11.8 us
    all_to_all x1, waiting for transfers between devices: 28.9 us -> 18.4 us  [per_device(): lax.all_to_all(sent, 'node', split_axis=0, concat_axis=0, axis_index_grou...]
    ppermute x2 -> x4, starting transfers between devices: 7.41 us -> 11.4 us  [the longest x2 5.07 us: per_device(): lax.ppermute(weight[0], 'local', swap)]
    pallas_call x3 -> x5, Pallas kernels: 3.06 us -> 5.85 us  [the longest x2 2.99 us: back_part(): call(functools.partial(back_kernel, pieces, width, held), jax.ShapeDtypeS...]
  transfers between devices with their start and end apart: 4 -> 6, of which waited for: 2 -> 3; matrix products, arithmetic and copies ran while one was open for 0% -> 0% of each run, Pallas kernels for 2% -> 3%
where the time goes in v5:
time: 181 us; the launch traced here: 180 us
  blocking collectives  99.8 us (55%)
  starting transfers between devices  44.3 us (24%)
  waiting for transfers between devices  21 us (12%)
  Pallas kernels  11.8 us (7%)
  local copies, waits for them, and re-layouts  2.14 us (1%)
    all_to_all x1, blocking collectives, per_device(): lax.all_to_all(back, 'node', split_axis=0, concat_axis=0, tiled=True)  58.6 us
    all_to_all x1, starting transfers between devices, per_device(): lax.all_to_all(sent, 'node', split_axis=0, concat_axis=0, axis_index_grou...  29.6 us
    all_to_all x1, blocking collectives, per_device(): lax.all_to_all(hidden, 'local', split_axis=0, concat_axis=0, axis_index_g...  21.9 us
    all_to_all x1, blocking collectives, per_device(): lax.all_to_all(partial, 'local', split_axis=0, concat_axis=0, axis_index_...  19.3 us
    all_to_all x1, waiting for transfers between devices, per_device(): lax.all_to_all(sent, 'node', split_axis=0, concat_axis=0, axis_index_grou...  18.4 us
    ppermute x2, starting transfers between devices, per_device(): lax.ppermute(weight[0], 'local', swap)  5.07 us
    ppermute x1, starting transfers between devices, per_device(): theirs = lax.ppermute(back_part(*others), 'local', swap)  4.28 us
  transfers between devices with their start and end apart: 6, of which 3 were waited for; matrix products, arithmetic and copies ran while one was open for 0% of the time, Pallas kernels for 3%

profile of v5, /device:TPU:1, one launch (start us, length us, event | category | flops | bytes accessed | tf_op | source)
XLA Modules:
  0.0 180.0 jit_solution(12438458971028913122)
XLA Ops:
  0.6 2.2 %shard_map.104.after_ref = bf16[32,4,1152]{2,1,0:T(4,128)(2,1)} custom-call(s32[4,128]{1,0:T(4,128)} %bitcast.32, s32[4,1,128]{2,1,0:T(1,128)} %bitcast.35, bf16[4,128]{1,0:T(4,128)(2,1)} %bitcast.36, bf16[224,128]{1,0:T(8,128)(2,1)} %bitcast.34), custom_call_target="tpu_custom_call" | custom-call | tf_op jit(solution)/shard_map/pallas_call | solution.py:338
  2.8 0.0 copy-start
  2.8 29.6 %all-to-all-start = ((bf16[32,4,1152]{2,1,0:T(4,128)(2,1)}), bf16[32,4,1152]{2,1,0:T(4,128)(2,1)S(1)}, u32[]{:S(2)}, u32[]{:S(2)}) async-start(bf16[32,4,1152]{2,1,0:T(4,128)(2,1)} %shard_map.104.after_ref), calls=%async_computation | async-start | bytes 589824 | tf_op jit(solution)/shard_map/all_to_all | solution.py:366
  32.4 3.1 %collective-permute-start.1 = (bf16[2,224,1024]{2,1,0:T(8,128)(2,1)}, bf16[2,224,1024]{2,1,0:T(8,128)(2,1)S(1)}, u32[]{:S(2)}, u32[]{:S(2)}) collective-permute-start(bf16[2,224,1024]{2,1,0:T(8,128)(2,1)} %bitcast.26), channel_id=1, source_target_pairs={{0,1},{1,0},{2,3},{3,2},{4,5},{5,4},{6,7},{7,6},{8,9},{9,8},{10,11... | collective-permute-start | bytes 2752520 | tf_op jit(solution)/shard_map/ppermute | solution.py:352
  35.5 1.9 %collective-permute-start.2 = (bf16[2,224,1024]{2,1,0:T(8,128)(2,1)}, bf16[2,224,1024]{2,1,0:T(8,128)(2,1)S(1)}, u32[]{:S(2)}, u32[]{:S(2)}) collective-permute-start(bf16[2,224,1024]{2,1,0:T(8,128)(2,1)} %bitcast.28), channel_id=1, source_target_pairs={{0,1},{1,0},{2,3},{3,2},{4,5},{5,4},{6,7},{7,6},{8,9},{9,8},{10,11... | collective-permute-start | bytes 2752520 | tf_op jit(solution)/shard_map/ppermute | solution.py:352
  37.5 0.4 collective-permute-done.1.refs_0_
  37.8 2.3 %collective-permute-done.2.refs_1_ = bf16[2,224,1024]{2,1,0:T(8,128)(2,1)S(1)} collective-permute-done((bf16[2,224,1024]{2,1,0:T(8,128)(2,1)}, bf16[2,224,1024]{2,1,0:T(8,128)(2,1)S(1)}, u32[]{:S(2)}, u32[]{:S(2)}) %collective-permute-start.2) | collective-permute-done | bytes 917536 | tf_op jit(solution)/shard_map/ppermute | solution.py:352
  40.1 0.9 copy-done.10
  41.0 2.8 %shard_map.105 = (bf16[2,224,1024]{2,1,0:T(8,128)(2,1)}, bf16[2,224,1024]{2,1,0:T(8,128)(2,1)}) custom-call(bf16[32,4,1152]{2,1,0:T(4,128)(2,1)} %shard_map.104.after_ref, bf16[2,224,1024]{2,1,0:T(8,128)(2,1)} %copy-done.9, bf16[2,224,1024]{2,1,0:T(8,128)(2,1)} %copy-done.10), custom_call_target="tpu_custom_call" | custom-call | tf_op jit(solution)/shard_map/pallas_call | solution.py:355
  43.8 1.2 copy-done.1
  45.0 0.1 shard_map.106
  45.0 2.0 %collective-permute-start.3 = (bf16[2,224,1024]{2,1,0:T(8,128)(2,1)S(1)}, bf16[2,224,1024]{2,1,0:T(8,128)(2,1)S(1)}, u32[]{:S(2)}, u32[]{:S(2)}) collective-permute-start(bf16[2,224,1024]{2,1,0:T(8,128)(2,1)S(1)} %shard_map.106), channel_id=1, source_target_pairs={{0,1},{1,0},{2,3},{3,2},{4,5},{5,4},{6,7},{7,6},{8,9},{9,8},{10,11... | collective-permute-start | bytes 2752520 | tf_op jit(solution)/shard_map/ppermute | solution.py:365
  47.1 18.4 %all-to-all-done = bf16[32,4,1152]{2,1,0:T(4,128)(2,1)S(1)} async-done(((bf16[32,4,1152]{2,1,0:T(4,128)(2,1)}), bf16[32,4,1152]{2,1,0:T(4,128)(2,1)S(1)}, u32[]{:S(2)}, u32[]{:S(2)}) %all-to-all-start) | async-done | bytes 294944 | tf_op jit(solution)/shard_map/all_to_all | solution.py:366
  65.5 3.4 %collective-permute-start = (bf16[16,2,4,1152]{3,2,1,0:T(4,128)(2,1)S(1)}, bf16[16,2,4,1152]{3,2,1,0:T(4,128)(2,1)S(1)}, u32[]{:S(2)}, u32[]{:S(2)}) collective-permute-start(bf16[16,2,4,1152]{3,2,1,0:T(4,128)(2,1)S(1)} %bitcast.22), channel_id=1, source_target_pairs={{0,1},{1,0},{2,3},{3,2},{4,5},{5,4},{6,7},{7,6},{8,9},{9,8},{10,11... | collective-permute-start | bytes 884744 | tf_op jit(solution)/shard_map/ppermute | solution.py:379
  68.8 1.2 shard_map.107.refs_0_
  70.1 0.0 copy-start.6
  70.1 0.0 copy-start.7
  70.1 0.0 collective-permute-done.3.down_ref
  70.1 0.0 collective-permute-done.in_ref
  70.1 1.2 shard_map.108
  71.3 19.3 %all_to_all.20.parts_ref = bf16[16,160,128]{2,1,0:T(8,128)(2,1)S(1)} all-to-all(bf16[16,160,128]{2,1,0:T(8,128)(2,1)S(1)} %shard_map.108), channel_id=1, replica_groups={{0,2,10,8,16,24,26,18,20,28,30,22,14,12,4,6},{1,3,11,9,17,25,27,19,21,2..., dimensions={0} | all-to-all | bytes 1310720 | tf_op jit(solution)/shard_map/all_to_all | solution.py:382
  90.6 0.0 copy-done.7
  90.6 0.3 shard_map.109
  90.9 21.9 %all_to_all.21.in_ref = bf16[16,336,128]{2,1,0:T(8,128)(2,1)S(1)} all-to-all(bf16[16,336,128]{2,1,0:T(8,128)(2,1)S(1)} %shard_map.109), channel_id=1, replica_groups={{0,2,10,8,16,24,26,18,20,28,30,22,14,12,4,6},{1,3,11,9,17,25,27,19,21,2..., dimensions={0} | all-to-all | bytes 2752512 | tf_op jit(solution)/shard_map/all_to_all | solution.py:391
  112.8 0.0 copy-done.2
  112.9 1.5 shard_map.111
  114.4 0.0 copy-start.8
  114.4 4.3 %collective-permute-start.4 = (bf16[16,4,1152]{2,1,0:T(4,128)(2,1)S(1)}, bf16[16,4,1152]{2,1,0:T(4,128)(2,1)S(1)}, u32[]{:S(2)}, u32[]{:S(2)}) collective-permute-start(bf16[16,4,1152]{2,1,0:T(4,128)(2,1)S(1)} %shard_map.111), channel_id=1, source_target_pairs={{0,1},{1,0},{2,3},{3,2},{4,5},{5,4},{6,7},{7,6},{8,9},{9,8},{10,11... | collective-permute-start | bytes 442376 | tf_op jit(solution)/shard_map/ppermute | solution.py:403
  118.7 1.5 shard_map.110.mine_ref
  120.2 0.0 collective-permute-done.4.other_ref
  120.2 58.6 %all_to_all.22.in_ref = bf16[32,4,1152]{2,1,0:T(4,128)(2,1)S(1)} all-to-all(bf16[32,4,1152]{2,1,0:T(4,128)(2,1)S(1)} %bitcast.25), channel_id=1, replica_groups=mesh['node'=32,'local'=32] {'node'}, dimensions={0} | all-to-all | bytes 589824 | tf_op jit(solution)/shard_map/all_to_all | solution.py:411
  178.9 1.1 shard_map.113
  (15 shorter events, 0.1 us)
Async XLA Ops:
  2.8 41.0 %copy-start = (bf16[1,2,1024,224]{2,3,1,0:T(8,128)(2,1)S(1)}, bf16[1,2,1024,224]{2,3,1,0:T(8,128)(2,1)}, u32[]{:S(2)}) copy-start(bf16[1,2,1024,224]{2,3,1,0:T(8,128)(2,1)} %param.15) | copy-start | bytes 2752516
  2.8 62.7 %all-to-all-start = ((bf16[32,4,1152]{2,1,0:T(4,128)(2,1)}), bf16[32,4,1152]{2,1,0:T(4,128)(2,1)S(1)}, u32[]{:S(2)}, u32[]{:S(2)}) async-start(bf16[32,4,1152]{2,1,0:T(4,128)(2,1)} %shard_map.104.after_ref), calls=%async_computation | async-start | bytes 589824 | tf_op jit(solution)/shard_map/all_to_all | solution.py:366
  32.4 5.4 %collective-permute-start.1 = (bf16[2,224,1024]{2,1,0:T(8,128)(2,1)}, bf16[2,224,1024]{2,1,0:T(8,128)(2,1)S(1)}, u32[]{:S(2)}, u32[]{:S(2)}) collective-permute-start(bf16[2,224,1024]{2,1,0:T(8,128)(2,1)} %bitcast.26), channel_id=1, source_target_pairs={{0,1},{1,0},{2,3},{3,2},{4,5},{5,4},{6,7},{7,6},{8,9},{9,8},{10,11... | collective-permute-start | bytes 2752520 | tf_op jit(solution)/shard_map/ppermute | solution.py:352
  35.5 4.6 %collective-permute-start.2 = (bf16[2,224,1024]{2,1,0:T(8,128)(2,1)}, bf16[2,224,1024]{2,1,0:T(8,128)(2,1)S(1)}, u32[]{:S(2)}, u32[]{:S(2)}) collective-permute-start(bf16[2,224,1024]{2,1,0:T(8,128)(2,1)} %bitcast.28), channel_id=1, source_target_pairs={{0,1},{1,0},{2,3},{3,2},{4,5},{5,4},{6,7},{7,6},{8,9},{9,8},{10,11... | collective-permute-start | bytes 2752520 | tf_op jit(solution)/shard_map/ppermute | solution.py:352
  37.8 2.3 %copy-start.9 = (bf16[2,224,1024]{2,1,0:T(8,128)(2,1)}, bf16[2,224,1024]{2,1,0:T(8,128)(2,1)S(1)}, u32[]{:S(2)}) copy-start(bf16[2,224,1024]{2,1,0:T(8,128)(2,1)S(1)} %collective-permute-done.1.refs_0_) | copy-start | bytes 2752516
  40.1 0.9 copy-start.10
  43.8 1.2 copy-start.1
  45.0 25.0 %collective-permute-start.3 = (bf16[2,224,1024]{2,1,0:T(8,128)(2,1)S(1)}, bf16[2,224,1024]{2,1,0:T(8,128)(2,1)S(1)}, u32[]{:S(2)}, u32[]{:S(2)}) collective-permute-start(bf16[2,224,1024]{2,1,0:T(8,128)(2,1)S(1)} %shard_map.106), channel_id=1, source_target_pairs={{0,1},{1,0},{2,3},{3,2},{4,5},{5,4},{6,7},{7,6},{8,9},{9,8},{10,11... | collective-permute-start | bytes 2752520 | tf_op jit(solution)/shard_map/ppermute | solution.py:365
  65.5 4.6 %collective-permute-start = (bf16[16,2,4,1152]{3,2,1,0:T(4,128)(2,1)S(1)}, bf16[16,2,4,1152]{3,2,1,0:T(4,128)(2,1)S(1)}, u32[]{:S(2)}, u32[]{:S(2)}) collective-permute-start(bf16[16,2,4,1152]{3,2,1,0:T(4,128)(2,1)S(1)} %bitcast.22), channel_id=1, source_target_pairs={{0,1},{1,0},{2,3},{3,2},{4,5},{5,4},{6,7},{7,6},{8,9},{9,8},{10,11... | collective-permute-start | bytes 884744 | tf_op jit(solution)/shard_map/ppermute | solution.py:379
  70.1 20.5 %copy-start.6 = (bf16[1,20,1,1024]{3,1,2,0:T(8,128)(2,1)S(1)}, bf16[1,20,1,1024]{3,1,2,0:T(8,128)(2,1)}, u32[]{:S(2)}) copy-start(bf16[1,20,1,1024]{3,1,2,0:T(8,128)(2,1)} %param.16) | copy-start | bytes 122884
  70.1 20.5 %copy-start.7 = (bf16[1,20,1,1024]{3,1,2,0:T(8,128)(2,1)S(1)}, bf16[1,20,1,1024]{3,1,2,0:T(8,128)(2,1)}, u32[]{:S(2)}) copy-start(bf16[1,20,1,1024]{3,1,2,0:T(8,128)(2,1)} %param.17) | copy-start | bytes 122884
  90.9 21.9 %copy-start.2 = (bf16[2,224,1024]{2,1,0:T(8,128)(2,1)S(1)}, bf16[2,224,1024]{2,1,0:T(8,128)(2,1)}, u32[]{:S(2)}) copy-start(bf16[2,224,1024]{2,1,0:T(8,128)(2,1)} %get-tuple-element.6.after_ref.gate_ref) | copy-start | bytes 2752516
  90.9 21.9 %copy-start.5 = (bf16[2,224,1024]{2,1,0:T(8,128)(2,1)S(1)}, bf16[2,224,1024]{2,1,0:T(8,128)(2,1)}, u32[]{:S(2)}) copy-start(bf16[2,224,1024]{2,1,0:T(8,128)(2,1)} %get-tuple-element.7.up_ref) | copy-start | bytes 2752516
  112.9 5.8 %copy-start.3 = (bf16[1,2,224,1024]{3,2,1,0:T(8,128)(2,1)S(1)}, bf16[1,2,224,1024]{3,2,1,0:T(8,128)(2,1)}, u32[]{:S(2)}) copy-start(bf16[1,2,224,1024]{3,2,1,0:T(8,128)(2,1)} %param.13) | copy-start | bytes 2752516
  112.9 5.8 %copy-start.4 = (bf16[1,2,224,1024]{3,2,1,0:T(8,128)(2,1)S(1)}, bf16[1,2,224,1024]{3,2,1,0:T(8,128)(2,1)}, u32[]{:S(2)}) copy-start(bf16[1,2,224,1024]{3,2,1,0:T(8,128)(2,1)} %param.14) | copy-start | bytes 2752516
  114.4 64.5 %copy-start.8 = (s32[128,4]{0,1:T(4,128)S(1)}, s32[128,4]{0,1:T(4,128)}, u32[]{:S(2)}) copy-start(s32[128,4]{0,1:T(4,128)} %param.10) | copy-start | bytes 6148
  114.4 5.8 %collective-permute-start.4 = (bf16[16,4,1152]{2,1,0:T(4,128)(2,1)S(1)}, bf16[16,4,1152]{2,1,0:T(4,128)(2,1)S(1)}, u32[]{:S(2)}, u32[]{:S(2)}) collective-permute-start(bf16[16,4,1152]{2,1,0:T(4,128)(2,1)S(1)} %shard_map.111), channel_id=1, source_target_pairs={{0,1},{1,0},{2,3},{3,2},{4,5},{5,4},{6,7},{7,6},{8,9},{9,8},{10,11... | collective-permute-start | bytes 442376 | tf_op jit(solution)/shard_map/ppermute | solution.py:403

commit v6 on v5

--- a/solution.py
+++ b/solution.py
@@ -12,7 +12,6 @@
 LANES = 128
 FOLD = 4
 VMEM_LIMIT = 32 * 1024 * 1024
-CURVE = (0, 1, 5, 4, 8, 12, 13, 9, 10, 14, 15, 11, 7, 6, 2, 3)
 VMEM_MOST = 58 * 1024 * 1024
 
 
@@ -45,17 +44,11 @@
     )
 
 
-def chip_order(chips):
-    return CURVE if chips == len(CURVE) else tuple(range(chips))
-
-
-def pair_maps(pick, nodes, backwards):
+def pair_maps(pick, nodes):
     groups, tokens = pick.shape
     rows = nodes * FOLD
     row = iota((rows, tokens), 0)
     node_of = row // FOLD
-    if backwards:
-        node_of = nodes - 1 - node_of
     hits = [pick[g : g + 1, :] == node_of for g in range(groups)]
     named = functools.reduce(jnp.logical_or, hits)
     earlier = (iota((tokens, tokens), 0) < iota((tokens, tokens), 1)).astype(F32).astype(BF16)
@@ -110,7 +103,7 @@
     rows = nodes * FOLD
     for copy in copies:
         copy.wait()
-    slot, hits = pair_maps(pick_ref[...], nodes, True)
+    slot, hits = pair_maps(pick_ref[...], nodes)
     weights = weight_ref[...].astype(F32)
     signed = functools.reduce(
         jnp.add,
@@ -139,12 +132,23 @@
         out_ref[...] = in_ref[...]
 
 
+def folded_row(row, blocks, pieces, held):
+    block = row // held
+    slot = row - block * held
+    folded = (slot // FOLD) * (blocks * FOLD) + block * FOLD + slot % FOLD
+    return jnp.where(slot < pieces * FOLD, folded, -1)
+
+
 def unfold_matrix(blocks, pieces, held):
-    shape = (blocks * held, pieces * blocks * FOLD)
-    row, column = iota(shape, 0), iota(shape, 1)
-    slot = row % held
-    source = (slot // FOLD) * (blocks * FOLD) + (row // held) * FOLD + slot % FOLD
-    return jnp.where(jnp.logical_and(source == column, slot < pieces * FOLD), 1.0, 0.0).astype(BF16)
+    rows, folds = blocks * held, pieces * blocks * FOLD
+    source = folded_row(iota((rows, 1), 0), blocks, pieces, held)
+    return jnp.where(iota((rows, folds), 1) == source, 1.0, 0.0).astype(BF16)
+
+
+def fold_matrix(blocks, pieces, held):
+    rows, folds = blocks * held, pieces * blocks * FOLD
+    target = folded_row(iota((1, rows), 1), blocks, pieces, held)
+    return jnp.where(iota((folds, rows), 0) == target, 1.0, 0.0).astype(BF16)
 
 
 def raw_kernel(pieces, width, held, which_ref, in_ref, down_ref, *refs):
@@ -152,7 +156,7 @@
     blocks = out_ref.shape[0]
     units = down_ref.shape[2]
     slots = pieces * FOLD
-    folded = in_ref[:, 1 - which_ref[0]].astype(F32).reshape(blocks * FOLD, in_ref.shape[3])
+    folded = in_ref[:, which_ref[0]].astype(F32).reshape(blocks * FOLD, in_ref.shape[3])
     base = pieces * width
     spare = jnp.zeros((blocks * FOLD, 2 * LANES - width - 1), F32)
     stacked = []
@@ -174,11 +178,9 @@
     rows = parts[0].shape[1]
     for at, part in enumerate(parts):
         span = slice(at * rows, (at + 1) * rows)
-        for to, chip in enumerate(chip_order(blocks)):
-            block = part[blocks - 1 - chip]
-            if len(refs) > 1:
-                block = block + refs[0][to, span]
-            out_ref[to, span] = block.astype(out_ref.dtype)
+        if len(refs) > 1:
+            part = part + refs[0][:, span, :]
+        out_ref[:, span, :] = part.astype(out_ref.dtype)
 
 
 def lanes_of(column):
@@ -195,8 +197,7 @@
     raw = jnp.concatenate(
         [total[tile * slots : (tile + 1) * slots] for tile in range(units // LANES)], axis=1
     )
-    at = 2 * in_ref.shape[0] - 1 - at_ref[0]
-    own = in_ref[at >> 1, at & 1].astype(F32)
+    own = in_ref[at_ref[0] >> 1, at_ref[0] & 1].astype(F32)
     base = pieces * width
     picked = jnp.concatenate(
         [own[:, base + at : base + at + 1] for at in range(pieces)], axis=0
@@ -228,7 +229,7 @@
     tiles = units // LANES
     slots = pieces * FOLD
     packed = tiles * slots
-    unfold = unfold_matrix(blocks, pieces, held)
+    fold = fold_matrix(blocks, pieces, held)
     block = in_ref[...].astype(F32)
 
     def spread(start):
@@ -252,7 +253,7 @@
         nt(by_gate, gate_ref[0]) + nt(by_up, up_ref[0]),
         nt(by_gate, gate_ref[1]) + nt(by_up, up_ref[1]),
     )
-    folded = tn(unfold, back.astype(BF16))
+    folded = nn(fold, back.astype(BF16))
     rows = blocks * FOLD
     parts = [folded[piece * rows : (piece + 1) * rows] for piece in range(pieces)]
     router = block[:, 2 * packed].astype(BF16)
@@ -268,8 +269,7 @@
     parts.append(nn(router, gather.astype(F32).astype(BF16)))
     sent = jnp.concatenate(parts, axis=1)
     sent = sent.reshape(blocks, FOLD, sent.shape[1]).astype(BF16)
-    for at, chip in enumerate(chip_order(blocks)):
-        out_ref[chip] = sent[at]
+    out_ref[...] = sent
 
 
 def merge_kernel(which_ref, mine_ref, other_ref, out_ref):
@@ -280,7 +280,7 @@
 
 def finish_kernel(pieces, width, in_ref, pick_ref, grad_ref, router_ref):
     nodes = in_ref.shape[0]
-    slot, hits = pair_maps(pick_ref[...], nodes, False)
+    slot, hits = pair_maps(pick_ref[...], nodes)
     rows = in_ref[...].astype(F32).reshape(nodes * FOLD, in_ref.shape[2])
     base = pieces * width
     routed = jnp.zeros(slot.shape, F32)
@@ -323,8 +323,7 @@
     place = lax.axis_index("local").astype(jnp.int32)
     own = place.reshape(1)
     mine = own & 1
-    same_core = [[2 * chip + c for chip in chip_order(chips)] for c in range(2)]
-    backwards = [list(range(nodes))[::-1]]
+    same_core = [[2 * chip + c for chip in range(chips)] for c in range(2)]
     swap = [(at, at ^ 1) for at in range(local_count)]
 
     pick = node_pick.T
@@ -363,9 +362,7 @@
     others = keep(sent, VMEM_MOST, *others)
     (sent_down,) = keep(others[0], VMEM_LIMIT, down)
     other_down = lax.ppermute(sent_down, "local", swap)
-    arrived = lax.all_to_all(
-        sent, "node", split_axis=0, concat_axis=0, axis_index_groups=backwards, tiled=True
-    )
+    arrived = lax.all_to_all(sent, "node", split_axis=0, concat_axis=0, tiled=True)
     arrived = arrived.reshape(half, 2, FOLD, block)
 
     def raw_part(rows, weight, dtype, *before):

time: 181 us -> 182 us (level)
  waiting for transfers between devices: 21 us -> 32.7 us
  blocking collectives: 99.8 us -> 88.8 us
    all_to_all x1, waiting for transfers between devices: 18.4 us -> 30.1 us  [per_device(): lax.all_to_all(sent, 'node', split_axis=0, concat_axis=0, tiled=True)]
    all_to_all x1, blocking collectives: 58.6 us -> 48.7 us  [per_device(): lax.all_to_all(back, 'node', split_axis=0, concat_axis=0, tiled=True)]
where the time goes in v6:
time: 182 us; the launch traced here: 181 us
  blocking collectives  88.8 us (49%)
  starting transfers between devices  45.1 us (25%)
  waiting for transfers between devices  32.7 us (18%)
  Pallas kernels  11.6 us (6%)
  local copies, waits for them, and re-layouts  2.14 us (1%)
    all_to_all x1, blocking collectives, per_device(): lax.all_to_all(back, 'node', split_axis=0, concat_axis=0, tiled=True)  48.7 us
    all_to_all x1, waiting for transfers between devices, per_device(): lax.all_to_all(sent, 'node', split_axis=0, concat_axis=0, tiled=True)  30.1 us
    all_to_all x1, starting transfers between devices, per_device(): lax.all_to_all(sent, 'node', split_axis=0, concat_axis=0, tiled=True)  29.4 us
    all_to_all x1, blocking collectives, per_device(): lax.all_to_all(hidden, 'local', split_axis=0, concat_axis=0, axis_index_g...  21.5 us
    all_to_all x1, blocking collectives, per_device(): lax.all_to_all(partial, 'local', split_axis=0, concat_axis=0, axis_index_...  18.6 us
    ppermute x1, starting transfers between devices, per_device(): theirs = lax.ppermute(back_part(*others), 'local', swap)  5.23 us
    ppermute x2, starting transfers between devices, per_device(): lax.ppermute(weight[0], 'local', swap)  4.79 us
    ppermute x1, starting transfers between devices, per_device(): received = lax.ppermute(arrived, 'local', swap)  3.67 us
  transfers between devices with their start and end apart: 6, of which 3 were waited for; matrix products, arithmetic and copies ran while one was open for 0% of the time, Pallas kernels for 3%

profile of v6, /device:TPU:1, one launch (start us, length us, event | category | flops | bytes accessed | tf_op | source)
XLA Modules:
  0.0 181.2 jit_solution(6791284038272576144)
XLA Ops:
  0.6 2.1 %shard_map.104.after_ref = bf16[32,4,1152]{2,1,0:T(4,128)(2,1)} custom-call(s32[4,128]{1,0:T(4,128)} %bitcast.32, s32[4,1,128]{2,1,0:T(1,128)} %bitcast.35, bf16[4,128]{1,0:T(4,128)(2,1)} %bitcast.36, bf16[224,128]{1,0:T(8,128)(2,1)} %bitcast.34), custom_call_target="tpu_custom_call" | custom-call | tf_op jit(solution)/shard_map/pallas_call | solution.py:337
  2.8 0.0 copy-start
  2.8 29.4 %all-to-all-start = ((bf16[32,4,1152]{2,1,0:T(4,128)(2,1)}), bf16[32,4,1152]{2,1,0:T(4,128)(2,1)S(1)}, u32[]{:S(2)}, u32[]{:S(2)}) async-start(bf16[32,4,1152]{2,1,0:T(4,128)(2,1)} %shard_map.104.after_ref), calls=%async_computation | async-start | bytes 589824 | tf_op jit(solution)/shard_map/all_to_all | solution.py:365
  32.2 2.9 %collective-permute-start.1 = (bf16[2,224,1024]{2,1,0:T(8,128)(2,1)}, bf16[2,224,1024]{2,1,0:T(8,128)(2,1)S(1)}, u32[]{:S(2)}, u32[]{:S(2)}) collective-permute-start(bf16[2,224,1024]{2,1,0:T(8,128)(2,1)} %bitcast.26), channel_id=1, source_target_pairs={{0,1},{1,0},{2,3},{3,2},{4,5},{5,4},{6,7},{7,6},{8,9},{9,8},{10,11... | collective-permute-start | bytes 2752520 | tf_op jit(solution)/shard_map/ppermute | solution.py:351
  35.1 1.9 %collective-permute-start.2 = (bf16[2,224,1024]{2,1,0:T(8,128)(2,1)}, bf16[2,224,1024]{2,1,0:T(8,128)(2,1)S(1)}, u32[]{:S(2)}, u32[]{:S(2)}) collective-permute-start(bf16[2,224,1024]{2,1,0:T(8,128)(2,1)} %bitcast.28), channel_id=1, source_target_pairs={{0,1},{1,0},{2,3},{3,2},{4,5},{5,4},{6,7},{7,6},{8,9},{9,8},{10,11... | collective-permute-start | bytes 2752520 | tf_op jit(solution)/shard_map/ppermute | solution.py:351
  37.0 0.4 collective-permute-done.1.refs_0_
  37.4 2.3 %collective-permute-done.2.refs_1_ = bf16[2,224,1024]{2,1,0:T(8,128)(2,1)S(1)} collective-permute-done((bf16[2,224,1024]{2,1,0:T(8,128)(2,1)}, bf16[2,224,1024]{2,1,0:T(8,128)(2,1)S(1)}, u32[]{:S(2)}, u32[]{:S(2)}) %collective-permute-start.2) | collective-permute-done | bytes 917536 | tf_op jit(solution)/shard_map/ppermute | solution.py:351
  39.7 0.0 copy-done.9
  39.7 0.9 copy-done.10
  40.6 2.8 %shard_map.105 = (bf16[2,224,1024]{2,1,0:T(8,128)(2,1)}, bf16[2,224,1024]{2,1,0:T(8,128)(2,1)}) custom-call(bf16[32,4,1152]{2,1,0:T(4,128)(2,1)} %shard_map.104.after_ref, bf16[2,224,1024]{2,1,0:T(8,128)(2,1)} %copy-done.9, bf16[2,224,1024]{2,1,0:T(8,128)(2,1)} %copy-done.10), custom_call_target="tpu_custom_call" | custom-call | tf_op jit(solution)/shard_map/pallas_call | solution.py:354
  43.4 0.0 copy-done
  43.4 1.2 copy-done.1
  44.6 0.1 shard_map.106
  44.6 2.0 %collective-permute-start.3 = (bf16[2,224,1024]{2,1,0:T(8,128)(2,1)S(1)}, bf16[2,224,1024]{2,1,0:T(8,128)(2,1)S(1)}, u32[]{:S(2)}, u32[]{:S(2)}) collective-permute-start(bf16[2,224,1024]{2,1,0:T(8,128)(2,1)S(1)} %shard_map.106), channel_id=1, source_target_pairs={{0,1},{1,0},{2,3},{3,2},{4,5},{5,4},{6,7},{7,6},{8,9},{9,8},{10,11... | collective-permute-start | bytes 2752520 | tf_op jit(solution)/shard_map/ppermute | solution.py:364
  46.7 30.1 %all-to-all-done = bf16[32,4,1152]{2,1,0:T(4,128)(2,1)S(1)} async-done(((bf16[32,4,1152]{2,1,0:T(4,128)(2,1)}), bf16[32,4,1152]{2,1,0:T(4,128)(2,1)S(1)}, u32[]{:S(2)}, u32[]{:S(2)}) %all-to-all-start) | async-done | bytes 294944 | tf_op jit(solution)/shard_map/all_to_all | solution.py:365
  76.7 3.7 %collective-permute-start = (bf16[16,2,4,1152]{3,2,1,0:T(4,128)(2,1)S(1)}, bf16[16,2,4,1152]{3,2,1,0:T(4,128)(2,1)S(1)}, u32[]{:S(2)}, u32[]{:S(2)}) collective-permute-start(bf16[16,2,4,1152]{3,2,1,0:T(4,128)(2,1)S(1)} %bitcast.22), channel_id=1, source_target_pairs={{0,1},{1,0},{2,3},{3,2},{4,5},{5,4},{6,7},{7,6},{8,9},{9,8},{10,11... | collective-permute-start | bytes 884744 | tf_op jit(solution)/shard_map/ppermute | solution.py:376
  80.4 1.2 shard_map.107.refs_0_
  81.6 0.0 copy-start.6
  81.6 0.0 copy-start.7
  81.6 0.0 collective-permute-done.3.down_ref
  81.6 0.0 collective-permute-done.in_ref
  81.6 1.2 shard_map.108
  82.8 18.6 %all_to_all.20.parts_ref = bf16[16,160,128]{2,1,0:T(8,128)(2,1)S(1)} all-to-all(bf16[16,160,128]{2,1,0:T(8,128)(2,1)S(1)} %shard_map.108), channel_id=1, replica_groups={{0,2,4,6,8,10,12,14,16,18,20,22,24,26,28,30},{1,3,5,7,9,11,13,15,17,19,..., dimensions={0} | all-to-all | bytes 1310720 | tf_op jit(solution)/shard_map/all_to_all | solution.py:379
  101.4 0.3 shard_map.109
  101.8 21.5 %all_to_all.21.in_ref = bf16[16,336,128]{2,1,0:T(8,128)(2,1)S(1)} all-to-all(bf16[16,336,128]{2,1,0:T(8,128)(2,1)S(1)} %shard_map.109), channel_id=1, replica_groups={{0,2,4,6,8,10,12,14,16,18,20,22,24,26,28,30},{1,3,5,7,9,11,13,15,17,19,..., dimensions={0} | all-to-all | bytes 2752512 | tf_op jit(solution)/shard_map/all_to_all | solution.py:388
  123.3 1.4 shard_map.111
  124.7 0.0 copy-start.8
  124.7 5.2 %collective-permute-start.4 = (bf16[16,4,1152]{2,1,0:T(4,128)(2,1)S(1)}, bf16[16,4,1152]{2,1,0:T(4,128)(2,1)S(1)}, u32[]{:S(2)}, u32[]{:S(2)}) collective-permute-start(bf16[16,4,1152]{2,1,0:T(4,128)(2,1)S(1)} %shard_map.111), channel_id=1, source_target_pairs={{0,1},{1,0},{2,3},{3,2},{4,5},{5,4},{6,7},{7,6},{8,9},{9,8},{10,11... | collective-permute-start | bytes 442376 | tf_op jit(solution)/shard_map/ppermute | solution.py:400
  129.9 1.4 shard_map.110.mine_ref
  131.3 0.0 collective-permute-done.4.other_ref
  131.4 48.7 %all_to_all.22.in_ref = bf16[32,4,1152]{2,1,0:T(4,128)(2,1)S(1)} all-to-all(bf16[32,4,1152]{2,1,0:T(4,128)(2,1)S(1)} %bitcast.25), channel_id=1, replica_groups=mesh['node'=32,'local'=32] {'node'}, dimensions={0} | all-to-all | bytes 589824 | tf_op jit(solution)/shard_map/all_to_all | solution.py:408
  180.1 1.1 shard_map.113
  (15 shorter events, 0.1 us)
Async XLA Ops:
  2.8 40.6 %copy-start = (bf16[1,2,1024,224]{2,3,1,0:T(8,128)(2,1)S(1)}, bf16[1,2,1024,224]{2,3,1,0:T(8,128)(2,1)}, u32[]{:S(2)}) copy-start(bf16[1,2,1024,224]{2,3,1,0:T(8,128)(2,1)} %param.15) | copy-start | bytes 2752516
  2.8 73.9 %all-to-all-start = ((bf16[32,4,1152]{2,1,0:T(4,128)(2,1)}), bf16[32,4,1152]{2,1,0:T(4,128)(2,1)S(1)}, u32[]{:S(2)}, u32[]{:S(2)}) async-start(bf16[32,4,1152]{2,1,0:T(4,128)(2,1)} %shard_map.104.after_ref), calls=%async_computation | async-start | bytes 589824 | tf_op jit(solution)/shard_map/all_to_all | solution.py:365
  32.2 5.2 %collective-permute-start.1 = (bf16[2,224,1024]{2,1,0:T(8,128)(2,1)}, bf16[2,224,1024]{2,1,0:T(8,128)(2,1)S(1)}, u32[]{:S(2)}, u32[]{:S(2)}) collective-permute-start(bf16[2,224,1024]{2,1,0:T(8,128)(2,1)} %bitcast.26), channel_id=1, source_target_pairs={{0,1},{1,0},{2,3},{3,2},{4,5},{5,4},{6,7},{7,6},{8,9},{9,8},{10,11... | collective-permute-start | bytes 2752520 | tf_op jit(solution)/shard_map/ppermute | solution.py:351
  35.1 4.6 %collective-permute-start.2 = (bf16[2,224,1024]{2,1,0:T(8,128)(2,1)}, bf16[2,224,1024]{2,1,0:T(8,128)(2,1)S(1)}, u32[]{:S(2)}, u32[]{:S(2)}) collective-permute-start(bf16[2,224,1024]{2,1,0:T(8,128)(2,1)} %bitcast.28), channel_id=1, source_target_pairs={{0,1},{1,0},{2,3},{3,2},{4,5},{5,4},{6,7},{7,6},{8,9},{9,8},{10,11... | collective-permute-start | bytes 2752520 | tf_op jit(solution)/shard_map/ppermute | solution.py:351
  37.4 2.3 %copy-start.9 = (bf16[2,224,1024]{2,1,0:T(8,128)(2,1)}, bf16[2,224,1024]{2,1,0:T(8,128)(2,1)S(1)}, u32[]{:S(2)}) copy-start(bf16[2,224,1024]{2,1,0:T(8,128)(2,1)S(1)} %collective-permute-done.1.refs_0_) | copy-start | bytes 2752516
  39.7 0.9 copy-start.10
  43.4 1.2 copy-start.1
  44.6 37.0 %collective-permute-start.3 = (bf16[2,224,1024]{2,1,0:T(8,128)(2,1)S(1)}, bf16[2,224,1024]{2,1,0:T(8,128)(2,1)S(1)}, u32[]{:S(2)}, u32[]{:S(2)}) collective-permute-start(bf16[2,224,1024]{2,1,0:T(8,128)(2,1)S(1)} %shard_map.106), channel_id=1, source_target_pairs={{0,1},{1,0},{2,3},{3,2},{4,5},{5,4},{6,7},{7,6},{8,9},{9,8},{10,11... | collective-permute-start | bytes 2752520 | tf_op jit(solution)/shard_map/ppermute | solution.py:364
  76.7 4.9 %collective-permute-start = (bf16[16,2,4,1152]{3,2,1,0:T(4,128)(2,1)S(1)}, bf16[16,2,4,1152]{3,2,1,0:T(4,128)(2,1)S(1)}, u32[]{:S(2)}, u32[]{:S(2)}) collective-permute-start(bf16[16,2,4,1152]{3,2,1,0:T(4,128)(2,1)S(1)} %bitcast.22), channel_id=1, source_target_pairs={{0,1},{1,0},{2,3},{3,2},{4,5},{5,4},{6,7},{7,6},{8,9},{9,8},{10,11... | collective-permute-start | bytes 884744 | tf_op jit(solution)/shard_map/ppermute | solution.py:376
  81.6 19.8 %copy-start.6 = (bf16[1,20,1,1024]{3,1,2,0:T(8,128)(2,1)S(1)}, bf16[1,20,1,1024]{3,1,2,0:T(8,128)(2,1)}, u32[]{:S(2)}) copy-start(bf16[1,20,1,1024]{3,1,2,0:T(8,128)(2,1)} %param.16) | copy-start | bytes 122884
  81.6 19.8 %copy-start.7 = (bf16[1,20,1,1024]{3,1,2,0:T(8,128)(2,1)S(1)}, bf16[1,20,1,1024]{3,1,2,0:T(8,128)(2,1)}, u32[]{:S(2)}) copy-start(bf16[1,20,1,1024]{3,1,2,0:T(8,128)(2,1)} %param.17) | copy-start | bytes 122884
  101.8 21.5 %copy-start.2 = (bf16[2,224,1024]{2,1,0:T(8,128)(2,1)S(1)}, bf16[2,224,1024]{2,1,0:T(8,128)(2,1)}, u32[]{:S(2)}) copy-start(bf16[2,224,1024]{2,1,0:T(8,128)(2,1)} %get-tuple-element.6.after_ref.gate_ref) | copy-start | bytes 2752516
  101.8 21.5 %copy-start.5 = (bf16[2,224,1024]{2,1,0:T(8,128)(2,1)S(1)}, bf16[2,224,1024]{2,1,0:T(8,128)(2,1)}, u32[]{:S(2)}) copy-start(bf16[2,224,1024]{2,1,0:T(8,128)(2,1)} %get-tuple-element.7.up_ref) | copy-start | bytes 2752516
  123.3 6.7 %copy-start.3 = (bf16[1,2,224,1024]{3,2,1,0:T(8,128)(2,1)S(1)}, bf16[1,2,224,1024]{3,2,1,0:T(8,128)(2,1)}, u32[]{:S(2)}) copy-start(bf16[1,2,224,1024]{3,2,1,0:T(8,128)(2,1)} %param.13) | copy-start | bytes 2752516
  123.3 6.7 %copy-start.4 = (bf16[1,2,224,1024]{3,2,1,0:T(8,128)(2,1)S(1)}, bf16[1,2,224,1024]{3,2,1,0:T(8,128)(2,1)}, u32[]{:S(2)}) copy-start(bf16[1,2,224,1024]{3,2,1,0:T(8,128)(2,1)} %param.14) | copy-start | bytes 2752516
  124.7 55.5 %copy-start.8 = (s32[128,4]{0,1:T(4,128)S(1)}, s32[128,4]{0,1:T(4,128)}, u32[]{:S(2)}) copy-start(s32[128,4]{0,1:T(4,128)} %param.10) | copy-start | bytes 6148
  124.7 6.7 %collective-permute-start.4 = (bf16[16,4,1152]{2,1,0:T(4,128)(2,1)S(1)}, bf16[16,4,1152]{2,1,0:T(4,128)(2,1)S(1)}, u32[]{:S(2)}, u32[]{:S(2)}) collective-permute-start(bf16[16,4,1152]{2,1,0:T(4,128)(2,1)S(1)} %shard_map.111), channel_id=1, source_target_pairs={{0,1},{1,0},{2,3},{3,2},{4,5},{5,4},{6,7},{7,6},{8,9},{9,8},{10,11... | collective-permute-start | bytes 442376 | tf_op jit(solution)/shard_map/ppermute | solution.py:400

commit v7 on v6

--- a/solution.py
+++ b/solution.py
@@ -12,6 +12,7 @@
 LANES = 128
 FOLD = 4
 VMEM_LIMIT = 32 * 1024 * 1024
+CURVE = (0, 1, 5, 4, 8, 12, 13, 9, 10, 14, 15, 11, 7, 6, 2, 3)
 VMEM_MOST = 58 * 1024 * 1024
 
 
@@ -44,11 +45,15 @@
     )
 
 
+def chip_order(chips):
+    return CURVE if chips == len(CURVE) else tuple(range(chips))
+
+
 def pair_maps(pick, nodes):
     groups, tokens = pick.shape
     rows = nodes * FOLD
     row = iota((rows, tokens), 0)
-    node_of = row // FOLD
+    node_of = nodes - 1 - row // FOLD
     hits = [pick[g : g + 1, :] == node_of for g in range(groups)]
     named = functools.reduce(jnp.logical_or, hits)
     earlier = (iota((tokens, tokens), 0) < iota((tokens, tokens), 1)).astype(F32).astype(BF16)
@@ -156,7 +161,7 @@
     blocks = out_ref.shape[0]
     units = down_ref.shape[2]
     slots = pieces * FOLD
-    folded = in_ref[:, which_ref[0]].astype(F32).reshape(blocks * FOLD, in_ref.shape[3])
+    folded = in_ref[:, 1 - which_ref[0]].astype(F32).reshape(blocks * FOLD, in_ref.shape[3])
     base = pieces * width
     spare = jnp.zeros((blocks * FOLD, 2 * LANES - width - 1), F32)
     stacked = []
@@ -178,9 +183,11 @@
     rows = parts[0].shape[1]
     for at, part in enumerate(parts):
         span = slice(at * rows, (at + 1) * rows)
-        if len(refs) > 1:
-            part = part + refs[0][:, span, :]
-        out_ref[:, span, :] = part.astype(out_ref.dtype)
+        for to, chip in enumerate(chip_order(blocks)):
+            block = part[blocks - 1 - chip]
+            if len(refs) > 1:
+                block = block + refs[0][to, span]
+            out_ref[to, span] = block.astype(out_ref.dtype)
 
 
 def lanes_of(column):
@@ -197,7 +204,8 @@
     raw = jnp.concatenate(
         [total[tile * slots : (tile + 1) * slots] for tile in range(units // LANES)], axis=1
     )
-    own = in_ref[at_ref[0] >> 1, at_ref[0] & 1].astype(F32)
+    at = 2 * in_ref.shape[0] - 1 - at_ref[0]
+    own = in_ref[at >> 1, at & 1].astype(F32)
     base = pieces * width
     picked = jnp.concatenate(
         [own[:, base + at : base + at + 1] for at in range(pieces)], axis=0
@@ -269,13 +277,14 @@
     parts.append(nn(router, gather.astype(F32).astype(BF16)))
     sent = jnp.concatenate(parts, axis=1)
     sent = sent.reshape(blocks, FOLD, sent.shape[1]).astype(BF16)
-    out_ref[...] = sent
+    for at, chip in enumerate(chip_order(blocks)):
+        out_ref[blocks - 1 - chip] = sent[at]
 
 
 def merge_kernel(which_ref, mine_ref, other_ref, out_ref):
     which = which_ref[0]
-    out_ref[:, which] = mine_ref[...]
-    out_ref[:, 1 - which] = other_ref[...]
+    out_ref[:, 1 - which] = mine_ref[...]
+    out_ref[:, which] = other_ref[...]
 
 
 def finish_kernel(pieces, width, in_ref, pick_ref, grad_ref, router_ref):
@@ -323,7 +332,8 @@
     place = lax.axis_index("local").astype(jnp.int32)
     own = place.reshape(1)
     mine = own & 1
-    same_core = [[2 * chip + c for chip in range(chips)] for c in range(2)]
+    same_core = [[2 * chip + c for chip in chip_order(chips)] for c in range(2)]
+    backwards = [list(range(nodes))[::-1]]
     swap = [(at, at ^ 1) for at in range(local_count)]
 
     pick = node_pick.T
@@ -362,7 +372,9 @@
     others = keep(sent, VMEM_MOST, *others)
     (sent_down,) = keep(others[0], VMEM_LIMIT, down)
     other_down = lax.ppermute(sent_down, "local", swap)
-    arrived = lax.all_to_all(sent, "node", split_axis=0, concat_axis=0, tiled=True)
+    arrived = lax.all_to_all(
+        sent, "node", split_axis=0, concat_axis=0, axis_index_groups=backwards, tiled=True
+    )
     arrived = arrived.reshape(half, 2, FOLD, block)
 
     def raw_part(rows, weight, dtype, *before):
@@ -405,7 +417,9 @@
         out_specs=vmem,
     )(mine, back_part(gate_weight[0], up_weight[0]), theirs)
     back = back.reshape(nodes, FOLD, block)
-    returned = lax.all_to_all(back, "node", split_axis=0, concat_axis=0, tiled=True)
+    returned = lax.all_to_all(
+        back, "node", split_axis=0, concat_axis=0, axis_index_groups=backwards, tiled=True
+    )
     grad, router = call(
         functools.partial(finish_kernel, pieces, width),
         (

time: 182 us -> 178 us (0.978)
  the two profiles are of different devices: /device:TPU:1 before, /device:TPU:33 now
where the time goes in v7:
time: 178 us; the launch traced here: 177 us
  blocking collectives  89.9 us (51%)
  starting transfers between devices  43.3 us (24%)
  waiting for transfers between devices  29.6 us (17%)
  Pallas kernels  11.6 us (7%)
  local copies, waits for them, and re-layouts  2.14 us (1%)
    all_to_all x1, blocking collectives, per_device(): lax.all_to_all(back, 'node', split_axis=0, concat_axis=0, axis_index_grou...  48.8 us
    all_to_all x1, starting transfers between devices, per_device(): lax.all_to_all(sent, 'node', split_axis=0, concat_axis=0, axis_index_grou...  28.3 us
    all_to_all x1, waiting for transfers between devices, per_device(): lax.all_to_all(sent, 'node', split_axis=0, concat_axis=0, axis_index_grou...  27 us
    all_to_all x1, blocking collectives, per_device(): lax.all_to_all(hidden, 'local', split_axis=0, concat_axis=0, axis_index_g...  21.9 us
    all_to_all x1, blocking collectives, per_device(): lax.all_to_all(partial, 'local', split_axis=0, concat_axis=0, axis_index_...  19.3 us
    ppermute x2, starting transfers between devices, per_device(): lax.ppermute(weight[0], 'local', swap)  5.07 us
    ppermute x1, starting transfers between devices, per_device(): theirs = lax.ppermute(back_part(*others), 'local', swap)  4.29 us
    ppermute x1, starting transfers between devices, per_device(): received = lax.ppermute(arrived, 'local', swap)  3.64 us
  transfers between devices with their start and end apart: 6, of which 3 were waited for; matrix products, arithmetic and copies ran while one was open for 0% of the time, Pallas kernels for 3%

profile of v7, /device:TPU:33, one launch (start us, length us, event | category | flops | bytes accessed | tf_op | source)
XLA Modules:
  0.0 177.4 jit_solution(2006272326886902286)
XLA Ops:
  0.6 2.2 %shard_map.104.after_ref = bf16[32,4,1152]{2,1,0:T(4,128)(2,1)} custom-call(s32[4,128]{1,0:T(4,128)} %bitcast.32, s32[4,1,128]{2,1,0:T(1,128)} %bitcast.35, bf16[4,128]{1,0:T(4,128)(2,1)} %bitcast.36, bf16[224,128]{1,0:T(8,128)(2,1)} %bitcast.34), custom_call_target="tpu_custom_call" | custom-call | tf_op jit(solution)/shard_map/pallas_call | solution.py:347
  2.8 0.0 copy-start
  2.8 28.3 %all-to-all-start = ((bf16[32,4,1152]{2,1,0:T(4,128)(2,1)}), bf16[32,4,1152]{2,1,0:T(4,128)(2,1)S(1)}, u32[]{:S(2)}, u32[]{:S(2)}) async-start(bf16[32,4,1152]{2,1,0:T(4,128)(2,1)} %shard_map.104.after_ref), calls=%async_computation | async-start | bytes 589824 | tf_op jit(solution)/shard_map/all_to_all | solution.py:375
  31.1 3.1 %collective-permute-start.1 = (bf16[2,224,1024]{2,1,0:T(8,128)(2,1)}, bf16[2,224,1024]{2,1,0:T(8,128)(2,1)S(1)}, u32[]{:S(2)}, u32[]{:S(2)}) collective-permute-start(bf16[2,224,1024]{2,1,0:T(8,128)(2,1)} %bitcast.26), channel_id=1, source_target_pairs={{0,1},{1,0},{2,3},{3,2},{4,5},{5,4},{6,7},{7,6},{8,9},{9,8},{10,11... | collective-permute-start | bytes 2752520 | tf_op jit(solution)/shard_map/ppermute | solution.py:361
  34.2 1.9 %collective-permute-start.2 = (bf16[2,224,1024]{2,1,0:T(8,128)(2,1)}, bf16[2,224,1024]{2,1,0:T(8,128)(2,1)S(1)}, u32[]{:S(2)}, u32[]{:S(2)}) collective-permute-start(bf16[2,224,1024]{2,1,0:T(8,128)(2,1)} %bitcast.28), channel_id=1, source_target_pairs={{0,1},{1,0},{2,3},{3,2},{4,5},{5,4},{6,7},{7,6},{8,9},{9,8},{10,11... | collective-permute-start | bytes 2752520 | tf_op jit(solution)/shard_map/ppermute | solution.py:361
  36.2 0.4 collective-permute-done.1.refs_0_
  36.5 2.3 %collective-permute-done.2.refs_1_ = bf16[2,224,1024]{2,1,0:T(8,128)(2,1)S(1)} collective-permute-done((bf16[2,224,1024]{2,1,0:T(8,128)(2,1)}, bf16[2,224,1024]{2,1,0:T(8,128)(2,1)S(1)}, u32[]{:S(2)}, u32[]{:S(2)}) %collective-permute-start.2) | collective-permute-done | bytes 917536 | tf_op jit(solution)/shard_map/ppermute | solution.py:361
  38.8 0.0 copy-done.9
  38.8 0.9 copy-done.10
  39.7 2.8 %shard_map.105 = (bf16[2,224,1024]{2,1,0:T(8,128)(2,1)}, bf16[2,224,1024]{2,1,0:T(8,128)(2,1)}) custom-call(bf16[32,4,1152]{2,1,0:T(4,128)(2,1)} %shard_map.104.after_ref, bf16[2,224,1024]{2,1,0:T(8,128)(2,1)} %copy-done.9, bf16[2,224,1024]{2,1,0:T(8,128)(2,1)} %copy-done.10), custom_call_target="tpu_custom_call" | custom-call | tf_op jit(solution)/shard_map/pallas_call | solution.py:364
  42.5 1.2 copy-done.1
  43.7 0.1 shard_map.106
  43.8 2.0 %collective-permute-start.3 = (bf16[2,224,1024]{2,1,0:T(8,128)(2,1)S(1)}, bf16[2,224,1024]{2,1,0:T(8,128)(2,1)S(1)}, u32[]{:S(2)}, u32[]{:S(2)}) collective-permute-start(bf16[2,224,1024]{2,1,0:T(8,128)(2,1)S(1)} %shard_map.106), channel_id=1, source_target_pairs={{0,1},{1,0},{2,3},{3,2},{4,5},{5,4},{6,7},{7,6},{8,9},{9,8},{10,11... | collective-permute-start | bytes 2752520 | tf_op jit(solution)/shard_map/ppermute | solution.py:374
  45.8 27.0 %all-to-all-done = bf16[32,4,1152]{2,1,0:T(4,128)(2,1)S(1)} async-done(((bf16[32,4,1152]{2,1,0:T(4,128)(2,1)}), bf16[32,4,1152]{2,1,0:T(4,128)(2,1)S(1)}, u32[]{:S(2)}, u32[]{:S(2)}) %all-to-all-start) | async-done | bytes 294944 | tf_op jit(solution)/shard_map/all_to_all | solution.py:375
  72.8 3.6 %collective-permute-start = (bf16[16,2,4,1152]{3,2,1,0:T(4,128)(2,1)S(1)}, bf16[16,2,4,1152]{3,2,1,0:T(4,128)(2,1)S(1)}, u32[]{:S(2)}, u32[]{:S(2)}) collective-permute-start(bf16[16,2,4,1152]{3,2,1,0:T(4,128)(2,1)S(1)} %bitcast.22), channel_id=1, source_target_pairs={{0,1},{1,0},{2,3},{3,2},{4,5},{5,4},{6,7},{7,6},{8,9},{9,8},{10,11... | collective-permute-start | bytes 884744 | tf_op jit(solution)/shard_map/ppermute | solution.py:388
  76.4 1.2 shard_map.107.refs_0_
  77.6 0.0 copy-start.6
  77.6 0.0 copy-start.7
  77.6 0.0 collective-permute-done.3.down_ref
  77.7 0.0 collective-permute-done.in_ref
  77.7 1.2 shard_map.108
  78.9 19.3 %all_to_all.20.parts_ref = bf16[16,160,128]{2,1,0:T(8,128)(2,1)S(1)} all-to-all(bf16[16,160,128]{2,1,0:T(8,128)(2,1)S(1)} %shard_map.108), channel_id=1, replica_groups={{0,2,10,8,16,24,26,18,20,28,30,22,14,12,4,6},{1,3,11,9,17,25,27,19,21,2..., dimensions={0} | all-to-all | bytes 1310720 | tf_op jit(solution)/shard_map/all_to_all | solution.py:391
  98.1 0.0 copy-done.6
  98.1 0.3 shard_map.109
  98.5 21.9 %all_to_all.21.in_ref = bf16[16,336,128]{2,1,0:T(8,128)(2,1)S(1)} all-to-all(bf16[16,336,128]{2,1,0:T(8,128)(2,1)S(1)} %shard_map.109), channel_id=1, replica_groups={{0,2,10,8,16,24,26,18,20,28,30,22,14,12,4,6},{1,3,11,9,17,25,27,19,21,2..., dimensions={0} | all-to-all | bytes 2752512 | tf_op jit(solution)/shard_map/all_to_all | solution.py:400
  120.4 1.4 shard_map.111
  121.8 0.0 copy-start.8
  121.8 4.3 %collective-permute-start.4 = (bf16[16,4,1152]{2,1,0:T(4,128)(2,1)S(1)}, bf16[16,4,1152]{2,1,0:T(4,128)(2,1)S(1)}, u32[]{:S(2)}, u32[]{:S(2)}) collective-permute-start(bf16[16,4,1152]{2,1,0:T(4,128)(2,1)S(1)} %shard_map.111), channel_id=1, source_target_pairs={{0,1},{1,0},{2,3},{3,2},{4,5},{5,4},{6,7},{7,6},{8,9},{9,8},{10,11... | collective-permute-start | bytes 442376 | tf_op jit(solution)/shard_map/ppermute | solution.py:412
  126.1 1.4 shard_map.110.mine_ref
  127.5 0.0 collective-permute-done.4.other_ref
  127.6 48.8 %all_to_all.22.in_ref = bf16[32,4,1152]{2,1,0:T(4,128)(2,1)S(1)} all-to-all(bf16[32,4,1152]{2,1,0:T(4,128)(2,1)S(1)} %bitcast.25), channel_id=1, replica_groups={{992,960,928,896,864,832,800,768,736,704,672,640,608,576,544,512,480,44..., dimensions={0} | all-to-all | bytes 589824 | tf_op jit(solution)/shard_map/all_to_all | solution.py:420
  176.3 1.1 shard_map.113
  (15 shorter events, 0.1 us)
Async XLA Ops:
  2.8 39.7 %copy-start = (bf16[1,2,1024,224]{2,3,1,0:T(8,128)(2,1)S(1)}, bf16[1,2,1024,224]{2,3,1,0:T(8,128)(2,1)}, u32[]{:S(2)}) copy-start(bf16[1,2,1024,224]{2,3,1,0:T(8,128)(2,1)} %param.15) | copy-start | bytes 2752516
  2.8 70.0 %all-to-all-start = ((bf16[32,4,1152]{2,1,0:T(4,128)(2,1)}), bf16[32,4,1152]{2,1,0:T(4,128)(2,1)S(1)}, u32[]{:S(2)}, u32[]{:S(2)}) async-start(bf16[32,4,1152]{2,1,0:T(4,128)(2,1)} %shard_map.104.after_ref), calls=%async_computation | async-start | bytes 589824 | tf_op jit(solution)/shard_map/all_to_all | solution.py:375
  31.1 5.4 %collective-permute-start.1 = (bf16[2,224,1024]{2,1,0:T(8,128)(2,1)}, bf16[2,224,1024]{2,1,0:T(8,128)(2,1)S(1)}, u32[]{:S(2)}, u32[]{:S(2)}) collective-permute-start(bf16[2,224,1024]{2,1,0:T(8,128)(2,1)} %bitcast.26), channel_id=1, source_target_pairs={{0,1},{1,0},{2,3},{3,2},{4,5},{5,4},{6,7},{7,6},{8,9},{9,8},{10,11... | collective-permute-start | bytes 2752520 | tf_op jit(solution)/shard_map/ppermute | solution.py:361
  34.2 4.6 %collective-permute-start.2 = (bf16[2,224,1024]{2,1,0:T(8,128)(2,1)}, bf16[2,224,1024]{2,1,0:T(8,128)(2,1)S(1)}, u32[]{:S(2)}, u32[]{:S(2)}) collective-permute-start(bf16[2,224,1024]{2,1,0:T(8,128)(2,1)} %bitcast.28), channel_id=1, source_target_pairs={{0,1},{1,0},{2,3},{3,2},{4,5},{5,4},{6,7},{7,6},{8,9},{9,8},{10,11... | collective-permute-start | bytes 2752520 | tf_op jit(solution)/shard_map/ppermute | solution.py:361
  36.5 2.3 %copy-start.9 = (bf16[2,224,1024]{2,1,0:T(8,128)(2,1)}, bf16[2,224,1024]{2,1,0:T(8,128)(2,1)S(1)}, u32[]{:S(2)}) copy-start(bf16[2,224,1024]{2,1,0:T(8,128)(2,1)S(1)} %collective-permute-done.1.refs_0_) | copy-start | bytes 2752516
  38.8 0.9 copy-start.10
  42.5 1.2 copy-start.1
  43.8 33.9 %collective-permute-start.3 = (bf16[2,224,1024]{2,1,0:T(8,128)(2,1)S(1)}, bf16[2,224,1024]{2,1,0:T(8,128)(2,1)S(1)}, u32[]{:S(2)}, u32[]{:S(2)}) collective-permute-start(bf16[2,224,1024]{2,1,0:T(8,128)(2,1)S(1)} %shard_map.106), channel_id=1, source_target_pairs={{0,1},{1,0},{2,3},{3,2},{4,5},{5,4},{6,7},{7,6},{8,9},{9,8},{10,11... | collective-permute-start | bytes 2752520 | tf_op jit(solution)/shard_map/ppermute | solution.py:374
  72.8 4.9 %collective-permute-start = (bf16[16,2,4,1152]{3,2,1,0:T(4,128)(2,1)S(1)}, bf16[16,2,4,1152]{3,2,1,0:T(4,128)(2,1)S(1)}, u32[]{:S(2)}, u32[]{:S(2)}) collective-permute-start(bf16[16,2,4,1152]{3,2,1,0:T(4,128)(2,1)S(1)} %bitcast.22), channel_id=1, source_target_pairs={{0,1},{1,0},{2,3},{3,2},{4,5},{5,4},{6,7},{7,6},{8,9},{9,8},{10,11... | collective-permute-start | bytes 884744 | tf_op jit(solution)/shard_map/ppermute | solution.py:388
  77.6 20.5 %copy-start.6 = (bf16[1,20,1,1024]{3,1,2,0:T(8,128)(2,1)S(1)}, bf16[1,20,1,1024]{3,1,2,0:T(8,128)(2,1)}, u32[]{:S(2)}) copy-start(bf16[1,20,1,1024]{3,1,2,0:T(8,128)(2,1)} %param.16) | copy-start | bytes 122884
  77.6 20.5 %copy-start.7 = (bf16[1,20,1,1024]{3,1,2,0:T(8,128)(2,1)S(1)}, bf16[1,20,1,1024]{3,1,2,0:T(8,128)(2,1)}, u32[]{:S(2)}) copy-start(bf16[1,20,1,1024]{3,1,2,0:T(8,128)(2,1)} %param.17) | copy-start | bytes 122884
  98.4 21.9 %copy-start.2 = (bf16[2,224,1024]{2,1,0:T(8,128)(2,1)S(1)}, bf16[2,224,1024]{2,1,0:T(8,128)(2,1)}, u32[]{:S(2)}) copy-start(bf16[2,224,1024]{2,1,0:T(8,128)(2,1)} %get-tuple-element.6.after_ref.gate_ref) | copy-start | bytes 2752516
  98.5 21.9 %copy-start.5 = (bf16[2,224,1024]{2,1,0:T(8,128)(2,1)S(1)}, bf16[2,224,1024]{2,1,0:T(8,128)(2,1)}, u32[]{:S(2)}) copy-start(bf16[2,224,1024]{2,1,0:T(8,128)(2,1)} %get-tuple-element.7.up_ref) | copy-start | bytes 2752516
  120.4 5.7 %copy-start.3 = (bf16[1,2,224,1024]{3,2,1,0:T(8,128)(2,1)S(1)}, bf16[1,2,224,1024]{3,2,1,0:T(8,128)(2,1)}, u32[]{:S(2)}) copy-start(bf16[1,2,224,1024]{3,2,1,0:T(8,128)(2,1)} %param.13) | copy-start | bytes 2752516
  120.4 5.7 %copy-start.4 = (bf16[1,2,224,1024]{3,2,1,0:T(8,128)(2,1)S(1)}, bf16[1,2,224,1024]{3,2,1,0:T(8,128)(2,1)}, u32[]{:S(2)}) copy-start(bf16[1,2,224,1024]{3,2,1,0:T(8,128)(2,1)} %param.14) | copy-start | bytes 2752516
  121.8 54.5 %copy-start.8 = (s32[128,4]{0,1:T(4,128)S(1)}, s32[128,4]{0,1:T(4,128)}, u32[]{:S(2)}) copy-start(s32[128,4]{0,1:T(4,128)} %param.10) | copy-start | bytes 6148
  121.8 5.7 %collective-permute-start.4 = (bf16[16,4,1152]{2,1,0:T(4,128)(2,1)S(1)}, bf16[16,4,1152]{2,1,0:T(4,128)(2,1)S(1)}, u32[]{:S(2)}, u32[]{:S(2)}) collective-permute-start(bf16[16,4,1152]{2,1,0:T(4,128)(2,1)S(1)} %shard_map.111), channel_id=1, source_target_pairs={{0,1},{1,0},{2,3},{3,2},{4,5},{5,4},{6,7},{7,6},{8,9},{9,8},{10,11... | collective-permute-start | bytes 442376 | tf_op jit(solution)/shard_map/ppermute | solution.py:412

commit v8 on v7

--- a/solution.py
+++ b/solution.py
@@ -53,7 +53,7 @@
     groups, tokens = pick.shape
     rows = nodes * FOLD
     row = iota((rows, tokens), 0)
-    node_of = nodes - 1 - row // FOLD
+    node_of = (3 * nodes // 2 - 1 - row // FOLD) % nodes
     hits = [pick[g : g + 1, :] == node_of for g in range(groups)]
     named = functools.reduce(jnp.logical_or, hits)
     earlier = (iota((tokens, tokens), 0) < iota((tokens, tokens), 1)).astype(F32).astype(BF16)
@@ -184,7 +184,7 @@
     for at, part in enumerate(parts):
         span = slice(at * rows, (at + 1) * rows)
         for to, chip in enumerate(chip_order(blocks)):
-            block = part[blocks - 1 - chip]
+            block = part[(3 * blocks // 2 - 1 - chip) % blocks]
             if len(refs) > 1:
                 block = block + refs[0][to, span]
             out_ref[to, span] = block.astype(out_ref.dtype)
@@ -204,7 +204,7 @@
     raw = jnp.concatenate(
         [total[tile * slots : (tile + 1) * slots] for tile in range(units // LANES)], axis=1
     )
-    at = 2 * in_ref.shape[0] - 1 - at_ref[0]
+    at = (3 * in_ref.shape[0] - 1 - at_ref[0]) & (2 * in_ref.shape[0] - 1)
     own = in_ref[at >> 1, at & 1].astype(F32)
     base = pieces * width
     picked = jnp.concatenate(
@@ -278,7 +278,7 @@
     sent = jnp.concatenate(parts, axis=1)
     sent = sent.reshape(blocks, FOLD, sent.shape[1]).astype(BF16)
     for at, chip in enumerate(chip_order(blocks)):
-        out_ref[blocks - 1 - chip] = sent[at]
+        out_ref[(3 * blocks // 2 - 1 - chip) % blocks] = sent[at]
 
 
 def merge_kernel(which_ref, mine_ref, other_ref, out_ref):
@@ -333,7 +333,7 @@
     own = place.reshape(1)
     mine = own & 1
     same_core = [[2 * chip + c for chip in chip_order(chips)] for c in range(2)]
-    backwards = [list(range(nodes))[::-1]]
+    backwards = [[(half - 1 - at) % nodes for at in range(nodes)]]
     swap = [(at, at ^ 1) for at in range(local_count)]
 
     pick = node_pick.T

time: 178 us -> 171 us (0.961)
  the two profiles are of different devices: /device:TPU:33 before, /device:TPU:1 now
where the time goes in v8:
time: 171 us
  blocking collectives  89.7 us (52%)
  starting transfers between devices  50.4 us (29%)
  waiting for transfers between devices  16.2 us (9%)
  Pallas kernels  11.6 us (7%)
  local copies, waits for them, and re-layouts  2.14 us (1%)
    all_to_all x1, blocking collectives, per_device(): lax.all_to_all(back, 'node', split_axis=0, concat_axis=0, axis_index_grou...  48.5 us
    all_to_all x1, starting transfers between devices, per_device(): lax.all_to_all(sent, 'node', split_axis=0, concat_axis=0, axis_index_grou...  36.3 us
    all_to_all x1, blocking collectives, per_device(): lax.all_to_all(hidden, 'local', split_axis=0, concat_axis=0, axis_index_g...  21.9 us
    all_to_all x1, blocking collectives, per_device(): lax.all_to_all(partial, 'local', split_axis=0, concat_axis=0, axis_index_...  19.3 us
    all_to_all x1, waiting for transfers between devices, per_device(): lax.all_to_all(sent, 'node', split_axis=0, concat_axis=0, axis_index_grou...  13.5 us
    ppermute x2, starting transfers between devices, per_device(): lax.ppermute(weight[0], 'local', swap)  5.07 us
    ppermute x1, starting transfers between devices, per_device(): theirs = lax.ppermute(back_part(*others), 'local', swap)  4.29 us
  transfers between devices with their start and end apart: 6, of which 3 were waited for; matrix products, arithmetic and copies ran while one was open for 0% of the time, Pallas kernels for 3%

profile of v8, /device:TPU:1, one launch (start us, length us, event | category | flops | bytes accessed | tf_op | source)
XLA Modules:
  0.0 170.8 jit_solution(15533864771783647934)
XLA Ops:
  0.6 2.1 %shard_map.104.after_ref = bf16[32,4,1152]{2,1,0:T(4,128)(2,1)} custom-call(s32[4,128]{1,0:T(4,128)} %bitcast.32, s32[4,1,128]{2,1,0:T(1,128)} %bitcast.35, bf16[4,128]{1,0:T(4,128)(2,1)} %bitcast.36, bf16[224,128]{1,0:T(8,128)(2,1)} %bitcast.34), custom_call_target="tpu_custom_call" | custom-call | tf_op jit(solution)/shard_map/pallas_call | solution.py:347
  2.8 0.0 copy-start
  2.8 36.3 %all-to-all-start = ((bf16[32,4,1152]{2,1,0:T(4,128)(2,1)}), bf16[32,4,1152]{2,1,0:T(4,128)(2,1)S(1)}, u32[]{:S(2)}, u32[]{:S(2)}) async-start(bf16[32,4,1152]{2,1,0:T(4,128)(2,1)} %shard_map.104.after_ref), calls=%async_computation | async-start | bytes 589824 | tf_op jit(solution)/shard_map/all_to_all | solution.py:375
  39.1 3.1 %collective-permute-start.1 = (bf16[2,224,1024]{2,1,0:T(8,128)(2,1)}, bf16[2,224,1024]{2,1,0:T(8,128)(2,1)S(1)}, u32[]{:S(2)}, u32[]{:S(2)}) collective-permute-start(bf16[2,224,1024]{2,1,0:T(8,128)(2,1)} %bitcast.26), channel_id=1, source_target_pairs={{0,1},{1,0},{2,3},{3,2},{4,5},{5,4},{6,7},{7,6},{8,9},{9,8},{10,11... | collective-permute-start | bytes 2752520 | tf_op jit(solution)/shard_map/ppermute | solution.py:361
  42.2 1.9 %collective-permute-start.2 = (bf16[2,224,1024]{2,1,0:T(8,128)(2,1)}, bf16[2,224,1024]{2,1,0:T(8,128)(2,1)S(1)}, u32[]{:S(2)}, u32[]{:S(2)}) collective-permute-start(bf16[2,224,1024]{2,1,0:T(8,128)(2,1)} %bitcast.28), channel_id=1, source_target_pairs={{0,1},{1,0},{2,3},{3,2},{4,5},{5,4},{6,7},{7,6},{8,9},{9,8},{10,11... | collective-permute-start | bytes 2752520 | tf_op jit(solution)/shard_map/ppermute | solution.py:361
  44.2 0.4 collective-permute-done.1.refs_0_
  44.5 2.3 %collective-permute-done.2.refs_1_ = bf16[2,224,1024]{2,1,0:T(8,128)(2,1)S(1)} collective-permute-done((bf16[2,224,1024]{2,1,0:T(8,128)(2,1)}, bf16[2,224,1024]{2,1,0:T(8,128)(2,1)S(1)}, u32[]{:S(2)}, u32[]{:S(2)}) %collective-permute-start.2) | collective-permute-done | bytes 917536 | tf_op jit(solution)/shard_map/ppermute | solution.py:361
  46.8 0.0 copy-done.9
  46.8 0.9 copy-done.10
  47.8 2.8 %shard_map.105 = (bf16[2,224,1024]{2,1,0:T(8,128)(2,1)}, bf16[2,224,1024]{2,1,0:T(8,128)(2,1)}) custom-call(bf16[32,4,1152]{2,1,0:T(4,128)(2,1)} %shard_map.104.after_ref, bf16[2,224,1024]{2,1,0:T(8,128)(2,1)} %copy-done.9, bf16[2,224,1024]{2,1,0:T(8,128)(2,1)} %copy-done.10), custom_call_target="tpu_custom_call" | custom-call | tf_op jit(solution)/shard_map/pallas_call | solution.py:364
  50.5 1.2 copy-done.1
  51.7 0.1 shard_map.106
  51.8 2.0 %collective-permute-start.3 = (bf16[2,224,1024]{2,1,0:T(8,128)(2,1)S(1)}, bf16[2,224,1024]{2,1,0:T(8,128)(2,1)S(1)}, u32[]{:S(2)}, u32[]{:S(2)}) collective-permute-start(bf16[2,224,1024]{2,1,0:T(8,128)(2,1)S(1)} %shard_map.106), channel_id=1, source_target_pairs={{0,1},{1,0},{2,3},{3,2},{4,5},{5,4},{6,7},{7,6},{8,9},{9,8},{10,11... | collective-permute-start | bytes 2752520 | tf_op jit(solution)/shard_map/ppermute | solution.py:374
  53.8 13.5 %all-to-all-done = bf16[32,4,1152]{2,1,0:T(4,128)(2,1)S(1)} async-done(((bf16[32,4,1152]{2,1,0:T(4,128)(2,1)}), bf16[32,4,1152]{2,1,0:T(4,128)(2,1)S(1)}, u32[]{:S(2)}, u32[]{:S(2)}) %all-to-all-start) | async-done | bytes 294944 | tf_op jit(solution)/shard_map/all_to_all | solution.py:375
  67.3 2.7 %collective-permute-start = (bf16[16,2,4,1152]{3,2,1,0:T(4,128)(2,1)S(1)}, bf16[16,2,4,1152]{3,2,1,0:T(4,128)(2,1)S(1)}, u32[]{:S(2)}, u32[]{:S(2)}) collective-permute-start(bf16[16,2,4,1152]{3,2,1,0:T(4,128)(2,1)S(1)} %bitcast.22), channel_id=1, source_target_pairs={{0,1},{1,0},{2,3},{3,2},{4,5},{5,4},{6,7},{7,6},{8,9},{9,8},{10,11... | collective-permute-start | bytes 884744 | tf_op jit(solution)/shard_map/ppermute | solution.py:388
  70.0 1.2 shard_map.107.refs_0_
  71.2 0.0 copy-start.6
  71.2 0.0 copy-start.7
  71.2 0.0 collective-permute-done.3.down_ref
  71.2 0.0 collective-permute-done.in_ref
  71.3 1.2 shard_map.108
  72.5 19.3 %all_to_all.20.parts_ref = bf16[16,160,128]{2,1,0:T(8,128)(2,1)S(1)} all-to-all(bf16[16,160,128]{2,1,0:T(8,128)(2,1)S(1)} %shard_map.108), channel_id=1, replica_groups={{0,2,10,8,16,24,26,18,20,28,30,22,14,12,4,6},{1,3,11,9,17,25,27,19,21,2..., dimensions={0} | all-to-all | bytes 1310720 | tf_op jit(solution)/shard_map/all_to_all | solution.py:391
  91.7 0.0 copy-done.6
  91.7 0.3 shard_map.109
  92.1 21.9 %all_to_all.21.in_ref = bf16[16,336,128]{2,1,0:T(8,128)(2,1)S(1)} all-to-all(bf16[16,336,128]{2,1,0:T(8,128)(2,1)S(1)} %shard_map.109), channel_id=1, replica_groups={{0,2,10,8,16,24,26,18,20,28,30,22,14,12,4,6},{1,3,11,9,17,25,27,19,21,2..., dimensions={0} | all-to-all | bytes 2752512 | tf_op jit(solution)/shard_map/all_to_all | solution.py:400
  114.0 1.4 shard_map.111
  115.4 0.0 copy-start.8
  115.4 4.3 %collective-permute-start.4 = (bf16[16,4,1152]{2,1,0:T(4,128)(2,1)S(1)}, bf16[16,4,1152]{2,1,0:T(4,128)(2,1)S(1)}, u32[]{:S(2)}, u32[]{:S(2)}) collective-permute-start(bf16[16,4,1152]{2,1,0:T(4,128)(2,1)S(1)} %shard_map.111), channel_id=1, source_target_pairs={{0,1},{1,0},{2,3},{3,2},{4,5},{5,4},{6,7},{7,6},{8,9},{9,8},{10,11... | collective-permute-start | bytes 442376 | tf_op jit(solution)/shard_map/ppermute | solution.py:412
  119.7 1.4 shard_map.110.mine_ref
  121.1 0.0 collective-permute-done.4.other_ref
  121.2 48.5 %all_to_all.22.in_ref = bf16[32,4,1152]{2,1,0:T(4,128)(2,1)S(1)} all-to-all(bf16[32,4,1152]{2,1,0:T(4,128)(2,1)S(1)} %bitcast.25), channel_id=1, replica_groups={{480,448,416,384,352,320,288,256,224,192,160,128,96,64,32,0,992,960,928..., dimensions={0} | all-to-all | bytes 589824 | tf_op jit(solution)/shard_map/all_to_all | solution.py:420
  169.7 1.1 shard_map.113
  (15 shorter events, 0.1 us)
Async XLA Ops:
  2.8 47.7 %copy-start = (bf16[1,2,1024,224]{2,3,1,0:T(8,128)(2,1)S(1)}, bf16[1,2,1024,224]{2,3,1,0:T(8,128)(2,1)}, u32[]{:S(2)}) copy-start(bf16[1,2,1024,224]{2,3,1,0:T(8,128)(2,1)} %param.15) | copy-start | bytes 2752516
  2.8 64.5 %all-to-all-start = ((bf16[32,4,1152]{2,1,0:T(4,128)(2,1)}), bf16[32,4,1152]{2,1,0:T(4,128)(2,1)S(1)}, u32[]{:S(2)}, u32[]{:S(2)}) async-start(bf16[32,4,1152]{2,1,0:T(4,128)(2,1)} %shard_map.104.after_ref), calls=%async_computation | async-start | bytes 589824 | tf_op jit(solution)/shard_map/all_to_all | solution.py:375
  39.1 5.4 %collective-permute-start.1 = (bf16[2,224,1024]{2,1,0:T(8,128)(2,1)}, bf16[2,224,1024]{2,1,0:T(8,128)(2,1)S(1)}, u32[]{:S(2)}, u32[]{:S(2)}) collective-permute-start(bf16[2,224,1024]{2,1,0:T(8,128)(2,1)} %bitcast.26), channel_id=1, source_target_pairs={{0,1},{1,0},{2,3},{3,2},{4,5},{5,4},{6,7},{7,6},{8,9},{9,8},{10,11... | collective-permute-start | bytes 2752520 | tf_op jit(solution)/shard_map/ppermute | solution.py:361
  42.2 4.6 %collective-permute-start.2 = (bf16[2,224,1024]{2,1,0:T(8,128)(2,1)}, bf16[2,224,1024]{2,1,0:T(8,128)(2,1)S(1)}, u32[]{:S(2)}, u32[]{:S(2)}) collective-permute-start(bf16[2,224,1024]{2,1,0:T(8,128)(2,1)} %bitcast.28), channel_id=1, source_target_pairs={{0,1},{1,0},{2,3},{3,2},{4,5},{5,4},{6,7},{7,6},{8,9},{9,8},{10,11... | collective-permute-start | bytes 2752520 | tf_op jit(solution)/shard_map/ppermute | solution.py:361
  44.5 2.3 %copy-start.9 = (bf16[2,224,1024]{2,1,0:T(8,128)(2,1)}, bf16[2,224,1024]{2,1,0:T(8,128)(2,1)S(1)}, u32[]{:S(2)}) copy-start(bf16[2,224,1024]{2,1,0:T(8,128)(2,1)S(1)} %collective-permute-done.1.refs_0_) | copy-start | bytes 2752516
  46.8 0.9 copy-start.10
  50.5 1.2 copy-start.1
  51.8 19.5 %collective-permute-start.3 = (bf16[2,224,1024]{2,1,0:T(8,128)(2,1)S(1)}, bf16[2,224,1024]{2,1,0:T(8,128)(2,1)S(1)}, u32[]{:S(2)}, u32[]{:S(2)}) collective-permute-start(bf16[2,224,1024]{2,1,0:T(8,128)(2,1)S(1)} %shard_map.106), channel_id=1, source_target_pairs={{0,1},{1,0},{2,3},{3,2},{4,5},{5,4},{6,7},{7,6},{8,9},{9,8},{10,11... | collective-permute-start | bytes 2752520 | tf_op jit(solution)/shard_map/ppermute | solution.py:374
  67.3 3.9 %collective-permute-start = (bf16[16,2,4,1152]{3,2,1,0:T(4,128)(2,1)S(1)}, bf16[16,2,4,1152]{3,2,1,0:T(4,128)(2,1)S(1)}, u32[]{:S(2)}, u32[]{:S(2)}) collective-permute-start(bf16[16,2,4,1152]{3,2,1,0:T(4,128)(2,1)S(1)} %bitcast.22), channel_id=1, source_target_pairs={{0,1},{1,0},{2,3},{3,2},{4,5},{5,4},{6,7},{7,6},{8,9},{9,8},{10,11... | collective-permute-start | bytes 884744 | tf_op jit(solution)/shard_map/ppermute | solution.py:388
  71.2 20.5 %copy-start.6 = (bf16[1,20,1,1024]{3,1,2,0:T(8,128)(2,1)S(1)}, bf16[1,20,1,1024]{3,1,2,0:T(8,128)(2,1)}, u32[]{:S(2)}) copy-start(bf16[1,20,1,1024]{3,1,2,0:T(8,128)(2,1)} %param.16) | copy-start | bytes 122884
  71.2 20.5 %copy-start.7 = (bf16[1,20,1,1024]{3,1,2,0:T(8,128)(2,1)S(1)}, bf16[1,20,1,1024]{3,1,2,0:T(8,128)(2,1)}, u32[]{:S(2)}) copy-start(bf16[1,20,1,1024]{3,1,2,0:T(8,128)(2,1)} %param.17) | copy-start | bytes 122884
  92.0 21.9 %copy-start.2 = (bf16[2,224,1024]{2,1,0:T(8,128)(2,1)S(1)}, bf16[2,224,1024]{2,1,0:T(8,128)(2,1)}, u32[]{:S(2)}) copy-start(bf16[2,224,1024]{2,1,0:T(8,128)(2,1)} %get-tuple-element.6.after_ref.gate_ref) | copy-start | bytes 2752516
  92.1 21.9 %copy-start.5 = (bf16[2,224,1024]{2,1,0:T(8,128)(2,1)S(1)}, bf16[2,224,1024]{2,1,0:T(8,128)(2,1)}, u32[]{:S(2)}) copy-start(bf16[2,224,1024]{2,1,0:T(8,128)(2,1)} %get-tuple-element.7.up_ref) | copy-start | bytes 2752516
  114.0 5.7 %copy-start.3 = (bf16[1,2,224,1024]{3,2,1,0:T(8,128)(2,1)S(1)}, bf16[1,2,224,1024]{3,2,1,0:T(8,128)(2,1)}, u32[]{:S(2)}) copy-start(bf16[1,2,224,1024]{3,2,1,0:T(8,128)(2,1)} %param.13) | copy-start | bytes 2752516
  114.0 5.7 %copy-start.4 = (bf16[1,2,224,1024]{3,2,1,0:T(8,128)(2,1)S(1)}, bf16[1,2,224,1024]{3,2,1,0:T(8,128)(2,1)}, u32[]{:S(2)}) copy-start(bf16[1,2,224,1024]{3,2,1,0:T(8,128)(2,1)} %param.14) | copy-start | bytes 2752516
  115.4 54.3 %copy-start.8 = (s32[128,4]{0,1:T(4,128)S(1)}, s32[128,4]{0,1:T(4,128)}, u32[]{:S(2)}) copy-start(s32[128,4]{0,1:T(4,128)} %param.10) | copy-start | bytes 6148
  115.4 5.7 %collective-permute-start.4 = (bf16[16,4,1152]{2,1,0:T(4,128)(2,1)S(1)}, bf16[16,4,1152]{2,1,0:T(4,128)(2,1)S(1)}, u32[]{:S(2)}, u32[]{:S(2)}) collective-permute-start(bf16[16,4,1152]{2,1,0:T(4,128)(2,1)S(1)} %shard_map.111), channel_id=1, source_target_pairs={{0,1},{1,0},{2,3},{3,2},{4,5},{5,4},{6,7},{7,6},{8,9},{9,8},{10,11... | collective-permute-start | bytes 442376 | tf_op jit(solution)/shard_map/ppermute | solution.py:412
